TPU v7x, 256 devices: a whole 4x4x8 slice. The times are simulated.
256 devices in a mesh: band: 16 (over x_lo, y, core), chan: 16 (over z, x_hi).
Axes of the slice: x: 4 (x_hi: 2, x_lo: 2; x = x_hi * 2 + x_lo), y: 4, z: 8, core: 2. Of those that a mesh axis runs over, the one named last changes fastest.
Arguments:
- inputs: bfloat16 [256, 256, 384], P('chan', 'band'), may hold values from -6 to 6
- cotangent: bfloat16 [256, 256, 384], P('chan', 'band'), may hold values from -6 to 6
- kernel: bfloat16 [256, 3, 3, 256], P('chan'), may hold values from -0.125 to 0.125
- channel_bias: float32 [256], P('chan'), may hold values from -4 to 4
Outputs:
- input_grad: bfloat16 [256, 256, 384], P('chan', 'band')
- kernel_grad: float32 [256, 3, 3, 256], P('chan')
All inputs are finite; a program needn't handle non-finite values.
Results may differ from a plain program's by a relative error of at most 0.0095.
Values may be sent and summed in bfloat16 or wider, within the bound.
No kernel may reach another device: no remote copies, remote signals or barrier semaphores. Data moves between devices by JAX's collectives and lax.ppermute only.
A program may use at most 128 MiB of HBM per device.

v0:
```python
import math

import jax
import jax.numpy as jnp
from jax import lax
from jax.sharding import PartitionSpec as P


def with_halo(shard, sides, width):
    for axis, dim in sides:
        count, length = (lax.axis_size(axis), shard.shape[dim])
        up = [(i, (i + 1) % count) for i in range(count - 1)]
        down = [(j, i) for i, j in up]
        last = lax.slice_in_dim(shard, length - width, length, axis=dim)
        initial = lax.slice_in_dim(shard, 0, width, axis=dim)
        before = lax.ppermute(last, axis, up)
        after = lax.ppermute(initial, axis, down)
        shard = jnp.concatenate([before, shard, after], axis=dim)
    return shard


def pad_columns(field):
    return jnp.pad(field, ((0, 0), (0, 0), (1, 1)))


def transpose_conv(weights, padded_grad, height, width):
    total = jnp.zeros((weights.shape[3], height, width), jnp.float32)
    for row_tap in range(3):
        for col_tap in range(3):
            total = total + jnp.einsum(
                "oi,ohw->ihw",
                weights[:, row_tap, col_tap, :],
                padded_grad[
                    :, 2 - row_tap : 2 - row_tap + height, 2 - col_tap : 2 - col_tap + width
                ],
                preferred_element_type=jnp.float32,
            )
    return total


def forward_grad(weights, biases, padded_in, cotangent, height, width):
    pre = jnp.zeros((weights.shape[0], height, width), jnp.float32) + biases[:, None, None]
    for row_tap in range(3):
        for col_tap in range(3):
            pre = pre + jnp.einsum(
                "oi,ihw->ohw",
                weights[:, row_tap, col_tap, :],
                padded_in[:, row_tap : row_tap + height, col_tap : col_tap + width],
                preferred_element_type=jnp.float32,
            )
    sigmo = jax.nn.sigmoid(pre)
    return (cotangent.astype(jnp.float32) * sigmo * (1.0 + pre * (1.0 - sigmo))).astype(
        jnp.bfloat16
    )


def weight_taps(grad_pre, padded_in, height, width):
    taps = []
    for row_tap in range(3):
        for col_tap in range(3):
            taps.append(
                jnp.einsum(
                    "ohw,ihw->oi",
                    grad_pre,
                    padded_in[:, row_tap : row_tap + height, col_tap : col_tap + width],
                    preferred_element_type=jnp.float32,
                )
            )
    return jnp.stack(taps, axis=1).reshape((grad_pre.shape[0], 3, 3, padded_in.shape[0]))


def shards(inputs, cotangent, kernel, channel_bias):
    height = inputs.shape[1]
    width = inputs.shape[2]
    factor = 1.0 / math.sqrt(height * lax.axis_size("band") * width)
    rimmed = with_halo(inputs, (("band", 1),), 1)
    gathered = lax.all_gather(rimmed, "chan", axis=0, tiled=True)
    padded_in = pad_columns(gathered)
    grad_pre = forward_grad(kernel, channel_bias, padded_in, cotangent, height, width)
    local_wgrad = weight_taps(grad_pre, padded_in, height, width) * factor
    grad_rimmed = with_halo(grad_pre, (("band", 1),), 1)
    padded_grad = pad_columns(grad_rimmed)
    summed = lax.psum_scatter(
        transpose_conv(kernel, padded_grad, height, width), "chan", scatter_dimension=0, tiled=True
    )
    input_grad = summed.astype(jnp.bfloat16)
    kernel_grad = lax.psum(local_wgrad, "band")
    return (input_grad, kernel_grad)


def solution(mesh):
    return jax.shard_map(
        shards,
        mesh=mesh,
        in_specs=(
            P("chan", "band", None),
            P("chan", "band", None),
            P("chan", None, None, None),
            P("chan"),
        ),
        out_specs=(P("chan", "band", None), P("chan", None, None, None)),
        check_vma=False,
    )
```

profile of v0, /device:TPU:1, one launch (start us, length us, event | category | flops | bytes accessed | tf_op | source)
XLA Modules:
  0.0 530.4 jit_solution(9314588924775291928)
XLA Ops:
  7.2 0.0 all-gather.2.cloned.1.call-start
  7.2 1.0 copy.12
  8.2 4.6 collective-permute-start
  12.8 1.9 collective-permute-start.1
  14.7 0.0 collective-permute-done
  14.7 3.1 collective-permute-done.1
  17.8 0.7 pad_maximum_fusion
  18.5 0.0 all-gather.2.cloned.1.call-update
  18.5 0.0 reduce-scatter.2.cloned.1.call-start
  18.6 96.4 %all-gather.2.cloned.1.call-done = bf16[256,18,384]{2,0,1:T(8,128)(2,1)} async-done(((bf16[16,18,384]{2,0,1:T(8,128)(2,1)}), bf16[256,18,384]{2,0,1:T(8,128)(2,1)}) %all-gather.2.cloned.1.call-update) | async-done | bytes 3538960 | tf_op jit(solution)/shard_map/all_gather | solution.py:77
  115.0 0.0 copy-start
  115.0 0.0 copy-start.4
  115.0 3.1 fusion.15
  118.2 0.0 copy-done
  118.2 0.0 copy-done.4
  118.2 1.1 fusion.17
  119.2 1.1 fusion.19
  120.3 1.1 fusion.21
  121.4 1.1 fusion.23
  122.5 0.5 fusion.2
  123.0 0.0 copy-start.5
  123.0 0.5 fusion.6
  123.5 0.5 fusion.10
  124.1 0.0 copy-done.5
  124.1 0.0 copy-done.6
  124.1 1.3 multiply_convert_fusion
  125.4 0.0 copy-start.1
  125.4 6.0 %collective-permute-start.3 = (bf16[16,1,384]{2,0,1:T(8,128)(2,1)S(1)}, bf16[16,1,384]{2,0,1:T(8,128)(2,1)S(1)}, u32[]{:S(2)}, u32[]{:S(2)}) collective-permute-start(bf16[16,1,384]{2,0,1:T(8,128)(2,1)S(1)} %get-tuple-element.4), channel_id=1, source_target_pairs={{16,0},{32,16},{48,32},{64,48},{80,64},{96,80},{112,96},{128,112},... | collective-permute-start | bytes 36872 | tf_op jit(solution)/shard_map/ppermute | solution.py:17
  131.5 3.2 collective-permute-start.2
  134.7 3.6 fusion.102
  138.3 0.0 collective-permute-done.3
  138.3 0.0 collective-permute-done.2
  138.3 0.2 fusion.69
  138.5 0.0 copy-start.3
  138.5 4.2 fusion.82
  142.6 3.7 fusion.84
  146.3 4.1 fusion.86
  150.4 3.7 fusion.88
  154.1 0.0 copy-done.3
  154.1 4.2 fusion.90
  158.3 3.6 fusion.74
  161.9 0.0 copy-done.1
  161.9 3.7 fusion.70
  165.6 20.5 %add_bitcast_fusion = f32[256,16,384]{0,2,1:T(8,128)} fusion(f32[16,384,256]{2,1,0:T(8,128)} %fusion.74, f32[16,384,256]{2,1,0:T(8,128)} %fusion.82, f32[16,384,256]{2,1,0:T(8,128)} %fusion.84, f32[16,384,256]{2,1,0:T(8,128)} %fusion.102, f32[16,384,256]{2,1,0:T(8,128)} %fusion.86, f32[16,384,256]{2,1,0:T(8,128)} %fusion.88, f32[16,384,256]{2,1,0:T(8,128)} %fusion.90, ...), kind=kOutput, calls=%fused_computation | convolution fusion | flops 62914560 | bytes 56827904 | tf_op jit(solution)/shard_map/oi,ohw->ihw/dot_general | solution.py:30
  186.1 6.7 %copy.15 = f32[256,16,384]{2,1,0:T(8,128)} copy(f32[256,16,384]{0,2,1:T(8,128)} %add_bitcast_fusion) | data formatting | bytes 12582912 | tf_op jit(solution)/shard_map/add | solution.py:30
  192.8 0.0 reduce-scatter.2.cloned.1.call-update
  192.8 0.3 all-reduce.4.cloned.1.call-start
  193.1 0.0 copy-start.2
  193.1 2.3 fusion.63
  195.4 0.0 copy-done.2
  195.4 0.9 fusion.37
  196.4 1.4 fusion.61
  197.7 1.4 fusion.59
  199.1 0.9 fusion.43
  200.0 1.4 fusion.57
  201.4 1.4 fusion.55
  202.7 0.9 fusion.49
  203.7 1.4 fusion.53
  205.0 0.7 broadcast_multiply_fusion
  205.8 0.0 all-reduce.4.cloned.1.call-update
  205.8 199.2 %reduce-scatter.2.cloned.1.call-done = f32[16,16,384]{2,1,0:T(8,128)} async-done(((f32[256,16,384]{2,1,0:T(8,128)}), f32[16,16,384]{2,1,0:T(8,128)}) %reduce-scatter.2.cloned.1.call-update) | async-done | bytes 393232 | tf_op jit(solution)/shard_map/reduce_scatter | solution.py:83
  404.9 1.7 convert_element_type.15
  406.6 115.6 %all-reduce.4.cloned.1.call-done = f32[16,3,3,256]{3,0,2,1:T(8,128)} async-done(((f32[16,3,3,256]{3,0,2,1:T(8,128)}), f32[16,3,3,256]{3,0,2,1:T(8,128)}) %all-reduce.4.cloned.1.call-update) | async-done | bytes 147472 | tf_op jit(solution)/shard_map/psum | solution.py:87
  522.2 1.6 copy.26
  (3 shorter events, 0.0 us)
Async XLA Ops:
  7.2 107.9 %all-gather.2.cloned.1.call-start = ((), (), s32[]{:S(2)}) async-start(), calls=%async_computation.1 | async-start | bytes 3760128 | tf_op jit(solution)/shard_map/all_gather | solution.py:77
  8.2 6.5 %collective-permute-start = (bf16[16,1,384]{2,0,1:T(8,128)(2,1)S(1)}, bf16[16,1,384]{2,0,1:T(8,128)(2,1)S(1)}, u32[]{:S(2)}, u32[]{:S(2)}) collective-permute-start(bf16[16,1,384]{2,0,1:T(8,128)(2,1)S(1)} %get-tuple-element.6), channel_id=1, source_target_pairs={{0,16},{16,32},{32,48},{48,64},{64,80},{80,96},{96,112},{112,128},... | collective-permute-start | bytes 36872 | tf_op jit(solution)/shard_map/ppermute | solution.py:16
  12.8 5.0 collective-permute-start.1
  18.5 386.4 %reduce-scatter.2.cloned.1.call-start = ((), (), s32[]{:S(2)}) async-start(), calls=%async_computation.2 | async-start | bytes 6684672 | tf_op jit(solution)/shard_map/reduce_scatter | solution.py:83
  115.0 3.1 copy-start
  115.0 3.1 copy-start.4
  123.0 1.1 copy-start.5
  123.0 1.1 copy-start.6
  125.4 36.5 %copy-start.1 = (bf16[16,16,384]{2,0,1:T(8,128)(2,1)}, bf16[16,16,384]{2,0,1:T(8,128)(2,1)S(1)}, u32[]{:S(2)}) copy-start(bf16[16,16,384]{2,0,1:T(8,128)(2,1)S(1)} %multiply_convert_fusion) | copy-start | bytes 589828
  125.4 12.9 %collective-permute-start.3 = (bf16[16,1,384]{2,0,1:T(8,128)(2,1)S(1)}, bf16[16,1,384]{2,0,1:T(8,128)(2,1)S(1)}, u32[]{:S(2)}, u32[]{:S(2)}) collective-permute-start(bf16[16,1,384]{2,0,1:T(8,128)(2,1)S(1)} %get-tuple-element.4), channel_id=1, source_target_pairs={{16,0},{32,16},{48,32},{64,48},{80,64},{96,80},{112,96},{128,112},... | collective-permute-start | bytes 36872 | tf_op jit(solution)/shard_map/ppermute | solution.py:17
  131.5 6.8 %collective-permute-start.2 = (bf16[16,1,384]{2,0,1:T(8,128)(2,1)S(1)}, bf16[16,1,384]{2,0,1:T(8,128)(2,1)S(1)}, u32[]{:S(2)}, u32[]{:S(2)}) collective-permute-start(bf16[16,1,384]{2,0,1:T(8,128)(2,1)S(1)} %get-tuple-element.5), channel_id=1, source_target_pairs={{0,16},{16,32},{32,48},{48,64},{64,80},{80,96},{96,112},{112,128},... | collective-permute-start | bytes 36872 | tf_op jit(solution)/shard_map/ppermute | solution.py:16
  138.5 15.6 %copy-start.3 = (bf16[16,18,386]{2,0,1:T(8,128)(2,1)}, bf16[16,18,386]{2,0,1:T(8,128)(2,1)S(1)}, u32[]{:S(2)}) copy-start(bf16[16,18,386]{2,0,1:T(8,128)(2,1)S(1)} %fusion.69) | copy-start | bytes 667012
  192.8 329.4 %all-reduce.4.cloned.1.call-start = ((), (), s32[]{:S(2)}) async-start(), calls=%async_computation.3 | async-start | bytes 294912 | tf_op jit(solution)/shard_map/psum | solution.py:87
  193.1 2.3 copy-start.2
Sparse Core Ops, SparseCore 0:
  18.7 96.3 all-gather.1
  192.9 211.9 reduce-scatter.1
  408.3 113.8 all-reduce.3
where the time goes:
time: 531 us; the launch traced here: 530 us
  waiting for transfers between devices  414 us (78%)
  matrix products  73.5 us (14%)
  starting transfers between devices  16.1 us (3%)
  between operations  13.9 us (3%)
  local copies, waits for them, and re-layouts  9.31 us (2%)
    reduce_scatter x1, waiting for transfers between devices, shards(): lax.psum_scatter(transpose_conv(kernel, padded_grad, height, width), 'cha...  199 us
    psum x1, waiting for transfers between devices, shards(): kernel_grad = lax.psum(local_wgrad, 'band')  116 us
    all_gather x1, waiting for transfers between devices, shards(): gathered = lax.all_gather(rimmed, 'chan', axis=0, tiled=True)  96.4 us
    dot_general x9, matrix products, transpose_conv(): jnp.einsum('oi,ohw->ihw', weights[:, row_tap, col_tap, :], padded_grad[:,...  51.2 us
    dot_general x9, matrix products, weight_taps(): jnp.einsum('ohw,ihw->oi', grad_pre, padded_in[:, row_tap:row_tap + height...  11.9 us
  transfers between devices with their start and end apart: 7, of which 4 were waited for; matrix products, arithmetic and copies ran while one was open for 3% of the time, Pallas kernels for 0%

commit v1 on v0

v1 whole, which is shorter than its diff:
```python
import math

import jax
import jax.numpy as jnp
from jax import lax
from jax.experimental import pallas as pl
from jax.experimental.pallas import tpu as pltpu
from jax.sharding import Mesh
from jax.sharding import PartitionSpec as P

BF = jnp.bfloat16
F32 = jnp.float32
CHAN = ("z", "xh")
BAND = ("xl", "y", "core")
PITCH = 32
NCOL = 24
PX = 1152
NT = (((1,), (1,)), ((), ()))
TN = (((0,), (0,)), ((), ()))


def dot(a, b, dims=(((1,), (0,)), ((), ()))):
    return lax.dot_general(a, b, dims, preferred_element_type=F32)


def iota(shape, dim):
    return lax.broadcasted_iota(jnp.int32, shape, dim)


def call(body, outs, *args, smem=True, scratch=()):
    specs = [pl.BlockSpec(memory_space=pltpu.VMEM)] * len(args)
    if smem:
        specs[0] = pl.BlockSpec(memory_space=pltpu.SMEM)
    return pl.pallas_call(
        body,
        out_shape=[jax.ShapeDtypeStruct(s, d) for s, d in outs],
        in_specs=specs,
        out_specs=[pl.BlockSpec(memory_space=pltpu.VMEM)] * len(outs),
        scratch_shapes=list(scratch),
        compiler_params=pltpu.CompilerParams(vmem_limit_bytes=48 * 1024 * 1024),
    )(*args)


def swap_blocks(arrays, block):
    lanes = arrays[0].shape[1]
    place = iota(arrays[0].shape, 1) // block
    bit = 1
    while bit < len(arrays):
        upper = (place & bit) != 0
        out = list(arrays)
        for s in range(len(arrays)):
            if s & bit:
                continue
            a, b = arrays[s], arrays[s | bit]
            out[s] = jnp.where(upper, pltpu.roll(b, bit * block, 1), a)
            out[s | bit] = jnp.where(upper, b, pltpu.roll(a, lanes - bit * block, 1))
        arrays = out
        bit *= 2
    return arrays


def window(first, count):
    row = iota((512, 384), 0)
    c = row & 31
    hit = (iota((512, 384), 1) == (row >> 5) * NCOL + c + first) & (c < count)
    return jnp.where(hit, 1.0, 0.0).astype(BF)


def pack_kernel(core_ref, x_ref, cot_ref, ker_ref, bias_ref, out_ref):
    core = core_ref[0]
    src = iota((256, 256), 0)
    dst = iota((256, 256), 1)
    ch, h = src >> 4, src & 15
    to_h_ch = jnp.where(dst == h * 16 + ch, 1.0, 0.0).astype(BF)
    other = (ch >> 3) ^ core
    to_half = jnp.where(dst == other * 128 + h * 8 + (ch & 7), 1.0, 0.0).astype(BF)

    x = dot(window(-2, 28), x_ref[...].reshape(256, 384), NT).astype(BF)
    x = dot(x, to_h_ch).astype(BF).reshape(16, 32, 256)
    out_ref[:, 0:32, :] = x[:, :, 0:128]
    out_ref[:, 32:64, :] = x[:, :, 128:256]

    bias = jnp.broadcast_to(bias_ref[...], (8, 16))
    hi = bias.astype(BF).astype(F32)
    mid = (bias - hi).astype(BF).astype(F32)
    low = bias - hi - mid
    k = iota((8, 16), 0)
    pieces = jnp.where(k == 4, hi, jnp.where(k == 5, mid, jnp.where(k == 6, low, 0.0)))
    spread = iota((16, 128), 0) == (core * 8 + (iota((16, 128), 1) & 7))
    pieces = dot(pieces.astype(BF), jnp.where(spread, 1.0, 0.0).astype(BF))
    rows = jnp.concatenate([jnp.zeros((24, 128), F32), pieces], axis=0)

    c = dot(window(-1, 26), cot_ref[...].reshape(256, 384), NT).astype(BF)
    c = dot(c, to_half).reshape(16, 32, 256)
    out_ref[:, 64:96, :] = (c[:, :, 0:128] + rows[None]).astype(BF)
    out_ref[:, 96:128, :] = c[:, :, 128:256].astype(BF)

    parts = []
    for t in range(9):
        both = ker_ref[t].astype(F32)
        mine = jnp.where(core == 0, both[0:8], both[8:16])
        parts += [mine[:, 0:128], mine[:, 128:256]]
    weights = jnp.concatenate(parts, axis=0).astype(BF)
    for j in range(16):
        out_ref[j, 128:272, :] = weights


def unpack_kernel(core_ref, r_ref, xo_ref, co_ref, ha_ref, hb_ref, w_ref):
    core = core_ref[0]
    edge = []
    for hh in range(2):
        halves = []
        for sh in range(2):
            got = [r_ref[sh * 8 + s, hh * 32 : hh * 32 + 32, :] for s in range(8)]
            halves.append(swap_blocks(got, 16))
        for hl in range(8):
            at = (hh * 8 + hl) * 32
            row = jnp.concatenate([halves[0][hl], halves[1][hl]], axis=1)
            xo_ref[at : at + 32, :] = row
            if (hh * 8 + hl) in (0, 1, 14, 15):
                edge.append(row)
    own = swap_blocks([r_ref[s, 64:96, :] for s in range(16)], 8)
    oth = swap_blocks([r_ref[s, 96:128, :] for s in range(16)], 8)
    for h in range(16):
        co_ref[h * 32 : h * 32 + 32, :] = own[h]
        at = 512 + (h % 8) * 32
        xo_ref[at : at + 32, (h // 8) * 128 : (h // 8) * 128 + 128] = oth[h]
    first = core == 0
    blank = jnp.zeros((32, 128), BF)
    for ref, cot in ((ha_ref, oth), (hb_ref, own)):
        ref[0:32, :] = jnp.where(first, edge[0], edge[2])
        ref[32:64, :] = jnp.where(first, edge[1], edge[3])
        ref[64:96, 0:128] = jnp.where(first, cot[0], cot[15])
        ref[64:96, 128:256] = blank
    chunks = [r_ref[s, 128:272, :].astype(F32) for s in range(16)]
    for t in range(9):
        for ih in range(2):
            at = (t * 2 + ih) * 8
            tap = jnp.concatenate([c[at : at + 8] for c in chunks], axis=0)
            w_ref[t * 128 : t * 128 + 128, ih * 128 : ih * 128 + 128] = tap.astype(BF)


def grad_kernel(
    scale, core_ref, xo_ref, xr_ref, co_ref, ha_ref, hb_ref, w_ref, kg_ref, g_ref, x, cot, y, gs
):
    core = core_ref[0]
    first = core == 0
    mine = pl.multiple_of(core * 512, 512)
    theirs = pl.multiple_of((1 - core) * 512, 512)
    x[0:64, :] = jnp.where(first, ha_ref[0:64, :], hb_ref[0:64, :])
    x[pl.ds(64 + mine, 512), :] = xo_ref[0:512, :]
    x[pl.ds(64 + theirs, 512), :] = xr_ref[0:512, :]
    x[1088:1152, :] = jnp.where(first, hb_ref[0:64, :], ha_ref[0:64, :])
    x[1152:1216, :] = jnp.zeros((64, 256), BF)
    cot[0:32, :] = jnp.where(first, ha_ref[64:96, 0:128], hb_ref[64:96, 0:128])
    cot[pl.ds(32 + mine, 512), :] = co_ref[...]
    cot[pl.ds(32 + theirs, 256), :] = xr_ref[512:768, 0:128]
    cot[pl.ds(32 + theirs + 256, 256), :] = xr_ref[512:768, 128:256]
    cot[1056:1088, :] = jnp.where(first, hb_ref[64:96, 0:128], ha_ref[64:96, 0:128])

    bias = co_ref[16:32, :].astype(F32)
    bias = bias[12:13] + bias[13:14] + bias[14:15]

    for m in range(0, PX, 384):
        y[m : m + 384, :] = (
            dot(x[m : m + 384, :], w_ref[0:384, :], NT)
            + dot(x[m + 32 : m + 416, :], w_ref[384:768, :], NT)
            + dot(x[m + 64 : m + 448, :], w_ref[768:1152, :], NT)
        )

    gs[0:16, :] = jnp.zeros((16, 128), F32)
    for m in range(0, 1088, 64):
        pre = (
            y[m : m + 64, 0:128]
            + y[m + 1 : m + 65, 128:256]
            + y[m + 2 : m + 66, 256:384]
            + bias
        )
        s = 1.0 / (1.0 + jnp.exp(-pre))
        c = iota((64, 128), 0) & 31
        grad = cot[m : m + 64, :].astype(F32) * s * (1.0 + pre * (1.0 - s))
        grad = jnp.where(c < 26, grad, 0.0).astype(BF)
        g_ref[m : m + 64, :] = grad
        p = iota((64, 128), 0) + m
        inner = (c >= 1) & (c <= NCOL) & (p >= 32) & (p < 1056)
        gs[16 + m : 16 + m + 64, :] = jnp.where(inner, grad.astype(F32), 0.0)
    g_ref[1088:PX, :] = jnp.zeros((PX - 1088, 128), BF)
    gs[16 + 1088 : 16 + PX, :] = jnp.zeros((PX - 1088, 128), F32)

    taps = []
    shifted = jnp.concatenate(
        [gs[16 - b : 16 - b + PX, :].astype(BF) for b in range(3)], axis=1
    )
    for a in range(3):
        block = dot(shifted, x[32 * a : 32 * a + PX, :], TN) * scale
        taps += [block[0:128], block[128:256], block[256:384]]
    for m in range(8):
        lane = (m // 4) * 128
        for j in range(16):
            o = slice(8 * j, 8 * j + 8)
            kg_ref[m * 16 + j] = jnp.concatenate(
                [taps[m][o, 0:128], taps[m][o, 128:256], taps[8][o, lane : lane + 128]], axis=0
            ).astype(BF)


def input_kernel(core_ref, g_ref, w_ref, own_ref, send_ref, z, total):
    core = core_ref[0]
    for m in (0, 352, 704):
        for b in range(3):
            z[b, m : m + 352, :] = (
                dot(g_ref[m + 64 : m + 416, :], w_ref[b * 128 : b * 128 + 128, :])
                + dot(g_ref[m + 32 : m + 384, :], w_ref[384 + b * 128 : 512 + b * 128, :])
                + dot(g_ref[m : m + 352, :], w_ref[768 + b * 128 : 896 + b * 128, :])
            )
    for m in range(0, 1024, 64):
        total[m : m + 64, :] = (
            z[0, m + 2 : m + 66, :] + z[1, m + 1 : m + 65, :] + z[2, m : m + 64, :]
        )
    own_ref[...] = total[pl.ds(pl.multiple_of(core * 512, 512), 512), :]
    send_ref[...] = total[pl.ds(pl.multiple_of((1 - core) * 512, 512), 512), :].astype(BF)


def repack_kernel(own_ref, recv_ref, out_ref):
    parts = []
    for hh in range(2):
        rows = []
        for hl in range(8):
            at = (hh * 8 + hl) * 32
            row = own_ref[at : at + 32, :] + recv_ref[at : at + 32, :].astype(F32)
            rows.append(row[0:NCOL])
        parts.append([swap_blocks([r[:, q : q + 128] for r in rows], 16) for q in (0, 128)])
    for d in range(16):
        out_ref[d] = jnp.concatenate(
            [parts[0][d // 8][d % 8], parts[1][d // 8][d % 8]], axis=0
        ).astype(BF)


def restore_kernel(r_ref, out_ref):
    halves = [[], []]
    for j in range(16):
        chunk = r_ref[j].astype(F32)
        halves[0].append(chunk[0:NCOL])
        halves[1].append(chunk[NCOL : 2 * NCOL])
    field = jnp.concatenate(
        [jnp.concatenate(half, axis=0) for half in halves], axis=1
    ).astype(BF)
    row = iota((256, 256), 0)
    pick = iota((256, 256), 1) == (row & 15) * 16 + (row >> 4)
    out = dot(jnp.where(pick, 1.0, 0.0).astype(BF), field, NT)
    out_ref[...] = out.astype(BF).reshape(16, 16, 384)


def sum_kernel(r_ref, out_ref):
    total = r_ref[0].astype(F32)
    for s in range(1, 128):
        total = total + r_ref[s].astype(F32)
    for b in range(16):
        out_ref[b] = total


def order_kernel(r_ref, out_ref):
    for m in range(8):
        for core in range(2):
            for ih in range(2):
                out_ref[m, 8 * core : 8 * core + 8, 128 * ih : 128 * ih + 128] = r_ref[
                    2 * m + core, 8 * ih : 8 * ih + 8, :
                ]
    for core in range(2):
        for ih in range(2):
            out_ref[8, 8 * core : 8 * core + 8, 128 * ih : 128 * ih + 128] = r_ref[
                8 * ih + core, 16:24, :
            ]


def shards(inputs, cotangent, kernel, channel_bias):
    core = lax.axis_index("core").astype(jnp.int32).reshape(1)
    taps = kernel.reshape(16, 9, 256).transpose(1, 0, 2)
    (packed,) = call(
        pack_kernel,
        [((16, 272, 128), BF)],
        core,
        inputs,
        cotangent,
        taps,
        channel_bias.reshape(1, 16),
    )
    got = lax.all_to_all(packed, CHAN, 0, 0)
    xo, co, ha, hb, w = call(
        unpack_kernel,
        [((768, 256), BF), ((512, 128), BF), ((96, 256), BF), ((96, 256), BF), ((1152, 256), BF)],
        core,
        got,
    )
    across = [(b, b + 1) for b in range(1, 15, 2)]
    across += [(b + 1, b) for b in range(1, 15, 2)]
    along = [(b, b + 2) for b in range(1, 14, 2)] + [(b, b - 2) for b in range(2, 16, 2)]
    xr = lax.ppermute(xo, "core", [(0, 1), (1, 0)])
    ha = lax.ppermute(ha, BAND, across)
    hb = lax.ppermute(hb, BAND, along)
    scale = 1.0 / math.sqrt(256 * 384)

    def grads(*refs):
        grad_kernel(scale, *refs)

    kg, g = call(
        grads,
        [((128, 24, 128), BF), ((PX, 128), BF)],
        core,
        xo,
        xr,
        co,
        ha,
        hb,
        w,
        scratch=[
            pltpu.VMEM((1216, 256), BF),
            pltpu.VMEM((1088, 128), BF),
            pltpu.VMEM((PX, 384), F32),
            pltpu.VMEM((PX + 16, 128), F32),
        ],
    )
    kg = lax.all_to_all(kg, ("xl", "y", "z", "xh"), 0, 0)
    own, send = call(
        input_kernel,
        [((512, 256), F32), ((512, 256), BF)],
        core,
        g,
        w,
        scratch=[pltpu.VMEM((3, 1056, 256), F32), pltpu.VMEM((1024, 256), F32)],
    )
    recv = lax.ppermute(send, "core", [(0, 1), (1, 0)])
    (back,) = call(repack_kernel, [((16, 48, 128), BF)], own, recv, smem=False)
    back = lax.all_to_all(back, CHAN, 0, 0)
    (input_grad,) = call(restore_kernel, [((16, 16, 384), BF)], back, smem=False)
    (pieces,) = call(sum_kernel, [((16, 24, 128), F32)], kg, smem=False)
    pieces = lax.all_to_all(pieces, BAND, 0, 0)
    (ordered,) = call(order_kernel, [((9, 16, 256), F32)], pieces, smem=False)
    kernel_grad = ordered.transpose(1, 0, 2).reshape(16, 3, 3, 256)
    return (input_grad, kernel_grad)


def solution(mesh):
    fine = Mesh(mesh.devices.reshape(2, 4, 2, 8, 2), ("xl", "y", "core", "z", "xh"))
    return jax.shard_map(
        shards,
        mesh=fine,
        in_specs=(
            P(CHAN, BAND, None),
            P(CHAN, BAND, None),
            P(CHAN, None, None, None),
            P(CHAN),
        ),
        out_specs=(P(CHAN, BAND, None), P(CHAN, None, None, None)),
        check_vma=False,
    )
```

time: 531 us -> 121 us (0.23)
  waiting for transfers between devices: 414 us -> 30.4 us
  matrix products: 73.5 us -> 0 us
  blocking collectives: 0 us -> 42.6 us
  starting transfers between devices: 16.1 us -> 33.3 us
  between operations: 13.9 us -> 0.72 us
  Pallas kernels: 0 us -> 10.4 us
  local copies, waits for them, and re-layouts: 9.31 us -> 3.38 us
    reduce_scatter x1 -> x0, waiting for transfers between devices: 199 us -> none  [shards(): lax.psum_scatter(transpose_conv(kernel, padded_grad, height, width), 'cha...]
    psum x1 -> x0, waiting for transfers between devices: 116 us -> none  [shards(): kernel_grad = lax.psum(local_wgrad, 'band')]
    all_gather x1 -> x0, waiting for transfers between devices: 96.4 us -> none  [shards(): gathered = lax.all_gather(rimmed, 'chan', axis=0, tiled=True)]
    dot_general x27 -> x0, matrix products: 73.5 us -> none  [the longest x9 51.2 us: transpose_conv(): jnp.einsum('oi,ohw->ihw', weights[:, row_tap, col_tap, :], padded_grad[:,...]
    all_to_all x0 -> x1, blocking collectives: none -> 42.6 us  [shards(): got = lax.all_to_all(packed, CHAN, 0, 0)]
    all_to_all x0 -> x3, waiting for transfers between devices: none -> 28 us  [the longest x1 12.6 us: shards(): kg = lax.all_to_all(kg, ('xl', 'y', 'z', 'xh'), 0, 0)]
    all_to_all x0 -> x3, starting transfers between devices: none -> 21.8 us  [the longest x1 8.78 us: shards(): pieces = lax.all_to_all(pieces, BAND, 0, 0)]
    pallas_call x0 -> x8, Pallas kernels: none -> 10.4 us  [call(): pl.pallas_call(body, out_shape=[jax.ShapeDtypeStruct(s, d) for s, d in ou...]
  transfers between devices with their start and end apart: 7 -> 7, of which waited for: 4 -> 5; matrix products, arithmetic and copies ran while one was open for 3% -> 0% of each run, Pallas kernels for 0% -> 4%
where the time goes in v1:
time: 121 us
  blocking collectives  42.6 us (35%)
  starting transfers between devices  33.3 us (28%)
  waiting for transfers between devices  30.4 us (25%)
  Pallas kernels  10.4 us (9%)
  local copies, waits for them, and re-layouts  3.38 us (3%)
    all_to_all x1, blocking collectives, shards(): got = lax.all_to_all(packed, CHAN, 0, 0)  42.6 us
    all_to_all x1, waiting for transfers between devices, shards(): kg = lax.all_to_all(kg, ('xl', 'y', 'z', 'xh'), 0, 0)  12.6 us
    pallas_call x8, Pallas kernels, call(): pl.pallas_call(body, out_shape=[jax.ShapeDtypeStruct(s, d) for s, d in ou...  10.4 us
    all_to_all x1, waiting for transfers between devices, shards(): back = lax.all_to_all(back, CHAN, 0, 0)  9.7 us
    all_to_all x1, starting transfers between devices, shards(): pieces = lax.all_to_all(pieces, BAND, 0, 0)  8.78 us
    all_to_all x1, starting transfers between devices, shards(): kg = lax.all_to_all(kg, ('xl', 'y', 'z', 'xh'), 0, 0)  7.05 us
    all_to_all x1, starting transfers between devices, shards(): back = lax.all_to_all(back, CHAN, 0, 0)  5.99 us
    all_to_all x1, waiting for transfers between devices, shards(): pieces = lax.all_to_all(pieces, BAND, 0, 0)  5.74 us
  transfers between devices with their start and end apart: 7, of which 5 were waited for; matrix products, arithmetic and copies ran while one was open for 0% of the time, Pallas kernels for 4%

profile of v1, /device:TPU:1, one launch (start us, length us, event | category | flops | bytes accessed | tf_op | source)
XLA Modules:
  0.0 120.8 jit_solution(9335864881293814992)
XLA Ops:
  0.6 0.0 copy-start
  0.6 0.9 copy-done
  1.6 0.0 copy-start.1
  1.6 0.9 copy-done.1
  2.5 0.0 copy-start.2
  2.5 0.9 copy-done.2
  3.4 0.0 copy-start.3
  3.4 0.7 copy-done.3
  4.0 1.1 shard_map.59
  5.1 42.6 %all_to_all.20.r_ref = bf16[16,272,128]{2,1,0:T(8,128)(2,1)S(1)} all-to-all(bf16[16,272,128]{2,1,0:T(8,128)(2,1)S(1)} %shard_map.59), channel_id=1, replica_groups=mesh['xl'=2,'y'=4,'core'=2,'z'=8,'xh'=2] {'z','xh'}, dimensions={0} | all-to-all | bytes 2228224 | tf_op jit(solution)/shard_map/all_to_all | solution.py:287
  47.8 1.1 shard_map.60
  48.8 2.1 %collective-permute-start = (bf16[768,256]{1,0:T(8,128)(2,1)S(1)}, bf16[768,256]{1,0:T(8,128)(2,1)S(1)}, u32[]{:S(2)}, u32[]{:S(2)}) collective-permute-start(bf16[768,256]{1,0:T(8,128)(2,1)S(1)} %get-tuple-element.11.refs_1_), channel_id=1, source_target_pairs={{0,16},{16,0},{1,17},{17,1},{2,18},{18,2},{3,19},{19,3},{4,20},{20... | collective-permute-start | bytes 1179656 | tf_op jit(solution)/shard_map/ppermute | solution.py:297
  50.9 3.1 %collective-permute-start.1 = (bf16[96,256]{1,0:T(8,128)(2,1)S(1)}, bf16[96,256]{1,0:T(8,128)(2,1)S(1)}, u32[]{:S(2)}, u32[]{:S(2)}) collective-permute-start(bf16[96,256]{1,0:T(8,128)(2,1)S(1)} %get-tuple-element.13), channel_id=1, source_target_pairs={{16,32},{48,64},{80,96},{112,128},{144,160},{176,192},{208,224},{3... | collective-permute-start | bytes 147464 | tf_op jit(solution)/shard_map/ppermute | solution.py:298
  54.0 3.2 %collective-permute-start.2 = (bf16[96,256]{1,0:T(8,128)(2,1)S(1)}, bf16[96,256]{1,0:T(8,128)(2,1)S(1)}, u32[]{:S(2)}, u32[]{:S(2)}) collective-permute-start(bf16[96,256]{1,0:T(8,128)(2,1)S(1)} %get-tuple-element.14), channel_id=1, source_target_pairs={{16,48},{48,80},{80,112},{112,144},{144,176},{176,208},{208,240},{... | collective-permute-start | bytes 147464 | tf_op jit(solution)/shard_map/ppermute | solution.py:299
  57.3 0.0 collective-permute-done.1.refs_4_
  57.3 1.1 collective-permute-done.2.refs_5_
  58.4 0.0 collective-permute-done.refs_2_
  58.4 3.2 %shard_map.61 = (bf16[128,24,128]{2,1,0:T(8,128)(2,1)}, bf16[1152,128]{1,0:T(8,128)(2,1)S(1)}) custom-call(s32[1]{0:T(128)} %bitcast.core_ref.refs_0_, bf16[768,256]{1,0:T(8,128)(2,1)S(1)} %get-tuple-element.11.refs_1_, bf16[768,256]{1,0:T(8,128)(2,1)S(1)} %collective-permute-done.refs_2_, bf16[512,128]{1,0:T(8,128)(2,1)S(1)} %get-tuple-element.12.refs_3_, ...), custom_call_target="tpu_custom_call" | custom-call | tf_op jit(solution)/shard_map/pallas_call | solution.py:34
  61.7 7.1 %all-to-all-start.2 = ((bf16[128,24,128]{2,1,0:T(8,128)(2,1)}), bf16[128,24,128]{2,1,0:T(8,128)(2,1)S(1)}, u32[]{:S(2)}, u32[]{:S(2)}) async-start(bf16[128,24,128]{2,1,0:T(8,128)(2,1)} %get-tuple-element.19), calls=%async_computation.2 | async-start | bytes 1572864 | tf_op jit(solution)/shard_map/all_to_all | solution.py:322
  68.7 1.5 %shard_map.62 = (f32[512,256]{1,0:T(8,128)S(1)}, bf16[512,256]{1,0:T(8,128)(2,1)S(1)}) custom-call(s32[1]{0:T(128)} %bitcast.core_ref.refs_0_, bf16[1152,128]{1,0:T(8,128)(2,1)S(1)} %get-tuple-element.16.g_ref, bf16[1152,256]{1,0:T(8,128)(2,1)S(1)} %get-tuple-element.15.refs_6_.w_ref), custom_call_target="tpu_custom_call" | custom-call | tf_op jit(solution)/shard_map/pallas_call | solution.py:34
  70.2 3.1 %collective-permute-start.3 = (bf16[512,256]{1,0:T(8,128)(2,1)S(1)}, bf16[512,256]{1,0:T(8,128)(2,1)S(1)}, u32[]{:S(2)}, u32[]{:S(2)}) collective-permute-start(bf16[512,256]{1,0:T(8,128)(2,1)S(1)} %get-tuple-element.18), channel_id=1, source_target_pairs={{0,16},{16,0},{1,17},{17,1},{2,18},{18,2},{3,19},{19,3},{4,20},{20... | collective-permute-start | bytes 786440 | tf_op jit(solution)/shard_map/ppermute | solution.py:331
  73.3 1.2 collective-permute-done.3.recv_ref
  74.5 1.0 shard_map.63
  75.5 12.6 %all-to-all-done.2.r_ref = bf16[128,24,128]{2,1,0:T(8,128)(2,1)S(1)} async-done(((bf16[128,24,128]{2,1,0:T(8,128)(2,1)}), bf16[128,24,128]{2,1,0:T(8,128)(2,1)S(1)}, u32[]{:S(2)}, u32[]{:S(2)}) %all-to-all-start.2) | async-done | bytes 786464 | tf_op jit(solution)/shard_map/all_to_all | solution.py:322
  88.1 6.0 %all-to-all-start.1 = ((bf16[16,48,128]{2,1,0:T(8,128)(2,1)}), bf16[16,48,128]{2,1,0:T(8,128)(2,1)S(1)}, u32[]{:S(2)}, u32[]{:S(2)}) async-start(bf16[16,48,128]{2,1,0:T(8,128)(2,1)} %shard_map.63), calls=%async_computation.1 | async-start | bytes 393216 | tf_op jit(solution)/shard_map/all_to_all | solution.py:333
  94.1 0.8 shard_map.65
  94.9 9.7 %all-to-all-done.1.r_ref = bf16[16,48,128]{2,1,0:T(8,128)(2,1)S(1)} async-done(((bf16[16,48,128]{2,1,0:T(8,128)(2,1)}), bf16[16,48,128]{2,1,0:T(8,128)(2,1)S(1)}, u32[]{:S(2)}, u32[]{:S(2)}) %all-to-all-start.1) | async-done | bytes 196640 | tf_op jit(solution)/shard_map/all_to_all | solution.py:333
  104.6 8.8 %all-to-all-start.3 = ((f32[16,24,128]{2,1,0:T(8,128)}), f32[16,24,128]{2,1,0:T(8,128)S(1)}, u32[]{:S(2)}, u32[]{:S(2)}) async-start(f32[16,24,128]{2,1,0:T(8,128)} %shard_map.65), calls=%async_computation.3 | async-start | bytes 393216 | tf_op jit(solution)/shard_map/all_to_all | solution.py:336
  113.4 0.9 shard_map.64
  114.4 5.7 %all-to-all-done.3.r_ref = f32[16,24,128]{2,1,0:T(8,128)S(1)} async-done(((f32[16,24,128]{2,1,0:T(8,128)}), f32[16,24,128]{2,1,0:T(8,128)S(1)}, u32[]{:S(2)}, u32[]{:S(2)}) %all-to-all-start.3) | async-done | bytes 196640 | tf_op jit(solution)/shard_map/all_to_all | solution.py:336
  120.1 0.7 shard_map.66
Async XLA Ops:
  0.6 0.9 copy-start
  1.6 0.9 copy-start.1
  2.5 0.9 copy-start.2
  3.4 0.7 copy-start.3
  48.8 9.6 %collective-permute-start = (bf16[768,256]{1,0:T(8,128)(2,1)S(1)}, bf16[768,256]{1,0:T(8,128)(2,1)S(1)}, u32[]{:S(2)}, u32[]{:S(2)}) collective-permute-start(bf16[768,256]{1,0:T(8,128)(2,1)S(1)} %get-tuple-element.11.refs_1_), channel_id=1, source_target_pairs={{0,16},{16,0},{1,17},{17,1},{2,18},{18,2},{3,19},{19,3},{4,20},{20... | collective-permute-start | bytes 1179656 | tf_op jit(solution)/shard_map/ppermute | solution.py:297
  50.9 6.3 %collective-permute-start.1 = (bf16[96,256]{1,0:T(8,128)(2,1)S(1)}, bf16[96,256]{1,0:T(8,128)(2,1)S(1)}, u32[]{:S(2)}, u32[]{:S(2)}) collective-permute-start(bf16[96,256]{1,0:T(8,128)(2,1)S(1)} %get-tuple-element.13), channel_id=1, source_target_pairs={{16,32},{48,64},{80,96},{112,128},{144,160},{176,192},{208,224},{3... | collective-permute-start | bytes 147464 | tf_op jit(solution)/shard_map/ppermute | solution.py:298
  54.0 4.4 %collective-permute-start.2 = (bf16[96,256]{1,0:T(8,128)(2,1)S(1)}, bf16[96,256]{1,0:T(8,128)(2,1)S(1)}, u32[]{:S(2)}, u32[]{:S(2)}) collective-permute-start(bf16[96,256]{1,0:T(8,128)(2,1)S(1)} %get-tuple-element.14), channel_id=1, source_target_pairs={{16,48},{48,80},{80,112},{112,144},{144,176},{176,208},{208,240},{... | collective-permute-start | bytes 147464 | tf_op jit(solution)/shard_map/ppermute | solution.py:299
  61.7 26.4 %all-to-all-start.2 = ((bf16[128,24,128]{2,1,0:T(8,128)(2,1)}), bf16[128,24,128]{2,1,0:T(8,128)(2,1)S(1)}, u32[]{:S(2)}, u32[]{:S(2)}) async-start(bf16[128,24,128]{2,1,0:T(8,128)(2,1)} %get-tuple-element.19), calls=%async_computation.2 | async-start | bytes 1572864 | tf_op jit(solution)/shard_map/all_to_all | solution.py:322
  70.2 4.2 %collective-permute-start.3 = (bf16[512,256]{1,0:T(8,128)(2,1)S(1)}, bf16[512,256]{1,0:T(8,128)(2,1)S(1)}, u32[]{:S(2)}, u32[]{:S(2)}) collective-permute-start(bf16[512,256]{1,0:T(8,128)(2,1)S(1)} %get-tuple-element.18), channel_id=1, source_target_pairs={{0,16},{16,0},{1,17},{17,1},{2,18},{18,2},{3,19},{19,3},{4,20},{20... | collective-permute-start | bytes 786440 | tf_op jit(solution)/shard_map/ppermute | solution.py:331
  88.1 16.5 %all-to-all-start.1 = ((bf16[16,48,128]{2,1,0:T(8,128)(2,1)}), bf16[16,48,128]{2,1,0:T(8,128)(2,1)S(1)}, u32[]{:S(2)}, u32[]{:S(2)}) async-start(bf16[16,48,128]{2,1,0:T(8,128)(2,1)} %shard_map.63), calls=%async_computation.1 | async-start | bytes 393216 | tf_op jit(solution)/shard_map/all_to_all | solution.py:333
  104.6 15.5 %all-to-all-start.3 = ((f32[16,24,128]{2,1,0:T(8,128)}), f32[16,24,128]{2,1,0:T(8,128)S(1)}, u32[]{:S(2)}, u32[]{:S(2)}) async-start(f32[16,24,128]{2,1,0:T(8,128)} %shard_map.65), calls=%async_computation.3 | async-start | bytes 393216 | tf_op jit(solution)/shard_map/all_to_all | solution.py:336

commit v2 on v1

--- a/solution.py
+++ b/solution.py
@@ -27,8 +27,10 @@
     return lax.broadcasted_iota(jnp.int32, shape, dim)
 
 
-def call(body, outs, *args, smem=True, scratch=()):
-    specs = [pl.BlockSpec(memory_space=pltpu.VMEM)] * len(args)
+def call(body, outs, *args, smem=True, scratch=(), hbm=(), mib=48):
+    specs = [
+        pl.BlockSpec(memory_space=pltpu.HBM if k in hbm else pltpu.VMEM) for k in range(len(args))
+    ]
     if smem:
         specs[0] = pl.BlockSpec(memory_space=pltpu.SMEM)
     return pl.pallas_call(
@@ -37,7 +39,7 @@
         in_specs=specs,
         out_specs=[pl.BlockSpec(memory_space=pltpu.VMEM)] * len(outs),
         scratch_shapes=list(scratch),
-        compiler_params=pltpu.CompilerParams(vmem_limit_bytes=48 * 1024 * 1024),
+        compiler_params=pltpu.CompilerParams(vmem_limit_bytes=mib * 1024 * 1024),
     )(*args)
 
 
@@ -66,8 +68,13 @@
     return jnp.where(hit, 1.0, 0.0).astype(BF)
 
 
-def pack_kernel(core_ref, x_ref, cot_ref, ker_ref, bias_ref, out_ref):
-    core = core_ref[0]
+def pack_kernel(place_ref, *refs):
+    out_ref, sems = refs[4], refs[9]
+    copies = [pltpu.make_async_copy(refs[k], refs[5 + k], sems.at[k]) for k in range(4)]
+    for copy in copies:
+        copy.start()
+    x_ref, cot_ref, bias_ref, ker_ref = refs[5:9]
+    core = place_ref[0]
     src = iota((256, 256), 0)
     dst = iota((256, 256), 1)
     ch, h = src >> 4, src & 15
@@ -75,11 +82,13 @@
     other = (ch >> 3) ^ core
     to_half = jnp.where(dst == other * 128 + h * 8 + (ch & 7), 1.0, 0.0).astype(BF)
 
+    copies[0].wait()
     x = dot(window(-2, 28), x_ref[...].reshape(256, 384), NT).astype(BF)
     x = dot(x, to_h_ch).astype(BF).reshape(16, 32, 256)
     out_ref[:, 0:32, :] = x[:, :, 0:128]
     out_ref[:, 32:64, :] = x[:, :, 128:256]
 
+    copies[2].wait()
     bias = jnp.broadcast_to(bias_ref[...], (8, 16))
     hi = bias.astype(BF).astype(F32)
     mid = (bias - hi).astype(BF).astype(F32)
@@ -90,19 +99,25 @@
     pieces = dot(pieces.astype(BF), jnp.where(spread, 1.0, 0.0).astype(BF))
     rows = jnp.concatenate([jnp.zeros((24, 128), F32), pieces], axis=0)
 
+    copies[1].wait()
     c = dot(window(-1, 26), cot_ref[...].reshape(256, 384), NT).astype(BF)
     c = dot(c, to_half).reshape(16, 32, 256)
     out_ref[:, 64:96, :] = (c[:, :, 0:128] + rows[None]).astype(BF)
     out_ref[:, 96:128, :] = c[:, :, 128:256].astype(BF)
 
+    copies[3].wait()
     parts = []
     for t in range(9):
         both = ker_ref[t].astype(F32)
         mine = jnp.where(core == 0, both[0:8], both[8:16])
-        parts += [mine[:, 0:128], mine[:, 128:256]]
+        parts.append(jnp.where(place_ref[1] == 0, mine[:, 0:128], mine[:, 128:256]))
+    parts.append(jnp.zeros((8, 128), F32))
     weights = jnp.concatenate(parts, axis=0).astype(BF)
     for j in range(16):
-        out_ref[j, 128:272, :] = weights
+        out_ref[j, 128:208, :] = weights
+
+
+SOURCES = [z * 2 + xh for xh in range(2) for z in range(8)]
 
 
 def unpack_kernel(core_ref, r_ref, xo_ref, co_ref, ha_ref, hb_ref, w_ref):
@@ -119,8 +134,8 @@
             xo_ref[at : at + 32, :] = row
             if (hh * 8 + hl) in (0, 1, 14, 15):
                 edge.append(row)
-    own = swap_blocks([r_ref[s, 64:96, :] for s in range(16)], 8)
-    oth = swap_blocks([r_ref[s, 96:128, :] for s in range(16)], 8)
+    own = swap_blocks([r_ref[s, 64:96, :] for s in SOURCES], 8)
+    oth = swap_blocks([r_ref[s, 96:128, :] for s in SOURCES], 8)
     for h in range(16):
         co_ref[h * 32 : h * 32 + 32, :] = own[h]
         at = 512 + (h % 8) * 32
@@ -132,18 +147,18 @@
         ref[32:64, :] = jnp.where(first, edge[1], edge[3])
         ref[64:96, 0:128] = jnp.where(first, cot[0], cot[15])
         ref[64:96, 128:256] = blank
-    chunks = [r_ref[s, 128:272, :].astype(F32) for s in range(16)]
+    chunks = [r_ref[s, 128:208, :].astype(F32) for s in SOURCES]
     for t in range(9):
-        for ih in range(2):
-            at = (t * 2 + ih) * 8
-            tap = jnp.concatenate([c[at : at + 8] for c in chunks], axis=0)
-            w_ref[t * 128 : t * 128 + 128, ih * 128 : ih * 128 + 128] = tap.astype(BF)
-
-
-def grad_kernel(
-    scale, core_ref, xo_ref, xr_ref, co_ref, ha_ref, hb_ref, w_ref, kg_ref, g_ref, x, cot, y, gs
-):
-    core = core_ref[0]
+        tap = jnp.concatenate([chunk[t * 8 : t * 8 + 8] for chunk in chunks], axis=0)
+        w_ref[t * 128 : t * 128 + 128, :] = tap.astype(BF)
+
+
+def grad_kernel(scale, place_ref, xo_ref, xr_ref, co_ref, ha_ref, hb_ref, wo_ref, wr_ref, *refs):
+    kg_ref, g_ref, w_ref, x, cot, y, gs = refs
+    core = place_ref[0]
+    low = place_ref[1] == 0
+    w_ref[:, 0:128] = jnp.where(low, wo_ref[...], wr_ref[...])
+    w_ref[:, 128:256] = jnp.where(low, wr_ref[...], wo_ref[...])
     first = core == 0
     mine = pl.multiple_of(core * 512, 512)
     theirs = pl.multiple_of((1 - core) * 512, 512)
@@ -194,13 +209,10 @@
     for a in range(3):
         block = dot(shifted, x[32 * a : 32 * a + PX, :], TN) * scale
         taps += [block[0:128], block[128:256], block[256:384]]
-    for m in range(8):
-        lane = (m // 4) * 128
-        for j in range(16):
-            o = slice(8 * j, 8 * j + 8)
-            kg_ref[m * 16 + j] = jnp.concatenate(
-                [taps[m][o, 0:128], taps[m][o, 128:256], taps[8][o, lane : lane + 128]], axis=0
-            ).astype(BF)
+    for k in range(16):
+        o = slice(8 * k, 8 * k + 8)
+        rows = [tap[o, lane : lane + 128] for tap in taps for lane in (0, 128)]
+        kg_ref[SOURCES[k]] = jnp.concatenate(rows, axis=0).astype(BF)
 
 
 def input_kernel(core_ref, g_ref, w_ref, own_ref, send_ref, z, total):
@@ -252,45 +264,59 @@
 
 def sum_kernel(r_ref, out_ref):
     total = r_ref[0].astype(F32)
-    for s in range(1, 128):
+    for s in range(1, 16):
         total = total + r_ref[s].astype(F32)
-    for b in range(16):
-        out_ref[b] = total
-
-
-def order_kernel(r_ref, out_ref):
-    for m in range(8):
-        for core in range(2):
-            for ih in range(2):
-                out_ref[m, 8 * core : 8 * core + 8, 128 * ih : 128 * ih + 128] = r_ref[
-                    2 * m + core, 8 * ih : 8 * ih + 8, :
-                ]
-    for core in range(2):
+    out_ref[...] = total.astype(BF)
+
+
+def ring_kernel(own_ref, next_ref, prev_ref, far_ref, out_ref):
+    even = own_ref[...].astype(F32) + far_ref[...].astype(F32)
+    odd = next_ref[...].astype(F32) + prev_ref[...].astype(F32)
+    out_ref[...] = (even + odd).astype(BF)
+
+
+def order_kernel(core_ref, own_ref, xl_ref, core_own_ref, core_xl_ref, out_ref):
+    first = core_ref[0] == 0
+    mine = own_ref[...].astype(F32) + xl_ref[...].astype(F32)
+    other = core_own_ref[...].astype(F32) + core_xl_ref[...].astype(F32)
+    low = jnp.where(first, mine, other)
+    high = jnp.where(first, other, mine)
+    for t in range(9):
         for ih in range(2):
-            out_ref[8, 8 * core : 8 * core + 8, 128 * ih : 128 * ih + 128] = r_ref[
-                8 * ih + core, 16:24, :
-            ]
+            rows = slice((t * 2 + ih) * 8, (t * 2 + ih) * 8 + 8)
+            out_ref[t, 0:8, ih * 128 : ih * 128 + 128] = low[rows]
+            out_ref[t, 8:16, ih * 128 : ih * 128 + 128] = high[rows]
 
 
 def shards(inputs, cotangent, kernel, channel_bias):
-    core = lax.axis_index("core").astype(jnp.int32).reshape(1)
-    taps = kernel.reshape(16, 9, 256).transpose(1, 0, 2)
+    core, y = (lax.axis_index(n).astype(jnp.int32) for n in ("core", "y"))
+    place = jnp.stack([core, y & 1])
     (packed,) = call(
         pack_kernel,
-        [((16, 272, 128), BF)],
-        core,
+        [((16, 208, 128), BF)],
+        place,
         inputs,
         cotangent,
-        taps,
         channel_bias.reshape(1, 16),
+        kernel.reshape(16, 9, 256).transpose(1, 0, 2),
+        hbm=(1, 2, 3, 4),
+        mib=56,
+        scratch=[
+            pltpu.VMEM((16, 16, 384), BF),
+            pltpu.VMEM((16, 16, 384), BF),
+            pltpu.VMEM((1, 16), F32),
+            pltpu.VMEM((9, 16, 256), BF),
+            pltpu.SemaphoreType.DMA((4,)),
+        ],
     )
     got = lax.all_to_all(packed, CHAN, 0, 0)
-    xo, co, ha, hb, w = call(
+    xo, co, ha, hb, w_here = call(
         unpack_kernel,
-        [((768, 256), BF), ((512, 128), BF), ((96, 256), BF), ((96, 256), BF), ((1152, 256), BF)],
-        core,
+        [((768, 256), BF), ((512, 128), BF), ((96, 256), BF), ((96, 256), BF), ((1152, 128), BF)],
+        core.reshape(1),
         got,
     )
+    w_there = lax.ppermute(w_here, "y", [(i, i ^ 1) for i in range(4)])
     across = [(b, b + 1) for b in range(1, 15, 2)]
     across += [(b + 1, b) for b in range(1, 15, 2)]
     along = [(b, b + 2) for b in range(1, 14, 2)] + [(b, b - 2) for b in range(2, 16, 2)]
@@ -302,16 +328,17 @@
     def grads(*refs):
         grad_kernel(scale, *refs)
 
-    kg, g = call(
+    kg, g, w = call(
         grads,
-        [((128, 24, 128), BF), ((PX, 128), BF)],
-        core,
+        [((16, 144, 128), BF), ((PX, 128), BF), ((1152, 256), BF)],
+        place,
         xo,
         xr,
         co,
         ha,
         hb,
-        w,
+        w_here,
+        w_there,
         scratch=[
             pltpu.VMEM((1216, 256), BF),
             pltpu.VMEM((1088, 128), BF),
@@ -319,11 +346,11 @@
             pltpu.VMEM((PX + 16, 128), F32),
         ],
     )
-    kg = lax.all_to_all(kg, ("xl", "y", "z", "xh"), 0, 0)
+    kg = lax.all_to_all(kg, CHAN, 0, 0)
     own, send = call(
         input_kernel,
         [((512, 256), F32), ((512, 256), BF)],
-        core,
+        core.reshape(1),
         g,
         w,
         scratch=[pltpu.VMEM((3, 1056, 256), F32), pltpu.VMEM((1024, 256), F32)],
@@ -332,9 +359,20 @@
     (back,) = call(repack_kernel, [((16, 48, 128), BF)], own, recv, smem=False)
     back = lax.all_to_all(back, CHAN, 0, 0)
     (input_grad,) = call(restore_kernel, [((16, 16, 384), BF)], back, smem=False)
-    (pieces,) = call(sum_kernel, [((16, 24, 128), F32)], kg, smem=False)
-    pieces = lax.all_to_all(pieces, BAND, 0, 0)
-    (ordered,) = call(order_kernel, [((9, 16, 256), F32)], pieces, smem=False)
+
+    part = ((144, 128), BF)
+    (sums,) = call(sum_kernel, [part], kg, smem=False)
+    ring = [lax.ppermute(sums, "y", [(i, (i + k) % 4) for i in range(4)]) for k in (3, 1, 2)]
+    (sums,) = call(ring_kernel, [part], sums, *ring, smem=False)
+    (ordered,) = call(
+        order_kernel,
+        [((9, 16, 256), F32)],
+        core.reshape(1),
+        sums,
+        lax.ppermute(sums, "xl", [(0, 1), (1, 0)]),
+        lax.ppermute(sums, "core", [(0, 1), (1, 0)]),
+        lax.ppermute(sums, ("xl", "core"), [(i, i ^ 3) for i in range(4)]),
+    )
     kernel_grad = ordered.transpose(1, 0, 2).reshape(16, 3, 3, 256)
     return (input_grad, kernel_grad)
 

time: 121 us -> 101 us (0.83); the launches traced: 121 us -> 99.1 us
  waiting for transfers between devices: 30.4 us -> 18.8 us
  blocking collectives: 42.6 us -> 36.3 us
  starting transfers between devices: 33.3 us -> 29.8 us
  local copies, waits for them, and re-layouts: 3.38 us -> 0.01 us
  Pallas kernels: 10.4 us -> 12.9 us
    all_to_all x2 -> x1, starting transfers between devices: 15.8 us -> 3.58 us  [shards(): kg = lax.all_to_all(kg, CHAN, 0, 0)]
    ppermute x0 -> x7, starting transfers between devices: none -> 11.4 us  [the longest x3 5.67 us: shards(): lax.ppermute(sums, 'y', [(i, (i + k) % 4) for i in range(4)])]
    all_to_all x1, waiting for transfers between devices: 9.7 us -> 0.01 us  [shards(): back = lax.all_to_all(back, CHAN, 0, 0)]
    all_to_all x1, blocking collectives: 42.6 us -> 36.3 us  [shards(): got = lax.all_to_all(packed, CHAN, 0, 0)]
    all_to_all x2 -> x1, waiting for transfers between devices: 18.3 us -> 13.2 us  [shards(): kg = lax.all_to_all(kg, CHAN, 0, 0)]
    unnamed x8 -> x2, local copies, waits for them, and re-layouts: 3.38 us -> 0.01 us
    ppermute x0 -> x7, waiting for transfers between devices: none -> 2.8 us  [the longest x3 2 us: shards(): lax.ppermute(sums, 'y', [(i, (i + k) % 4) for i in range(4)])]
    pallas_call x8 -> x9, Pallas kernels: 10.4 us -> 12.9 us  [call(): pl.pallas_call(body, out_shape=[jax.ShapeDtypeStruct(s, d) for s, d in ou...]
  transfers between devices with their start and end apart: 7 -> 13, of which waited for: 5 -> 5; matrix products, arithmetic and copies ran while one was open for 0% -> 0% of each run, Pallas kernels for 4% -> 4%
where the time goes in v2:
time: 101 us; the launch traced here: 99.1 us
  blocking collectives  36.3 us (36%)
  starting transfers between devices  29.8 us (30%)
  waiting for transfers between devices  18.8 us (19%)
  Pallas kernels  12.9 us (13%)
    all_to_all x1, blocking collectives, shards(): got = lax.all_to_all(packed, CHAN, 0, 0)  36.3 us
    all_to_all x1, waiting for transfers between devices, shards(): kg = lax.all_to_all(kg, CHAN, 0, 0)  13.2 us
    pallas_call x9, Pallas kernels, call(): pl.pallas_call(body, out_shape=[jax.ShapeDtypeStruct(s, d) for s, d in ou...  12.9 us
    ppermute x3, starting transfers between devices, shards(): lax.ppermute(sums, 'y', [(i, (i + k) % 4) for i in range(4)])  5.67 us
    all_to_all x1, starting transfers between devices, shards(): back = lax.all_to_all(back, CHAN, 0, 0)  4.85 us
    ppermute x1, starting transfers between devices, shards(): hb = lax.ppermute(hb, BAND, along)  4.04 us
    all_to_all x1, starting transfers between devices, shards(): kg = lax.all_to_all(kg, CHAN, 0, 0)  3.58 us
    ppermute x1, starting transfers between devices, shards(): lax.ppermute(sums, ('xl', 'core'), [(i, i ^ 3) for i in range(4)])  3.24 us
  transfers between devices with their start and end apart: 13, of which 5 were waited for; matrix products, arithmetic and copies ran while one was open for 0% of the time, Pallas kernels for 4%

profile of v2, /device:TPU:1, one launch (start us, length us, event | category | flops | bytes accessed | tf_op | source)
XLA Modules:
  0.0 99.1 jit_solution(24345554495521740)
XLA Ops:
  0.6 0.6 pad_add_fusion.place_ref.refs_0_
  1.2 3.8 %shard_map.59 = bf16[16,208,128]{2,1,0:T(8,128)(2,1)} custom-call(s32[2]{0:T(128)} %pad_add_fusion.place_ref.refs_0_, bf16[16,16,384]{2,1,0:T(8,128)(2,1)} %refs_0_.1, bf16[16,16,384]{2,1,0:T(8,128)(2,1)} %refs_1_.1, f32[1,16]{1,0:T(1,128)} %bitcast.11, bf16[9,16,256]{2,1,0:T(8,128)(2,1)} %bitcast.10), custom_call_target="tpu_custom_call" | custom-call | tf_op jit(solution)/shard_map/pallas_call | solution.py:36
  5.1 36.3 %all_to_all.15.r_ref = bf16[16,208,128]{2,1,0:T(8,128)(2,1)S(1)} all-to-all(bf16[16,208,128]{2,1,0:T(8,128)(2,1)} %shard_map.59), channel_id=1, replica_groups=mesh['xl'=2,'y'=4,'core'=2,'z'=8,'xh'=2] {'z','xh'}, dimensions={0} | all-to-all | bytes 1703936 | tf_op jit(solution)/shard_map/all_to_all | solution.py:312
  41.4 1.1 %shard_map.60 = (bf16[768,256]{1,0:T(8,128)(2,1)S(1)}, bf16[512,128]{1,0:T(8,128)(2,1)S(1)}, bf16[96,256]{1,0:T(8,128)(2,1)S(1)}, bf16[96,256]{1,0:T(8,128)(2,1)S(1)}, bf16[1152,128]{1,0:T(8,128)(2,1)S(1)}) custom-call(s32[1]{0:T(128)} %bitcast.core_ref, bf16[16,208,128]{2,1,0:T(8,128)(2,1)S(1)} %all_to_all.15.r_ref), custom_call_target="tpu_custom_call" | custom-call | tf_op jit(solution)/shard_map/pallas_call | solution.py:36
  42.5 2.3 %collective-permute-start = (bf16[768,256]{1,0:T(8,128)(2,1)S(1)}, bf16[768,256]{1,0:T(8,128)(2,1)S(1)}, u32[]{:S(2)}, u32[]{:S(2)}) collective-permute-start(bf16[768,256]{1,0:T(8,128)(2,1)S(1)} %get-tuple-element.12.refs_1_), channel_id=1, source_target_pairs={{0,16},{16,0},{1,17},{17,1},{2,18},{18,2},{3,19},{19,3},{4,20},{20... | collective-permute-start | bytes 1179656 | tf_op jit(solution)/shard_map/ppermute | solution.py:323
  44.8 1.3 %collective-permute-start.3 = (bf16[1152,128]{1,0:T(8,128)(2,1)S(1)}, bf16[1152,128]{1,0:T(8,128)(2,1)S(1)}, u32[]{:S(2)}, u32[]{:S(2)}) collective-permute-start(bf16[1152,128]{1,0:T(8,128)(2,1)S(1)} %get-tuple-element.16.refs_6_), channel_id=1, source_target_pairs={{0,32},{32,0},{64,96},{96,64},{1,33},{33,1},{65,97},{97,65},{2,34}... | collective-permute-start | bytes 884744 | tf_op jit(solution)/shard_map/ppermute | solution.py:319
  46.1 2.3 %collective-permute-start.1 = (bf16[96,256]{1,0:T(8,128)(2,1)S(1)}, bf16[96,256]{1,0:T(8,128)(2,1)S(1)}, u32[]{:S(2)}, u32[]{:S(2)}) collective-permute-start(bf16[96,256]{1,0:T(8,128)(2,1)S(1)} %get-tuple-element.14), channel_id=1, source_target_pairs={{16,32},{48,64},{80,96},{112,128},{144,160},{176,192},{208,224},{3... | collective-permute-start | bytes 147464 | tf_op jit(solution)/shard_map/ppermute | solution.py:324
  48.4 0.0 copy-start
  48.4 4.0 %collective-permute-start.2 = (bf16[96,256]{1,0:T(8,128)(2,1)S(1)}, bf16[96,256]{1,0:T(8,128)(2,1)S(1)}, u32[]{:S(2)}, u32[]{:S(2)}) collective-permute-start(bf16[96,256]{1,0:T(8,128)(2,1)S(1)} %get-tuple-element.15), channel_id=1, source_target_pairs={{16,48},{48,80},{80,112},{112,144},{144,176},{176,208},{208,240},{... | collective-permute-start | bytes 147464 | tf_op jit(solution)/shard_map/ppermute | solution.py:325
  52.5 1.6 %collective-permute-done.1.refs_4_ = bf16[96,256]{1,0:T(8,128)(2,1)S(1)} collective-permute-done((bf16[96,256]{1,0:T(8,128)(2,1)S(1)}, bf16[96,256]{1,0:T(8,128)(2,1)S(1)}, u32[]{:S(2)}, u32[]{:S(2)}) %collective-permute-start.1) | collective-permute-done | bytes 49184 | tf_op jit(solution)/shard_map/ppermute | solution.py:324
  54.1 0.0 collective-permute-done.2.refs_5_
  54.1 0.0 collective-permute-done.3.refs_7_
  54.1 0.0 collective-permute-done.refs_2_
  54.1 0.0 copy-done
  54.1 3.7 %shard_map.61 = (bf16[16,144,128]{2,1,0:T(8,128)(2,1)}, bf16[1152,128]{1,0:T(8,128)(2,1)S(1)}, bf16[1152,256]{1,0:T(8,128)(2,1)S(1)}) custom-call(s32[2]{0:T(128)S(1)} %copy-done, bf16[768,256]{1,0:T(8,128)(2,1)S(1)} %get-tuple-element.12.refs_1_, bf16[768,256]{1,0:T(8,128)(2,1)S(1)} %collective-permute-done.refs_2_, ...), custom_call_target="tpu_custom_call" | custom-call | tf_op jit(solution)/shard_map/pallas_call | solution.py:36
  57.8 3.6 %all-to-all-start.2 = ((bf16[16,144,128]{2,1,0:T(8,128)(2,1)}), bf16[16,144,128]{2,1,0:T(8,128)(2,1)S(1)}, u32[]{:S(2)}, u32[]{:S(2)}) async-start(bf16[16,144,128]{2,1,0:T(8,128)(2,1)} %get-tuple-element.21), calls=%async_computation.2 | async-start | bytes 1179648 | tf_op jit(solution)/shard_map/all_to_all | solution.py:349
  61.4 1.5 %shard_map.62 = (f32[512,256]{1,0:T(8,128)S(1)}, bf16[512,256]{1,0:T(8,128)(2,1)S(1)}) custom-call(s32[1]{0:T(128)} %bitcast.core_ref, bf16[1152,128]{1,0:T(8,128)(2,1)S(1)} %get-tuple-element.17.g_ref, bf16[1152,256]{1,0:T(8,128)(2,1)S(1)} %get-tuple-element.18.w_ref), custom_call_target="tpu_custom_call" | custom-call | tf_op jit(solution)/shard_map/pallas_call | solution.py:36
  62.9 1.3 %collective-permute-start.4 = (bf16[512,256]{1,0:T(8,128)(2,1)S(1)}, bf16[512,256]{1,0:T(8,128)(2,1)S(1)}, u32[]{:S(2)}, u32[]{:S(2)}) collective-permute-start(bf16[512,256]{1,0:T(8,128)(2,1)S(1)} %get-tuple-element.20), channel_id=1, source_target_pairs={{0,16},{16,0},{1,17},{17,1},{2,18},{18,2},{3,19},{19,3},{4,20},{20... | collective-permute-start | bytes 786440 | tf_op jit(solution)/shard_map/ppermute | solution.py:358
  64.2 1.2 %collective-permute-done.4.recv_ref = bf16[512,256]{1,0:T(8,128)(2,1)S(1)} collective-permute-done((bf16[512,256]{1,0:T(8,128)(2,1)S(1)}, bf16[512,256]{1,0:T(8,128)(2,1)S(1)}, u32[]{:S(2)}, u32[]{:S(2)}) %collective-permute-start.4) | collective-permute-done | bytes 262176 | tf_op jit(solution)/shard_map/ppermute | solution.py:358
  65.4 1.0 %shard_map.63 = bf16[16,48,128]{2,1,0:T(8,128)(2,1)} custom-call(f32[512,256]{1,0:T(8,128)S(1)} %get-tuple-element.19.own_ref, bf16[512,256]{1,0:T(8,128)(2,1)S(1)} %collective-permute-done.4.recv_ref), custom_call_target="tpu_custom_call" | custom-call | tf_op jit(solution)/shard_map/pallas_call | solution.py:36
  66.4 13.2 %all-to-all-done.2.r_ref = bf16[16,144,128]{2,1,0:T(8,128)(2,1)S(1)} async-done(((bf16[16,144,128]{2,1,0:T(8,128)(2,1)}), bf16[16,144,128]{2,1,0:T(8,128)(2,1)S(1)}, u32[]{:S(2)}, u32[]{:S(2)}) %all-to-all-start.2) | async-done | bytes 589856 | tf_op jit(solution)/shard_map/all_to_all | solution.py:349
  79.6 4.9 %all-to-all-start.1 = ((bf16[16,48,128]{2,1,0:T(8,128)(2,1)}), bf16[16,48,128]{2,1,0:T(8,128)(2,1)S(1)}, u32[]{:S(2)}, u32[]{:S(2)}) async-start(bf16[16,48,128]{2,1,0:T(8,128)(2,1)} %shard_map.63), calls=%async_computation.1 | async-start | bytes 393216 | tf_op jit(solution)/shard_map/all_to_all | solution.py:360
  84.4 0.1 shard_map.65.own_ref
  84.5 3.0 %collective-permute-start.7 = (bf16[144,128]{1,0:T(8,128)(2,1)S(1)}, bf16[144,128]{1,0:T(8,128)(2,1)S(1)}, u32[]{:S(2)}, u32[]{:S(2)}) collective-permute-start(bf16[144,128]{1,0:T(8,128)(2,1)S(1)} %shard_map.65.own_ref), channel_id=1, source_target_pairs={{0,64},{32,96},{64,0},{96,32},{1,65},{33,97},{65,1},{97,33},{2,66}... | collective-permute-start | bytes 110600 | tf_op jit(solution)/shard_map/ppermute | solution.py:365
  87.5 0.0 collective-permute-start.6
  87.5 2.7 %collective-permute-start.5 = (bf16[144,128]{1,0:T(8,128)(2,1)S(1)}, bf16[144,128]{1,0:T(8,128)(2,1)S(1)}, u32[]{:S(2)}, u32[]{:S(2)}) collective-permute-start(bf16[144,128]{1,0:T(8,128)(2,1)S(1)} %shard_map.65.own_ref), channel_id=1, source_target_pairs={{0,96},{32,0},{64,32},{96,64},{1,97},{33,1},{65,33},{97,65},{2,98}... | collective-permute-start | bytes 110600 | tf_op jit(solution)/shard_map/ppermute | solution.py:365
  90.2 0.0 collective-permute-done.7.far_ref
  90.2 2.0 %collective-permute-done.6.prev_ref = bf16[144,128]{1,0:T(8,128)(2,1)S(1)} collective-permute-done((bf16[144,128]{1,0:T(8,128)(2,1)S(1)}, bf16[144,128]{1,0:T(8,128)(2,1)S(1)}, u32[]{:S(2)}, u32[]{:S(2)}) %collective-permute-start.6) | collective-permute-done | bytes 36896 | tf_op jit(solution)/shard_map/ppermute | solution.py:365
  92.2 0.0 collective-permute-done.5.next_ref
  92.2 3.2 %collective-permute-start.10 = (bf16[144,128]{1,0:T(8,128)(2,1)S(1)}, bf16[144,128]{1,0:T(8,128)(2,1)S(1)}, u32[]{:S(2)}, u32[]{:S(2)}) collective-permute-start(bf16[144,128]{1,0:T(8,128)(2,1)S(1)} %shard_map.66.own_ref), channel_id=1, source_target_pairs={{0,144},{16,128},{128,16},{144,0},{1,145},{17,129},{129,17},{145,1... | collective-permute-start | bytes 110600 | tf_op jit(solution)/shard_map/ppermute | solution.py:374
  95.5 0.0 collective-permute-start.9
  95.5 1.1 %collective-permute-start.8 = (bf16[144,128]{1,0:T(8,128)(2,1)S(1)}, bf16[144,128]{1,0:T(8,128)(2,1)S(1)}, u32[]{:S(2)}, u32[]{:S(2)}) collective-permute-start(bf16[144,128]{1,0:T(8,128)(2,1)S(1)} %shard_map.66.own_ref), channel_id=1, source_target_pairs={{0,128},{128,0},{1,129},{129,1},{2,130},{130,2},{3,131},{131,3},{4... | collective-permute-start | bytes 110600 | tf_op jit(solution)/shard_map/ppermute | solution.py:372
  96.6 0.0 all-to-all-done.1.r_ref
  96.6 0.9 shard_map.64
  97.6 0.0 collective-permute-done.10.core_xl_ref
  97.6 0.0 collective-permute-done.9.core_own_ref
  97.6 0.8 collective-permute-done.8.xl_ref
  98.4 0.7 shard_map.67
  (1 shorter events, 0.0 us)
Async XLA Ops:
  42.5 11.6 %collective-permute-start = (bf16[768,256]{1,0:T(8,128)(2,1)S(1)}, bf16[768,256]{1,0:T(8,128)(2,1)S(1)}, u32[]{:S(2)}, u32[]{:S(2)}) collective-permute-start(bf16[768,256]{1,0:T(8,128)(2,1)S(1)} %get-tuple-element.12.refs_1_), channel_id=1, source_target_pairs={{0,16},{16,0},{1,17},{17,1},{2,18},{18,2},{3,19},{19,3},{4,20},{20... | collective-permute-start | bytes 1179656 | tf_op jit(solution)/shard_map/ppermute | solution.py:323
  44.8 9.3 %collective-permute-start.3 = (bf16[1152,128]{1,0:T(8,128)(2,1)S(1)}, bf16[1152,128]{1,0:T(8,128)(2,1)S(1)}, u32[]{:S(2)}, u32[]{:S(2)}) collective-permute-start(bf16[1152,128]{1,0:T(8,128)(2,1)S(1)} %get-tuple-element.16.refs_6_), channel_id=1, source_target_pairs={{0,32},{32,0},{64,96},{96,64},{1,33},{33,1},{65,97},{97,65},{2,34}... | collective-permute-start | bytes 884744 | tf_op jit(solution)/shard_map/ppermute | solution.py:319
  46.1 8.0 %collective-permute-start.1 = (bf16[96,256]{1,0:T(8,128)(2,1)S(1)}, bf16[96,256]{1,0:T(8,128)(2,1)S(1)}, u32[]{:S(2)}, u32[]{:S(2)}) collective-permute-start(bf16[96,256]{1,0:T(8,128)(2,1)S(1)} %get-tuple-element.14), channel_id=1, source_target_pairs={{16,32},{48,64},{80,96},{112,128},{144,160},{176,192},{208,224},{3... | collective-permute-start | bytes 147464 | tf_op jit(solution)/shard_map/ppermute | solution.py:324
  48.4 5.7 %copy-start = (s32[2]{0:T(128)S(1)}, s32[2]{0:T(128)}, u32[]{:S(2)}) copy-start(s32[2]{0:T(128)} %pad_add_fusion.place_ref.refs_0_) | copy-start | bytes 28
  48.4 5.6 %collective-permute-start.2 = (bf16[96,256]{1,0:T(8,128)(2,1)S(1)}, bf16[96,256]{1,0:T(8,128)(2,1)S(1)}, u32[]{:S(2)}, u32[]{:S(2)}) collective-permute-start(bf16[96,256]{1,0:T(8,128)(2,1)S(1)} %get-tuple-element.15), channel_id=1, source_target_pairs={{16,48},{48,80},{80,112},{112,144},{144,176},{176,208},{208,240},{... | collective-permute-start | bytes 147464 | tf_op jit(solution)/shard_map/ppermute | solution.py:325
  57.8 21.8 %all-to-all-start.2 = ((bf16[16,144,128]{2,1,0:T(8,128)(2,1)}), bf16[16,144,128]{2,1,0:T(8,128)(2,1)S(1)}, u32[]{:S(2)}, u32[]{:S(2)}) async-start(bf16[16,144,128]{2,1,0:T(8,128)(2,1)} %get-tuple-element.21), calls=%async_computation.2 | async-start | bytes 1179648 | tf_op jit(solution)/shard_map/all_to_all | solution.py:349
  62.9 2.5 %collective-permute-start.4 = (bf16[512,256]{1,0:T(8,128)(2,1)S(1)}, bf16[512,256]{1,0:T(8,128)(2,1)S(1)}, u32[]{:S(2)}, u32[]{:S(2)}) collective-permute-start(bf16[512,256]{1,0:T(8,128)(2,1)S(1)} %get-tuple-element.20), channel_id=1, source_target_pairs={{0,16},{16,0},{1,17},{17,1},{2,18},{18,2},{3,19},{19,3},{4,20},{20... | collective-permute-start | bytes 786440 | tf_op jit(solution)/shard_map/ppermute | solution.py:358
  79.6 17.1 %all-to-all-start.1 = ((bf16[16,48,128]{2,1,0:T(8,128)(2,1)}), bf16[16,48,128]{2,1,0:T(8,128)(2,1)S(1)}, u32[]{:S(2)}, u32[]{:S(2)}) async-start(bf16[16,48,128]{2,1,0:T(8,128)(2,1)} %shard_map.63), calls=%async_computation.1 | async-start | bytes 393216 | tf_op jit(solution)/shard_map/all_to_all | solution.py:360
  84.5 5.7 %collective-permute-start.7 = (bf16[144,128]{1,0:T(8,128)(2,1)S(1)}, bf16[144,128]{1,0:T(8,128)(2,1)S(1)}, u32[]{:S(2)}, u32[]{:S(2)}) collective-permute-start(bf16[144,128]{1,0:T(8,128)(2,1)S(1)} %shard_map.65.own_ref), channel_id=1, source_target_pairs={{0,64},{32,96},{64,0},{96,32},{1,65},{33,97},{65,1},{97,33},{2,66}... | collective-permute-start | bytes 110600 | tf_op jit(solution)/shard_map/ppermute | solution.py:365
  87.5 4.7 %collective-permute-start.6 = (bf16[144,128]{1,0:T(8,128)(2,1)S(1)}, bf16[144,128]{1,0:T(8,128)(2,1)S(1)}, u32[]{:S(2)}, u32[]{:S(2)}) collective-permute-start(bf16[144,128]{1,0:T(8,128)(2,1)S(1)} %shard_map.65.own_ref), channel_id=1, source_target_pairs={{0,32},{32,64},{64,96},{96,0},{1,33},{33,65},{65,97},{97,1},{2,34}... | collective-permute-start | bytes 110600 | tf_op jit(solution)/shard_map/ppermute | solution.py:365
  87.5 4.7 %collective-permute-start.5 = (bf16[144,128]{1,0:T(8,128)(2,1)S(1)}, bf16[144,128]{1,0:T(8,128)(2,1)S(1)}, u32[]{:S(2)}, u32[]{:S(2)}) collective-permute-start(bf16[144,128]{1,0:T(8,128)(2,1)S(1)} %shard_map.65.own_ref), channel_id=1, source_target_pairs={{0,96},{32,0},{64,32},{96,64},{1,97},{33,1},{65,33},{97,65},{2,98}... | collective-permute-start | bytes 110600 | tf_op jit(solution)/shard_map/ppermute | solution.py:365
  92.2 5.3 %collective-permute-start.10 = (bf16[144,128]{1,0:T(8,128)(2,1)S(1)}, bf16[144,128]{1,0:T(8,128)(2,1)S(1)}, u32[]{:S(2)}, u32[]{:S(2)}) collective-permute-start(bf16[144,128]{1,0:T(8,128)(2,1)S(1)} %shard_map.66.own_ref), channel_id=1, source_target_pairs={{0,144},{16,128},{128,16},{144,0},{1,145},{17,129},{129,17},{145,1... | collective-permute-start | bytes 110600 | tf_op jit(solution)/shard_map/ppermute | solution.py:374
  95.5 2.1 %collective-permute-start.9 = (bf16[144,128]{1,0:T(8,128)(2,1)S(1)}, bf16[144,128]{1,0:T(8,128)(2,1)S(1)}, u32[]{:S(2)}, u32[]{:S(2)}) collective-permute-start(bf16[144,128]{1,0:T(8,128)(2,1)S(1)} %shard_map.66.own_ref), channel_id=1, source_target_pairs={{0,16},{16,0},{1,17},{17,1},{2,18},{18,2},{3,19},{19,3},{4,20},{20... | collective-permute-start | bytes 110600 | tf_op jit(solution)/shard_map/ppermute | solution.py:373
  95.5 2.9 %collective-permute-start.8 = (bf16[144,128]{1,0:T(8,128)(2,1)S(1)}, bf16[144,128]{1,0:T(8,128)(2,1)S(1)}, u32[]{:S(2)}, u32[]{:S(2)}) collective-permute-start(bf16[144,128]{1,0:T(8,128)(2,1)S(1)} %shard_map.66.own_ref), channel_id=1, source_target_pairs={{0,128},{128,0},{1,129},{129,1},{2,130},{130,2},{3,131},{131,3},{4... | collective-permute-start | bytes 110600 | tf_op jit(solution)/shard_map/ppermute | solution.py:372

commit v3 on v2

--- a/solution.py
+++ b/solution.py
@@ -27,17 +27,21 @@
     return lax.broadcasted_iota(jnp.int32, shape, dim)
 
 
-def call(body, outs, *args, smem=True, scratch=(), hbm=(), mib=48):
+def call(body, outs, *args, smem=1, scratch=(), hbm=(), copied=(), mib=48):
     specs = [
-        pl.BlockSpec(memory_space=pltpu.HBM if k in hbm else pltpu.VMEM) for k in range(len(args))
+        pl.BlockSpec(
+            memory_space=pltpu.SMEM if k < smem else pltpu.HBM if k in hbm else pltpu.VMEM
+        )
+        for k in range(len(args))
     ]
-    if smem:
-        specs[0] = pl.BlockSpec(memory_space=pltpu.SMEM)
     return pl.pallas_call(
         body,
         out_shape=[jax.ShapeDtypeStruct(s, d) for s, d in outs],
         in_specs=specs,
-        out_specs=[pl.BlockSpec(memory_space=pltpu.VMEM)] * len(outs),
+        out_specs=[
+            pl.BlockSpec(memory_space=pltpu.HBM if k in copied else pltpu.VMEM)
+            for k in range(len(outs))
+        ],
         scratch_shapes=list(scratch),
         compiler_params=pltpu.CompilerParams(vmem_limit_bytes=mib * 1024 * 1024),
     )(*args)
@@ -62,80 +66,112 @@
 
 
 def window(first, count):
-    row = iota((512, 384), 0)
+    row = iota((512, 1), 0)
     c = row & 31
-    hit = (iota((512, 384), 1) == (row >> 5) * NCOL + c + first) & (c < count)
-    return jnp.where(hit, 1.0, 0.0).astype(BF)
-
-
-def pack_kernel(place_ref, *refs):
-    out_ref, sems = refs[4], refs[9]
+    column = jnp.where(c < count, (row >> 5) * NCOL + c + first, -1)
+    return jnp.where(iota((512, 384), 1) == column, 1.0, 0.0).astype(BF)
+
+
+def half_up(tile):
+    return pltpu.roll(tile, 4, tile.ndim - 2)
+
+
+def fold(field):
+    low = iota((16, 8, 128), 1) < 4
+    rest = jnp.where(low, field[:, 24:32, 0:128], half_up(field[:, 24:32, 128:256]))
+    return [field[:, 0:24, 0:128], field[:, 0:24, 128:256], rest]
+
+
+def unfold(chunk):
+    rest = chunk[48:56]
+    return [
+        jnp.concatenate([chunk[0:24], rest], axis=0).astype(BF),
+        jnp.concatenate([chunk[24:48], half_up(rest)], axis=0).astype(BF),
+    ]
+
+
+def copy_rows(buffer, out, first, last, sem):
+    rows = pl.ds(first, last - first)
+    copy = pltpu.make_async_copy(buffer.at[:, rows, :], out.at[:, rows, :], sem)
+    copy.start()
+    return copy
+
+
+def pack_kernel(core_ref, y_ref, *refs):
+    out_hbm, buffer, sems, out_sems = refs[4], refs[9], refs[10], refs[11]
     copies = [pltpu.make_async_copy(refs[k], refs[5 + k], sems.at[k]) for k in range(4)]
     for copy in copies:
         copy.start()
-    x_ref, cot_ref, bias_ref, ker_ref = refs[5:9]
-    core = place_ref[0]
-    src = iota((256, 256), 0)
-    dst = iota((256, 256), 1)
+    ker_ref, bias_ref, x_ref, cot_ref = refs[5:9]
+    core = core_ref[0]
+    dst = iota((256, 256), 0)
+    src = iota((256, 256), 1)
     ch, h = src >> 4, src & 15
     to_h_ch = jnp.where(dst == h * 16 + ch, 1.0, 0.0).astype(BF)
     other = (ch >> 3) ^ core
     to_half = jnp.where(dst == other * 128 + h * 8 + (ch & 7), 1.0, 0.0).astype(BF)
+    x_window = window(-2, 28)
+    cot_window = window(-1, 26)
 
     copies[0].wait()
-    x = dot(window(-2, 28), x_ref[...].reshape(256, 384), NT).astype(BF)
-    x = dot(x, to_h_ch).astype(BF).reshape(16, 32, 256)
-    out_ref[:, 0:32, :] = x[:, :, 0:128]
-    out_ref[:, 32:64, :] = x[:, :, 128:256]
-
-    copies[2].wait()
+    parts = []
+    for t in range(9):
+        both = ker_ref[t].astype(F32)
+        mine = jnp.where(core == 0, both[0:8], both[8:16])
+        parts.append(jnp.where(y_ref[0] == 0, mine[:, 0:128], mine[:, 128:256]))
+    parts.append(jnp.zeros((8, 128), F32))
+    weights = jnp.concatenate(parts, axis=0).astype(BF)
+    for j in range(16):
+        buffer[j, 112:192, :] = weights
+    sent = [copy_rows(buffer, out_hbm, 112, 192, out_sems.at[0])]
+
+    copies[1].wait()
     bias = jnp.broadcast_to(bias_ref[...], (8, 16))
     hi = bias.astype(BF).astype(F32)
     mid = (bias - hi).astype(BF).astype(F32)
     low = bias - hi - mid
     k = iota((8, 16), 0)
-    pieces = jnp.where(k == 4, hi, jnp.where(k == 5, mid, jnp.where(k == 6, low, 0.0)))
+    pieces = jnp.where(k == 2, hi, jnp.where(k == 3, mid, jnp.where(k == 6, low, 0.0)))
     spread = iota((16, 128), 0) == (core * 8 + (iota((16, 128), 1) & 7))
     pieces = dot(pieces.astype(BF), jnp.where(spread, 1.0, 0.0).astype(BF))
-    rows = jnp.concatenate([jnp.zeros((24, 128), F32), pieces], axis=0)
-
-    copies[1].wait()
-    c = dot(window(-1, 26), cot_ref[...].reshape(256, 384), NT).astype(BF)
-    c = dot(c, to_half).reshape(16, 32, 256)
-    out_ref[:, 64:96, :] = (c[:, :, 0:128] + rows[None]).astype(BF)
-    out_ref[:, 96:128, :] = c[:, :, 128:256].astype(BF)
+
+    copies[2].wait()
+    x = dot(to_h_ch, x_ref[...].reshape(256, 384)).astype(BF)
+    x = fold(dot(x_window, x, NT).reshape(16, 32, 256))
+    buffer[:, 0:48, :] = jnp.concatenate(x[:2], axis=1).astype(BF)
+    sent.append(copy_rows(buffer, out_hbm, 0, 48, out_sems.at[1]))
 
     copies[3].wait()
-    parts = []
-    for t in range(9):
-        both = ker_ref[t].astype(F32)
-        mine = jnp.where(core == 0, both[0:8], both[8:16])
-        parts.append(jnp.where(place_ref[1] == 0, mine[:, 0:128], mine[:, 128:256]))
-    parts.append(jnp.zeros((8, 128), F32))
-    weights = jnp.concatenate(parts, axis=0).astype(BF)
-    for j in range(16):
-        out_ref[j, 128:208, :] = weights
+    c = dot(to_half, cot_ref[...].reshape(256, 384)).astype(BF)
+    c = fold(dot(cot_window, c, NT).reshape(16, 32, 256))
+    c[2] = c[2] + pieces[None]
+    buffer[:, 48:112, :] = jnp.concatenate([x[2]] + c, axis=1).astype(BF)
+    sent.append(copy_rows(buffer, out_hbm, 48, 112, out_sems.at[2]))
+    for copy in sent:
+        copy.wait()
 
 
 SOURCES = [z * 2 + xh for xh in range(2) for z in range(8)]
 
 
-def unpack_kernel(core_ref, r_ref, xo_ref, co_ref, ha_ref, hb_ref, w_ref):
+def unpack_kernel(core_ref, r_ref, xo_ref, co_ref, ha_ref, hb_ref):
     core = core_ref[0]
     edge = []
+    chunks = [r_ref[s, 0:112, :].astype(F32) for s in range(16)]
+    fields = [unfold(chunk[0:56]) for chunk in chunks]
     for hh in range(2):
         halves = []
         for sh in range(2):
-            got = [r_ref[sh * 8 + s, hh * 32 : hh * 32 + 32, :] for s in range(8)]
-            halves.append(swap_blocks(got, 16))
+            halves.append(swap_blocks([fields[sh * 8 + s][hh] for s in range(8)], 16))
         for hl in range(8):
             at = (hh * 8 + hl) * 32
             row = jnp.concatenate([halves[0][hl], halves[1][hl]], axis=1)
             xo_ref[at : at + 32, :] = row
             if (hh * 8 + hl) in (0, 1, 14, 15):
                 edge.append(row)
-    own = swap_blocks([r_ref[s, 64:96, :] for s in SOURCES], 8)
-    oth = swap_blocks([r_ref[s, 96:128, :] for s in SOURCES], 8)
+    cots = [unfold(chunks[s][56:112]) for s in SOURCES]
+    own = swap_blocks([cot[0] for cot in cots], 8)
+    oth = swap_blocks([cot[1] for cot in cots], 8)
     for h in range(16):
         co_ref[h * 32 : h * 32 + 32, :] = own[h]
         at = 512 + (h % 8) * 32
@@ -147,34 +183,45 @@
         ref[32:64, :] = jnp.where(first, edge[1], edge[3])
         ref[64:96, 0:128] = jnp.where(first, cot[0], cot[15])
         ref[64:96, 128:256] = blank
-    chunks = [r_ref[s, 128:208, :].astype(F32) for s in SOURCES]
-    for t in range(9):
-        tap = jnp.concatenate([chunk[t * 8 : t * 8 + 8] for chunk in chunks], axis=0)
-        w_ref[t * 128 : t * 128 + 128, :] = tap.astype(BF)
-
-
-def grad_kernel(scale, place_ref, xo_ref, xr_ref, co_ref, ha_ref, hb_ref, wo_ref, wr_ref, *refs):
-    kg_ref, g_ref, w_ref, x, cot, y, gs = refs
-    core = place_ref[0]
-    low = place_ref[1] == 0
-    w_ref[:, 0:128] = jnp.where(low, wo_ref[...], wr_ref[...])
-    w_ref[:, 128:256] = jnp.where(low, wr_ref[...], wo_ref[...])
+    for k in range(16):
+        at = 96 + (k % 8) * 80
+        hb_ref[at : at + 80, (k // 8) * 128 : (k // 8) * 128 + 128] = r_ref[SOURCES[k], 112:192, :]
+
+
+def weight_kernel(y_ref, own_ref, got_ref, w_ref):
+    low = y_ref[0] == 0
+    own = own_ref[96:736, :].astype(F32).reshape(8, 80, 256)
+    got = got_ref[96:736, :].astype(F32).reshape(8, 80, 256)
+    for ih, field in enumerate((jnp.where(low, own, got), jnp.where(low, got, own))):
+        for t in range(9):
+            for k in range(2):
+                tap = field[:, t * 8 : t * 8 + 8, k * 128 : k * 128 + 128].reshape(64, 128)
+                at = t * 128 + k * 64
+                w_ref[at : at + 64, ih * 128 : ih * 128 + 128] = tap.astype(BF)
+
+
+def grad_kernel(scale, core_ref, edge_ref, xo_ref, xr_ref, co_ref, ha_ref, hb_ref, w_ref, *refs):
+    kg_hbm, g_ref, x, cot, y, gs, buffer, sems = refs
+    core = core_ref[0]
     first = core == 0
     mine = pl.multiple_of(core * 512, 512)
     theirs = pl.multiple_of((1 - core) * 512, 512)
-    x[0:64, :] = jnp.where(first, ha_ref[0:64, :], hb_ref[0:64, :])
+    keep = edge_ref[0] == 0
+    hb_x = jnp.where(keep, hb_ref[0:64, :], jnp.zeros((64, 256), BF))
+    hb_c = jnp.where(keep, hb_ref[64:96, 0:128], jnp.zeros((32, 128), BF))
+    x[0:64, :] = jnp.where(first, ha_ref[0:64, :], hb_x)
     x[pl.ds(64 + mine, 512), :] = xo_ref[0:512, :]
     x[pl.ds(64 + theirs, 512), :] = xr_ref[0:512, :]
-    x[1088:1152, :] = jnp.where(first, hb_ref[0:64, :], ha_ref[0:64, :])
+    x[1088:1152, :] = jnp.where(first, hb_x, ha_ref[0:64, :])
     x[1152:1216, :] = jnp.zeros((64, 256), BF)
-    cot[0:32, :] = jnp.where(first, ha_ref[64:96, 0:128], hb_ref[64:96, 0:128])
+    cot[0:32, :] = jnp.where(first, ha_ref[64:96, 0:128], hb_c)
     cot[pl.ds(32 + mine, 512), :] = co_ref[...]
     cot[pl.ds(32 + theirs, 256), :] = xr_ref[512:768, 0:128]
     cot[pl.ds(32 + theirs + 256, 256), :] = xr_ref[512:768, 128:256]
-    cot[1056:1088, :] = jnp.where(first, hb_ref[64:96, 0:128], ha_ref[64:96, 0:128])
+    cot[1056:1088, :] = jnp.where(first, hb_c, ha_ref[64:96, 0:128])
 
     bias = co_ref[16:32, :].astype(F32)
-    bias = bias[12:13] + bias[13:14] + bias[14:15]
+    bias = bias[10:11] + bias[11:12] + bias[14:15]
 
     for m in range(0, PX, 384):
         y[m : m + 384, :] = (
@@ -202,17 +249,21 @@
     g_ref[1088:PX, :] = jnp.zeros((PX - 1088, 128), BF)
     gs[16 + 1088 : 16 + PX, :] = jnp.zeros((PX - 1088, 128), F32)
 
-    taps = []
     shifted = jnp.concatenate(
         [gs[16 - b : 16 - b + PX, :].astype(BF) for b in range(3)], axis=1
     )
+    sent = []
     for a in range(3):
         block = dot(shifted, x[32 * a : 32 * a + PX, :], TN) * scale
-        taps += [block[0:128], block[128:256], block[256:384]]
-    for k in range(16):
-        o = slice(8 * k, 8 * k + 8)
-        rows = [tap[o, lane : lane + 128] for tap in taps for lane in (0, 128)]
-        kg_ref[SOURCES[k]] = jnp.concatenate(rows, axis=0).astype(BF)
+        for k in range(16):
+            rows = []
+            for b in range(3):
+                tap = block[128 * b + 8 * k : 128 * b + 8 * k + 8]
+                rows += [tap[:, 0:128], tap[:, 128:256]]
+            buffer[SOURCES[k], 48 * a : 48 * a + 48, :] = jnp.concatenate(rows, axis=0).astype(BF)
+        sent.append(copy_rows(buffer, kg_hbm, 48 * a, 48 * a + 48, sems.at[a]))
+    for copy in sent:
+        copy.wait()
 
 
 def input_kernel(core_ref, g_ref, w_ref, own_ref, send_ref, z, total):
@@ -289,85 +340,98 @@
 
 
 def shards(inputs, cotangent, kernel, channel_bias):
-    core, y = (lax.axis_index(n).astype(jnp.int32) for n in ("core", "y"))
-    place = jnp.stack([core, y & 1])
+    core, y, xl = (
+        lax.axis_index(n).astype(jnp.int32).reshape(1) for n in ("core", "y", "xl")
+    )
+    edge = jnp.where(4 * xl + y == 7 * (1 - core), 1, 0).astype(jnp.int32)
+    y = y & 1
     (packed,) = call(
         pack_kernel,
-        [((16, 208, 128), BF)],
-        place,
+        [((16, 192, 128), BF)],
+        core,
+        y,
+        kernel.reshape(16, 9, 256).transpose(1, 0, 2),
+        channel_bias.reshape(1, 16),
         inputs,
         cotangent,
-        channel_bias.reshape(1, 16),
-        kernel.reshape(16, 9, 256).transpose(1, 0, 2),
-        hbm=(1, 2, 3, 4),
+        smem=2,
+        hbm=(2, 3, 4, 5),
+        copied=(0,),
         mib=56,
         scratch=[
+            pltpu.VMEM((9, 16, 256), BF),
+            pltpu.VMEM((1, 16), F32),
             pltpu.VMEM((16, 16, 384), BF),
             pltpu.VMEM((16, 16, 384), BF),
-            pltpu.VMEM((1, 16), F32),
-            pltpu.VMEM((9, 16, 256), BF),
+            pltpu.VMEM((16, 192, 128), BF),
             pltpu.SemaphoreType.DMA((4,)),
+            pltpu.SemaphoreType.DMA((3,)),
         ],
     )
     got = lax.all_to_all(packed, CHAN, 0, 0)
-    xo, co, ha, hb, w_here = call(
+    xo, co, ha, hb = call(
         unpack_kernel,
-        [((768, 256), BF), ((512, 128), BF), ((96, 256), BF), ((96, 256), BF), ((1152, 128), BF)],
-        core.reshape(1),
+        [((768, 256), BF), ((512, 128), BF), ((96, 256), BF), ((736, 256), BF)],
+        core,
         got,
     )
-    w_there = lax.ppermute(w_here, "y", [(i, i ^ 1) for i in range(4)])
     across = [(b, b + 1) for b in range(1, 15, 2)]
     across += [(b + 1, b) for b in range(1, 15, 2)]
-    along = [(b, b + 2) for b in range(1, 14, 2)] + [(b, b - 2) for b in range(2, 16, 2)]
+    along = [(b, (b + 2) % 16) for b in range(1, 16, 2)]
+    along += [(b, (b - 2) % 16) for b in range(0, 16, 2)]
     xr = lax.ppermute(xo, "core", [(0, 1), (1, 0)])
     ha = lax.ppermute(ha, BAND, across)
-    hb = lax.ppermute(hb, BAND, along)
+    hr = lax.ppermute(hb, BAND, along)
+    (w,) = call(weight_kernel, [((1152, 256), BF)], y, hb, hr)
     scale = 1.0 / math.sqrt(256 * 384)
 
     def grads(*refs):
         grad_kernel(scale, *refs)
 
-    kg, g, w = call(
+    kg, g = call(
         grads,
-        [((16, 144, 128), BF), ((PX, 128), BF), ((1152, 256), BF)],
-        place,
+        [((16, 144, 128), BF), ((PX, 128), BF)],
+        core,
+        edge,
         xo,
         xr,
         co,
         ha,
-        hb,
-        w_here,
-        w_there,
+        hr,
+        w,
+        smem=2,
         scratch=[
             pltpu.VMEM((1216, 256), BF),
             pltpu.VMEM((1088, 128), BF),
             pltpu.VMEM((PX, 384), F32),
             pltpu.VMEM((PX + 16, 128), F32),
+            pltpu.VMEM((16, 144, 128), BF),
+            pltpu.SemaphoreType.DMA((3,)),
         ],
+        copied=(0,),
     )
     kg = lax.all_to_all(kg, CHAN, 0, 0)
     own, send = call(
         input_kernel,
         [((512, 256), F32), ((512, 256), BF)],
-        core.reshape(1),
+        core,
         g,
         w,
         scratch=[pltpu.VMEM((3, 1056, 256), F32), pltpu.VMEM((1024, 256), F32)],
     )
     recv = lax.ppermute(send, "core", [(0, 1), (1, 0)])
-    (back,) = call(repack_kernel, [((16, 48, 128), BF)], own, recv, smem=False)
+    (back,) = call(repack_kernel, [((16, 48, 128), BF)], own, recv, smem=0)
     back = lax.all_to_all(back, CHAN, 0, 0)
-    (input_grad,) = call(restore_kernel, [((16, 16, 384), BF)], back, smem=False)
+    (input_grad,) = call(restore_kernel, [((16, 16, 384), BF)], back, smem=0)
 
     part = ((144, 128), BF)
-    (sums,) = call(sum_kernel, [part], kg, smem=False)
+    (sums,) = call(sum_kernel, [part], kg, smem=0)
     ring = [lax.ppermute(sums, "y", [(i, (i + k) % 4) for i in range(4)]) for k in (3, 1, 2)]
-    (sums,) = call(ring_kernel, [part], sums, *ring, smem=False)
+    (sums,) = call(ring_kernel, [part], sums, *ring, smem=0)
     (ordered,) = call(
         order_kernel,
         [((9, 16, 256), F32)],
-        core.reshape(1),
+        core,
         sums,
         lax.ppermute(sums, "xl", [(0, 1), (1, 0)]),
         lax.ppermute(sums, "core", [(0, 1), (1, 0)]),

time: 101 us -> 96.6 us (0.956); the launches traced: 99.1 us -> 95.9 us
  starting transfers between devices: 29.8 us -> 22.7 us
  waiting for transfers between devices: 18.8 us -> 25.9 us
  Pallas kernels: 12.9 us -> 11.5 us
  blocking collectives: 36.3 us -> 35.1 us
    ppermute x2 -> x1, waiting for transfers between devices: 0.01 us -> 4.92 us  [shards(): hr = lax.ppermute(hb, BAND, along)]
    ppermute x2 -> x1, starting transfers between devices: 5.35 us -> 1.3 us  [shards(): hr = lax.ppermute(hb, BAND, along)]
    all_to_all x1, waiting for transfers between devices: 13.2 us -> 15.4 us  [shards(): kg = lax.all_to_all(kg, CHAN, 0, 0)]
    ppermute x1, waiting for transfers between devices: 1.59 us -> 0.01 us  [shards(): ha = lax.ppermute(ha, BAND, across)]
    ppermute x1, starting transfers between devices: 0.01 us -> 1.48 us  [shards(): lax.ppermute(sums, 'core', [(0, 1), (1, 0)])]
    pallas_call x9 -> x10, Pallas kernels: 12.9 us -> 11.5 us  [call(): pl.pallas_call(body, out_shape=[jax.ShapeDtypeStruct(s, d) for s, d in ou...]
    ppermute x3, starting transfers between devices: 5.67 us -> 4.38 us  [shards(): lax.ppermute(sums, 'y', [(i, (i + k) % 4) for i in range(4)])]
    all_to_all x1, blocking collectives: 36.3 us -> 35.1 us  [shards(): got = lax.all_to_all(packed, CHAN, 0, 0)]
  transfers between devices with their start and end apart: 13 -> 12, of which waited for: 5 -> 6; matrix products, arithmetic and copies ran while one was open for 0% -> 0% of each run, Pallas kernels for 4% -> 4%
where the time goes in v3:
time: 96.6 us; the launch traced here: 95.9 us
  blocking collectives  35.1 us (36%)
  waiting for transfers between devices  25.9 us (27%)
  starting transfers between devices  22.7 us (23%)
  Pallas kernels  11.5 us (12%)
    all_to_all x1, blocking collectives, shards(): got = lax.all_to_all(packed, CHAN, 0, 0)  35.1 us
    all_to_all x1, waiting for transfers between devices, shards(): kg = lax.all_to_all(kg, CHAN, 0, 0)  15.4 us
    pallas_call x10, Pallas kernels, call(): pl.pallas_call(body, out_shape=[jax.ShapeDtypeStruct(s, d) for s, d in ou...  11.5 us
    ppermute x1, waiting for transfers between devices, shards(): hr = lax.ppermute(hb, BAND, along)  4.92 us
    ppermute x3, starting transfers between devices, shards(): lax.ppermute(sums, 'y', [(i, (i + k) % 4) for i in range(4)])  4.38 us
    all_to_all x1, starting transfers between devices, shards(): back = lax.all_to_all(back, CHAN, 0, 0)  3.75 us
    all_to_all x1, starting transfers between devices, shards(): kg = lax.all_to_all(kg, CHAN, 0, 0)  3.59 us
    ppermute x3, waiting for transfers between devices, shards(): lax.ppermute(sums, 'y', [(i, (i + k) % 4) for i in range(4)])  2.93 us
  transfers between devices with their start and end apart: 12, of which 6 were waited for; matrix products, arithmetic and copies ran while one was open for 0% of the time, Pallas kernels for 4%

profile of v3, /device:TPU:1, one launch (start us, length us, event | category | flops | bytes accessed | tf_op | source)
XLA Modules:
  0.0 95.9 jit_solution(12136691356046564964)
XLA Ops:
  0.6 3.0 %shard_map.59 = bf16[16,192,128]{2,1,0:T(8,128)(2,1)} custom-call(s32[1]{0:T(128)} %bitcast.core_ref.refs_0_, s32[1]{0:T(128)} %bitcast.2.y_ref, bf16[9,16,256]{2,1,0:T(8,128)(2,1)} %bitcast.11, f32[1,16]{1,0:T(1,128)} %bitcast.12, bf16[16,16,384]{2,1,0:T(8,128)(2,1)} %refs_2_.1, bf16[16,16,384]{2,1,0:T(8,128)(2,1)} %refs_3_.1), custom_call_target="tpu_custom_call" | custom-call | tf_op jit(solution)/shard_map/pallas_call | solution.py:37
  3.6 35.1 %all_to_all.15.r_ref = bf16[16,192,128]{2,1,0:T(8,128)(2,1)S(1)} all-to-all(bf16[16,192,128]{2,1,0:T(8,128)(2,1)} %shard_map.59), channel_id=1, replica_groups=mesh['xl'=2,'y'=4,'core'=2,'z'=8,'xh'=2] {'z','xh'}, dimensions={0} | all-to-all | bytes 1572864 | tf_op jit(solution)/shard_map/all_to_all | solution.py:371
  38.7 1.0 %shard_map.60 = (bf16[768,256]{1,0:T(8,128)(2,1)S(1)}, bf16[512,128]{1,0:T(8,128)(2,1)S(1)}, bf16[96,256]{1,0:T(8,128)(2,1)S(1)}, bf16[736,256]{1,0:T(8,128)(2,1)S(1)}) custom-call(s32[1]{0:T(128)} %bitcast.core_ref.refs_0_, bf16[16,192,128]{2,1,0:T(8,128)(2,1)S(1)} %all_to_all.15.r_ref), custom_call_target="tpu_custom_call" | custom-call | tf_op jit(solution)/shard_map/pallas_call | solution.py:37
  39.7 2.4 %collective-permute-start = (bf16[768,256]{1,0:T(8,128)(2,1)S(1)}, bf16[768,256]{1,0:T(8,128)(2,1)S(1)}, u32[]{:S(2)}, u32[]{:S(2)}) collective-permute-start(bf16[768,256]{1,0:T(8,128)(2,1)S(1)} %get-tuple-element.10.refs_2_), channel_id=1, source_target_pairs={{0,16},{16,0},{1,17},{17,1},{2,18},{18,2},{3,19},{19,3},{4,20},{20... | collective-permute-start | bytes 1179656 | tf_op jit(solution)/shard_map/ppermute | solution.py:382
  42.2 1.3 %collective-permute-start.2 = (bf16[736,256]{1,0:T(8,128)(2,1)S(1)}, bf16[736,256]{1,0:T(8,128)(2,1)S(1)}, u32[]{:S(2)}, u32[]{:S(2)}) collective-permute-start(bf16[736,256]{1,0:T(8,128)(2,1)S(1)} %get-tuple-element.13.own_ref), channel_id=1, source_target_pairs={{16,48},{48,80},{80,112},{112,144},{144,176},{176,208},{208,240},{... | collective-permute-start | bytes 1130504 | tf_op jit(solution)/shard_map/ppermute | solution.py:384
  43.5 2.3 %collective-permute-start.1 = (bf16[96,256]{1,0:T(8,128)(2,1)S(1)}, bf16[96,256]{1,0:T(8,128)(2,1)S(1)}, u32[]{:S(2)}, u32[]{:S(2)}) collective-permute-start(bf16[96,256]{1,0:T(8,128)(2,1)S(1)} %get-tuple-element.12), channel_id=1, source_target_pairs={{16,32},{48,64},{80,96},{112,128},{144,160},{176,192},{208,224},{3... | collective-permute-start | bytes 147464 | tf_op jit(solution)/shard_map/ppermute | solution.py:383
  45.8 4.9 %collective-permute-done.2.got_ref.refs_6_ = bf16[736,256]{1,0:T(8,128)(2,1)S(1)} collective-permute-done((bf16[736,256]{1,0:T(8,128)(2,1)S(1)}, bf16[736,256]{1,0:T(8,128)(2,1)S(1)}, u32[]{:S(2)}, u32[]{:S(2)}) %collective-permute-start.2) | collective-permute-done | bytes 376864 | tf_op jit(solution)/shard_map/ppermute | solution.py:384
  50.7 0.2 shard_map.61.refs_7_.w_ref
  50.9 0.0 collective-permute-done.1.refs_5_
  50.9 0.0 collective-permute-done.refs_3_
  50.9 3.1 %shard_map.62 = (bf16[16,144,128]{2,1,0:T(8,128)(2,1)}, bf16[1152,128]{1,0:T(8,128)(2,1)S(1)}) custom-call(s32[1]{0:T(128)} %bitcast.core_ref.refs_0_, s32[1]{0:T(128)S(6)} %select_n.4.refs_1_, bf16[768,256]{1,0:T(8,128)(2,1)S(1)} %get-tuple-element.10.refs_2_, bf16[768,256]{1,0:T(8,128)(2,1)S(1)} %collective-permute-done.refs_3_, ...), custom_call_target="tpu_custom_call" | custom-call | tf_op jit(solution)/shard_map/pallas_call | solution.py:37
  54.0 3.6 %all-to-all-start.2 = ((bf16[16,144,128]{2,1,0:T(8,128)(2,1)}), bf16[16,144,128]{2,1,0:T(8,128)(2,1)S(1)}, u32[]{:S(2)}, u32[]{:S(2)}) async-start(bf16[16,144,128]{2,1,0:T(8,128)(2,1)} %get-tuple-element.17), calls=%async_computation.2 | async-start | bytes 1179648 | tf_op jit(solution)/shard_map/all_to_all | solution.py:413
  57.6 1.5 %shard_map.63 = (f32[512,256]{1,0:T(8,128)S(1)}, bf16[512,256]{1,0:T(8,128)(2,1)S(1)}) custom-call(s32[1]{0:T(128)} %bitcast.core_ref.refs_0_, bf16[1152,128]{1,0:T(8,128)(2,1)S(1)} %get-tuple-element.14.g_ref, bf16[1152,256]{1,0:T(8,128)(2,1)S(1)} %shard_map.61.refs_7_.w_ref), custom_call_target="tpu_custom_call" | custom-call | tf_op jit(solution)/shard_map/pallas_call | solution.py:37
  59.1 0.1 collective-permute-start.3
  59.2 1.5 %collective-permute-done.3.recv_ref = bf16[512,256]{1,0:T(8,128)(2,1)S(1)} collective-permute-done((bf16[512,256]{1,0:T(8,128)(2,1)S(1)}, bf16[512,256]{1,0:T(8,128)(2,1)S(1)}, u32[]{:S(2)}, u32[]{:S(2)}) %collective-permute-start.3) | collective-permute-done | bytes 262176 | tf_op jit(solution)/shard_map/ppermute | solution.py:422
  60.7 1.0 %shard_map.64 = bf16[16,48,128]{2,1,0:T(8,128)(2,1)} custom-call(f32[512,256]{1,0:T(8,128)S(1)} %get-tuple-element.15.own_ref, bf16[512,256]{1,0:T(8,128)(2,1)S(1)} %collective-permute-done.3.recv_ref), custom_call_target="tpu_custom_call" | custom-call | tf_op jit(solution)/shard_map/pallas_call | solution.py:37
  61.7 15.4 %all-to-all-done.2.r_ref = bf16[16,144,128]{2,1,0:T(8,128)(2,1)S(1)} async-done(((bf16[16,144,128]{2,1,0:T(8,128)(2,1)}), bf16[16,144,128]{2,1,0:T(8,128)(2,1)S(1)}, u32[]{:S(2)}, u32[]{:S(2)}) %all-to-all-start.2) | async-done | bytes 589856 | tf_op jit(solution)/shard_map/all_to_all | solution.py:413
  77.2 3.7 %all-to-all-start.1 = ((bf16[16,48,128]{2,1,0:T(8,128)(2,1)}), bf16[16,48,128]{2,1,0:T(8,128)(2,1)S(1)}, u32[]{:S(2)}, u32[]{:S(2)}) async-start(bf16[16,48,128]{2,1,0:T(8,128)(2,1)} %shard_map.64), calls=%async_computation.1 | async-start | bytes 393216 | tf_op jit(solution)/shard_map/all_to_all | solution.py:424
  80.9 0.1 shard_map.66.own_ref
  81.0 1.7 %collective-permute-start.6 = (bf16[144,128]{1,0:T(8,128)(2,1)S(1)}, bf16[144,128]{1,0:T(8,128)(2,1)S(1)}, u32[]{:S(2)}, u32[]{:S(2)}) collective-permute-start(bf16[144,128]{1,0:T(8,128)(2,1)S(1)} %shard_map.66.own_ref), channel_id=1, source_target_pairs={{0,64},{32,96},{64,0},{96,32},{1,65},{33,97},{65,1},{97,33},{2,66}... | collective-permute-start | bytes 110600 | tf_op jit(solution)/shard_map/ppermute | solution.py:429
  82.7 2.5 %collective-permute-start.5 = (bf16[144,128]{1,0:T(8,128)(2,1)S(1)}, bf16[144,128]{1,0:T(8,128)(2,1)S(1)}, u32[]{:S(2)}, u32[]{:S(2)}) collective-permute-start(bf16[144,128]{1,0:T(8,128)(2,1)S(1)} %shard_map.66.own_ref), channel_id=1, source_target_pairs={{0,32},{32,64},{64,96},{96,0},{1,33},{33,65},{65,97},{97,1},{2,34}... | collective-permute-start | bytes 110600 | tf_op jit(solution)/shard_map/ppermute | solution.py:429
  85.2 0.2 collective-permute-start.4
  85.4 0.0 collective-permute-done.6.far_ref
  85.4 1.6 %collective-permute-done.5.prev_ref = bf16[144,128]{1,0:T(8,128)(2,1)S(1)} collective-permute-done((bf16[144,128]{1,0:T(8,128)(2,1)S(1)}, bf16[144,128]{1,0:T(8,128)(2,1)S(1)}, u32[]{:S(2)}, u32[]{:S(2)}) %collective-permute-start.5) | collective-permute-done | bytes 36896 | tf_op jit(solution)/shard_map/ppermute | solution.py:429
  87.0 1.3 %collective-permute-done.4.next_ref = bf16[144,128]{1,0:T(8,128)(2,1)S(1)} collective-permute-done((bf16[144,128]{1,0:T(8,128)(2,1)S(1)}, bf16[144,128]{1,0:T(8,128)(2,1)S(1)}, u32[]{:S(2)}, u32[]{:S(2)}) %collective-permute-start.4) | collective-permute-done | bytes 36896 | tf_op jit(solution)/shard_map/ppermute | solution.py:429
  88.3 2.1 %collective-permute-start.9 = (bf16[144,128]{1,0:T(8,128)(2,1)S(1)}, bf16[144,128]{1,0:T(8,128)(2,1)S(1)}, u32[]{:S(2)}, u32[]{:S(2)}) collective-permute-start(bf16[144,128]{1,0:T(8,128)(2,1)S(1)} %shard_map.67.own_ref), channel_id=1, source_target_pairs={{0,144},{16,128},{128,16},{144,0},{1,145},{17,129},{129,17},{145,1... | collective-permute-start | bytes 110600 | tf_op jit(solution)/shard_map/ppermute | solution.py:438
  90.4 1.5 %collective-permute-start.8 = (bf16[144,128]{1,0:T(8,128)(2,1)S(1)}, bf16[144,128]{1,0:T(8,128)(2,1)S(1)}, u32[]{:S(2)}, u32[]{:S(2)}) collective-permute-start(bf16[144,128]{1,0:T(8,128)(2,1)S(1)} %shard_map.67.own_ref), channel_id=1, source_target_pairs={{0,16},{16,0},{1,17},{17,1},{2,18},{18,2},{3,19},{19,3},{4,20},{20... | collective-permute-start | bytes 110600 | tf_op jit(solution)/shard_map/ppermute | solution.py:437
  91.9 1.3 %collective-permute-start.7 = (bf16[144,128]{1,0:T(8,128)(2,1)S(1)}, bf16[144,128]{1,0:T(8,128)(2,1)S(1)}, u32[]{:S(2)}, u32[]{:S(2)}) collective-permute-start(bf16[144,128]{1,0:T(8,128)(2,1)S(1)} %shard_map.67.own_ref), channel_id=1, source_target_pairs={{0,128},{128,0},{1,129},{129,1},{2,130},{130,2},{3,131},{131,3},{4... | collective-permute-start | bytes 110600 | tf_op jit(solution)/shard_map/ppermute | solution.py:436
  93.2 0.0 all-to-all-done.1.r_ref
  93.2 0.9 shard_map.65
  94.1 0.0 collective-permute-done.9.core_xl_ref
  94.1 0.0 collective-permute-done.8.core_own_ref
  94.1 1.1 %collective-permute-done.7.xl_ref = bf16[144,128]{1,0:T(8,128)(2,1)S(1)} collective-permute-done((bf16[144,128]{1,0:T(8,128)(2,1)S(1)}, bf16[144,128]{1,0:T(8,128)(2,1)S(1)}, u32[]{:S(2)}, u32[]{:S(2)}) %collective-permute-start.7) | collective-permute-done | bytes 36896 | tf_op jit(solution)/shard_map/ppermute | solution.py:436
  95.3 0.7 shard_map.68
  (1 shorter events, 0.0 us)
Async XLA Ops:
  39.7 11.2 %collective-permute-start = (bf16[768,256]{1,0:T(8,128)(2,1)S(1)}, bf16[768,256]{1,0:T(8,128)(2,1)S(1)}, u32[]{:S(2)}, u32[]{:S(2)}) collective-permute-start(bf16[768,256]{1,0:T(8,128)(2,1)S(1)} %get-tuple-element.10.refs_2_), channel_id=1, source_target_pairs={{0,16},{16,0},{1,17},{17,1},{2,18},{18,2},{3,19},{19,3},{4,20},{20... | collective-permute-start | bytes 1179656 | tf_op jit(solution)/shard_map/ppermute | solution.py:382
  42.2 8.6 %collective-permute-start.2 = (bf16[736,256]{1,0:T(8,128)(2,1)S(1)}, bf16[736,256]{1,0:T(8,128)(2,1)S(1)}, u32[]{:S(2)}, u32[]{:S(2)}) collective-permute-start(bf16[736,256]{1,0:T(8,128)(2,1)S(1)} %get-tuple-element.13.own_ref), channel_id=1, source_target_pairs={{16,48},{48,80},{80,112},{112,144},{144,176},{176,208},{208,240},{... | collective-permute-start | bytes 1130504 | tf_op jit(solution)/shard_map/ppermute | solution.py:384
  43.5 7.4 %collective-permute-start.1 = (bf16[96,256]{1,0:T(8,128)(2,1)S(1)}, bf16[96,256]{1,0:T(8,128)(2,1)S(1)}, u32[]{:S(2)}, u32[]{:S(2)}) collective-permute-start(bf16[96,256]{1,0:T(8,128)(2,1)S(1)} %get-tuple-element.12), channel_id=1, source_target_pairs={{16,32},{48,64},{80,96},{112,128},{144,160},{176,192},{208,224},{3... | collective-permute-start | bytes 147464 | tf_op jit(solution)/shard_map/ppermute | solution.py:383
  54.0 23.2 %all-to-all-start.2 = ((bf16[16,144,128]{2,1,0:T(8,128)(2,1)}), bf16[16,144,128]{2,1,0:T(8,128)(2,1)S(1)}, u32[]{:S(2)}, u32[]{:S(2)}) async-start(bf16[16,144,128]{2,1,0:T(8,128)(2,1)} %get-tuple-element.17), calls=%async_computation.2 | async-start | bytes 1179648 | tf_op jit(solution)/shard_map/all_to_all | solution.py:413
  59.1 1.6 %collective-permute-start.3 = (bf16[512,256]{1,0:T(8,128)(2,1)S(1)}, bf16[512,256]{1,0:T(8,128)(2,1)S(1)}, u32[]{:S(2)}, u32[]{:S(2)}) collective-permute-start(bf16[512,256]{1,0:T(8,128)(2,1)S(1)} %get-tuple-element.16), channel_id=1, source_target_pairs={{0,16},{16,0},{1,17},{17,1},{2,18},{18,2},{3,19},{19,3},{4,20},{20... | collective-permute-start | bytes 786440 | tf_op jit(solution)/shard_map/ppermute | solution.py:422
  77.2 16.0 %all-to-all-start.1 = ((bf16[16,48,128]{2,1,0:T(8,128)(2,1)}), bf16[16,48,128]{2,1,0:T(8,128)(2,1)S(1)}, u32[]{:S(2)}, u32[]{:S(2)}) async-start(bf16[16,48,128]{2,1,0:T(8,128)(2,1)} %shard_map.64), calls=%async_computation.1 | async-start | bytes 393216 | tf_op jit(solution)/shard_map/all_to_all | solution.py:424
  81.0 4.4 %collective-permute-start.6 = (bf16[144,128]{1,0:T(8,128)(2,1)S(1)}, bf16[144,128]{1,0:T(8,128)(2,1)S(1)}, u32[]{:S(2)}, u32[]{:S(2)}) collective-permute-start(bf16[144,128]{1,0:T(8,128)(2,1)S(1)} %shard_map.66.own_ref), channel_id=1, source_target_pairs={{0,64},{32,96},{64,0},{96,32},{1,65},{33,97},{65,1},{97,33},{2,66}... | collective-permute-start | bytes 110600 | tf_op jit(solution)/shard_map/ppermute | solution.py:429
  82.7 4.3 %collective-permute-start.5 = (bf16[144,128]{1,0:T(8,128)(2,1)S(1)}, bf16[144,128]{1,0:T(8,128)(2,1)S(1)}, u32[]{:S(2)}, u32[]{:S(2)}) collective-permute-start(bf16[144,128]{1,0:T(8,128)(2,1)S(1)} %shard_map.66.own_ref), channel_id=1, source_target_pairs={{0,32},{32,64},{64,96},{96,0},{1,33},{33,65},{65,97},{97,1},{2,34}... | collective-permute-start | bytes 110600 | tf_op jit(solution)/shard_map/ppermute | solution.py:429
  85.2 3.1 %collective-permute-start.4 = (bf16[144,128]{1,0:T(8,128)(2,1)S(1)}, bf16[144,128]{1,0:T(8,128)(2,1)S(1)}, u32[]{:S(2)}, u32[]{:S(2)}) collective-permute-start(bf16[144,128]{1,0:T(8,128)(2,1)S(1)} %shard_map.66.own_ref), channel_id=1, source_target_pairs={{0,96},{32,0},{64,32},{96,64},{1,97},{33,1},{65,33},{97,65},{2,98}... | collective-permute-start | bytes 110600 | tf_op jit(solution)/shard_map/ppermute | solution.py:429
  88.3 5.8 %collective-permute-start.9 = (bf16[144,128]{1,0:T(8,128)(2,1)S(1)}, bf16[144,128]{1,0:T(8,128)(2,1)S(1)}, u32[]{:S(2)}, u32[]{:S(2)}) collective-permute-start(bf16[144,128]{1,0:T(8,128)(2,1)S(1)} %shard_map.67.own_ref), channel_id=1, source_target_pairs={{0,144},{16,128},{128,16},{144,0},{1,145},{17,129},{129,17},{145,1... | collective-permute-start | bytes 110600 | tf_op jit(solution)/shard_map/ppermute | solution.py:438
  90.4 3.7 %collective-permute-start.8 = (bf16[144,128]{1,0:T(8,128)(2,1)S(1)}, bf16[144,128]{1,0:T(8,128)(2,1)S(1)}, u32[]{:S(2)}, u32[]{:S(2)}) collective-permute-start(bf16[144,128]{1,0:T(8,128)(2,1)S(1)} %shard_map.67.own_ref), channel_id=1, source_target_pairs={{0,16},{16,0},{1,17},{17,1},{2,18},{18,2},{3,19},{19,3},{4,20},{20... | collective-permute-start | bytes 110600 | tf_op jit(solution)/shard_map/ppermute | solution.py:437
  91.9 3.3 %collective-permute-start.7 = (bf16[144,128]{1,0:T(8,128)(2,1)S(1)}, bf16[144,128]{1,0:T(8,128)(2,1)S(1)}, u32[]{:S(2)}, u32[]{:S(2)}) collective-permute-start(bf16[144,128]{1,0:T(8,128)(2,1)S(1)} %shard_map.67.own_ref), channel_id=1, source_target_pairs={{0,128},{128,0},{1,129},{129,1},{2,130},{130,2},{3,131},{131,3},{4... | collective-permute-start | bytes 110600 | tf_op jit(solution)/shard_map/ppermute | solution.py:436

commit v4 on v3

--- a/solution.py
+++ b/solution.py
@@ -97,7 +97,7 @@
     return copy
 
 
-def pack_kernel(core_ref, y_ref, *refs):
+def pack_kernel(core_ref, *refs):
     out_hbm, buffer, sems, out_sems = refs[4], refs[9], refs[10], refs[11]
     copies = [pltpu.make_async_copy(refs[k], refs[5 + k], sems.at[k]) for k in range(4)]
     for copy in copies:
@@ -114,16 +114,15 @@
     cot_window = window(-1, 26)
 
     copies[0].wait()
-    parts = []
+    taps = []
     for t in range(9):
         both = ker_ref[t].astype(F32)
-        mine = jnp.where(core == 0, both[0:8], both[8:16])
-        parts.append(jnp.where(y_ref[0] == 0, mine[:, 0:128], mine[:, 128:256]))
-    parts.append(jnp.zeros((8, 128), F32))
-    weights = jnp.concatenate(parts, axis=0).astype(BF)
+        taps.append(jnp.where(core == 0, both[0:8], both[8:16]))
+    taps = jnp.concatenate(taps, axis=0).astype(BF)
     for j in range(16):
-        buffer[j, 112:192, :] = weights
-    sent = [copy_rows(buffer, out_hbm, 112, 192, out_sems.at[0])]
+        lane = (j // 2 % 2) * 128
+        buffer[j, 112:184, :] = taps[:, lane : lane + 128]
+    sent = [copy_rows(buffer, out_hbm, 112, 184, out_sems.at[0])]
 
     copies[1].wait()
     bias = jnp.broadcast_to(bias_ref[...], (8, 16))
@@ -136,12 +135,12 @@
     pieces = dot(pieces.astype(BF), jnp.where(spread, 1.0, 0.0).astype(BF))
 
     copies[2].wait()
+    copies[3].wait()
     x = dot(to_h_ch, x_ref[...].reshape(256, 384)).astype(BF)
     x = fold(dot(x_window, x, NT).reshape(16, 32, 256))
     buffer[:, 0:48, :] = jnp.concatenate(x[:2], axis=1).astype(BF)
     sent.append(copy_rows(buffer, out_hbm, 0, 48, out_sems.at[1]))
 
-    copies[3].wait()
     c = dot(to_half, cot_ref[...].reshape(256, 384)).astype(BF)
     c = fold(dot(cot_window, c, NT).reshape(16, 32, 256))
     c[2] = c[2] + pieces[None]
@@ -154,7 +153,7 @@
 SOURCES = [z * 2 + xh for xh in range(2) for z in range(8)]
 
 
-def unpack_kernel(core_ref, r_ref, xo_ref, co_ref, ha_ref, hb_ref):
+def unpack_kernel(core_ref, r_ref, xo_ref, co_ref, ha_ref, w_ref):
     core = core_ref[0]
     edge = []
     chunks = [r_ref[s, 0:112, :].astype(F32) for s in range(16)]
@@ -177,48 +176,40 @@
         at = 512 + (h % 8) * 32
         xo_ref[at : at + 32, (h // 8) * 128 : (h // 8) * 128 + 128] = oth[h]
     first = core == 0
-    blank = jnp.zeros((32, 128), BF)
-    for ref, cot in ((ha_ref, oth), (hb_ref, own)):
-        ref[0:32, :] = jnp.where(first, edge[0], edge[2])
-        ref[32:64, :] = jnp.where(first, edge[1], edge[3])
-        ref[64:96, 0:128] = jnp.where(first, cot[0], cot[15])
-        ref[64:96, 128:256] = blank
+    ha_ref[0:32, :] = jnp.where(first, edge[0], edge[2])
+    ha_ref[32:64, :] = jnp.where(first, edge[1], edge[3])
+    ha_ref[64:96, 0:128] = jnp.where(first, oth[0], oth[15])
+    ha_ref[64:96, 128:256] = jnp.where(first, own[0], own[15])
     for k in range(16):
-        at = 96 + (k % 8) * 80
-        hb_ref[at : at + 80, (k // 8) * 128 : (k // 8) * 128 + 128] = r_ref[SOURCES[k], 112:192, :]
-
-
-def weight_kernel(y_ref, own_ref, got_ref, w_ref):
-    low = y_ref[0] == 0
-    own = own_ref[96:736, :].astype(F32).reshape(8, 80, 256)
-    got = got_ref[96:736, :].astype(F32).reshape(8, 80, 256)
+        w_ref[k] = r_ref[SOURCES[k], 112:184, :]
+
+
+def weight_kernel(half_ref, own_ref, got_ref, w_ref):
+    low = half_ref[0] == 0
+    own = own_ref[...].astype(F32)
+    got = got_ref[...].astype(F32)
     for ih, field in enumerate((jnp.where(low, own, got), jnp.where(low, got, own))):
         for t in range(9):
-            for k in range(2):
-                tap = field[:, t * 8 : t * 8 + 8, k * 128 : k * 128 + 128].reshape(64, 128)
-                at = t * 128 + k * 64
-                w_ref[at : at + 64, ih * 128 : ih * 128 + 128] = tap.astype(BF)
-
-
-def grad_kernel(scale, core_ref, edge_ref, xo_ref, xr_ref, co_ref, ha_ref, hb_ref, w_ref, *refs):
+            tap = field[:, t * 8 : t * 8 + 8].reshape(128, 128)
+            w_ref[t * 128 : t * 128 + 128, ih * 128 : ih * 128 + 128] = tap.astype(BF)
+
+
+def grad_kernel(scale, core_ref, xo_ref, xr_ref, co_ref, ha_ref, hb_ref, w_ref, *refs):
     kg_hbm, g_ref, x, cot, y, gs, buffer, sems = refs
     core = core_ref[0]
     first = core == 0
     mine = pl.multiple_of(core * 512, 512)
     theirs = pl.multiple_of((1 - core) * 512, 512)
-    keep = edge_ref[0] == 0
-    hb_x = jnp.where(keep, hb_ref[0:64, :], jnp.zeros((64, 256), BF))
-    hb_c = jnp.where(keep, hb_ref[64:96, 0:128], jnp.zeros((32, 128), BF))
-    x[0:64, :] = jnp.where(first, ha_ref[0:64, :], hb_x)
+    x[0:64, :] = jnp.where(first, ha_ref[0:64, :], hb_ref[0:64, :])
     x[pl.ds(64 + mine, 512), :] = xo_ref[0:512, :]
     x[pl.ds(64 + theirs, 512), :] = xr_ref[0:512, :]
-    x[1088:1152, :] = jnp.where(first, hb_x, ha_ref[0:64, :])
+    x[1088:1152, :] = jnp.where(first, hb_ref[0:64, :], ha_ref[0:64, :])
     x[1152:1216, :] = jnp.zeros((64, 256), BF)
-    cot[0:32, :] = jnp.where(first, ha_ref[64:96, 0:128], hb_c)
+    cot[0:32, :] = jnp.where(first, ha_ref[64:96, 0:128], hb_ref[64:96, 128:256])
     cot[pl.ds(32 + mine, 512), :] = co_ref[...]
     cot[pl.ds(32 + theirs, 256), :] = xr_ref[512:768, 0:128]
     cot[pl.ds(32 + theirs + 256, 256), :] = xr_ref[512:768, 128:256]
-    cot[1056:1088, :] = jnp.where(first, hb_c, ha_ref[64:96, 0:128])
+    cot[1056:1088, :] = jnp.where(first, hb_ref[64:96, 128:256], ha_ref[64:96, 0:128])
 
     bias = co_ref[16:32, :].astype(F32)
     bias = bias[10:11] + bias[11:12] + bias[14:15]
@@ -283,7 +274,7 @@
     send_ref[...] = total[pl.ds(pl.multiple_of((1 - core) * 512, 512), 512), :].astype(BF)
 
 
-def repack_kernel(own_ref, recv_ref, out_ref):
+def repack_kernel(xh_ref, own_ref, recv_ref, keep_ref, send_ref, chunks):
     parts = []
     for hh in range(2):
         rows = []
@@ -293,15 +284,23 @@
             rows.append(row[0:NCOL])
         parts.append([swap_blocks([r[:, q : q + 128] for r in rows], 16) for q in (0, 128)])
     for d in range(16):
-        out_ref[d] = jnp.concatenate(
+        chunks[d // 2, d % 2] = jnp.concatenate(
             [parts[0][d // 8][d % 8], parts[1][d // 8][d % 8]], axis=0
         ).astype(BF)
+    keep_ref[...] = chunks[:, pl.ds(xh_ref[0], 1)].reshape(8, 48, 128)
+    send_ref[...] = chunks[:, pl.ds(1 - xh_ref[0], 1)].reshape(8, 48, 128)
+
+
+def join_kernel(xh_ref, keep_ref, recv_ref, out_ref):
+    first = xh_ref[0] == 0
+    out_ref[:, 0:48, :] = jnp.where(first, keep_ref[...], recv_ref[...])
+    out_ref[:, 48:96, :] = jnp.where(first, recv_ref[...], keep_ref[...])
 
 
 def restore_kernel(r_ref, out_ref):
     halves = [[], []]
     for j in range(16):
-        chunk = r_ref[j].astype(F32)
+        chunk = r_ref[j // 2, (j % 2) * 48 : (j % 2) * 48 + 48, :].astype(F32)
         halves[0].append(chunk[0:NCOL])
         halves[1].append(chunk[NCOL : 2 * NCOL])
     field = jnp.concatenate(
@@ -313,7 +312,7 @@
     out_ref[...] = out.astype(BF).reshape(16, 16, 384)
 
 
-def sum_kernel(r_ref, out_ref):
+def sum_kernel(r_ref, after_ref, out_ref):
     total = r_ref[0].astype(F32)
     for s in range(1, 16):
         total = total + r_ref[s].astype(F32)
@@ -340,22 +339,19 @@
 
 
 def shards(inputs, cotangent, kernel, channel_bias):
-    core, y, xl = (
-        lax.axis_index(n).astype(jnp.int32).reshape(1) for n in ("core", "y", "xl")
-    )
-    edge = jnp.where(4 * xl + y == 7 * (1 - core), 1, 0).astype(jnp.int32)
-    y = y & 1
+    core, z, xh = (
+        lax.axis_index(n).astype(jnp.int32).reshape(1) for n in ("core", "z", "xh")
+    )
+    half = z & 1
     (packed,) = call(
         pack_kernel,
-        [((16, 192, 128), BF)],
+        [((16, 184, 128), BF)],
         core,
-        y,
         kernel.reshape(16, 9, 256).transpose(1, 0, 2),
         channel_bias.reshape(1, 16),
         inputs,
         cotangent,
-        smem=2,
-        hbm=(2, 3, 4, 5),
+        hbm=(1, 2, 3, 4),
         copied=(0,),
         mib=56,
         scratch=[
@@ -363,26 +359,26 @@
             pltpu.VMEM((1, 16), F32),
             pltpu.VMEM((16, 16, 384), BF),
             pltpu.VMEM((16, 16, 384), BF),
-            pltpu.VMEM((16, 192, 128), BF),
+            pltpu.VMEM((16, 184, 128), BF),
             pltpu.SemaphoreType.DMA((4,)),
             pltpu.SemaphoreType.DMA((3,)),
         ],
     )
     got = lax.all_to_all(packed, CHAN, 0, 0)
-    xo, co, ha, hb = call(
+    xo, co, ha, w_half = call(
         unpack_kernel,
-        [((768, 256), BF), ((512, 128), BF), ((96, 256), BF), ((736, 256), BF)],
+        [((768, 256), BF), ((512, 128), BF), ((96, 256), BF), ((16, 72, 128), BF)],
         core,
         got,
     )
     across = [(b, b + 1) for b in range(1, 15, 2)]
     across += [(b + 1, b) for b in range(1, 15, 2)]
-    along = [(b, (b + 2) % 16) for b in range(1, 16, 2)]
-    along += [(b, (b - 2) % 16) for b in range(0, 16, 2)]
     xr = lax.ppermute(xo, "core", [(0, 1), (1, 0)])
     ha = lax.ppermute(ha, BAND, across)
-    hr = lax.ppermute(hb, BAND, along)
-    (w,) = call(weight_kernel, [((1152, 256), BF)], y, hb, hr)
+    hb = lax.ppermute(ha, "core", [(0, 1), (1, 0)])
+    ring = [(i, (i + 7) % 8) for i in range(8)] + [(8 + i, 8 + (i + 1) % 8) for i in range(8)]
+    w_rest = lax.ppermute(w_half, ("core", "z"), ring)
+    (w,) = call(weight_kernel, [((1152, 256), BF)], half, w_half, w_rest)
     scale = 1.0 / math.sqrt(256 * 384)
 
     def grads(*refs):
@@ -392,14 +388,12 @@
         grads,
         [((16, 144, 128), BF), ((PX, 128), BF)],
         core,
-        edge,
         xo,
         xr,
         co,
         ha,
-        hr,
+        hb,
         w,
-        smem=2,
         scratch=[
             pltpu.VMEM((1216, 256), BF),
             pltpu.VMEM((1088, 128), BF),
@@ -420,12 +414,22 @@
         scratch=[pltpu.VMEM((3, 1056, 256), F32), pltpu.VMEM((1024, 256), F32)],
     )
     recv = lax.ppermute(send, "core", [(0, 1), (1, 0)])
-    (back,) = call(repack_kernel, [((16, 48, 128), BF)], own, recv, smem=0)
-    back = lax.all_to_all(back, CHAN, 0, 0)
+    block = ((8, 48, 128), BF)
+    keep, send = call(
+        repack_kernel,
+        [block, block],
+        xh,
+        own,
+        recv,
+        scratch=[pltpu.VMEM((8, 2, 48, 128), BF)],
+    )
+    recv = lax.ppermute(send, "xh", [(0, 1), (1, 0)])
+    (joined,) = call(join_kernel, [((8, 96, 128), BF)], xh, keep, recv)
+    back = lax.all_to_all(joined, "z", 0, 0)
     (input_grad,) = call(restore_kernel, [((16, 16, 384), BF)], back, smem=0)
 
     part = ((144, 128), BF)
-    (sums,) = call(sum_kernel, [part], kg, smem=0)
+    (sums,) = call(sum_kernel, [part], kg, joined, smem=0, hbm=(1,))
     ring = [lax.ppermute(sums, "y", [(i, (i + k) % 4) for i in range(4)]) for k in (3, 1, 2)]
     (sums,) = call(ring_kernel, [part], sums, *ring, smem=0)
     (ordered,) = call(

time: 96.6 us -> 94.7 us (0.980)
  waiting for transfers between devices: 25.9 us -> 19.5 us
  starting transfers between devices: 22.7 us -> 28.8 us
    all_to_all x1, waiting for transfers between devices: 15.4 us -> 8.28 us  [shards(): kg = lax.all_to_all(kg, CHAN, 0, 0)]
    ppermute x1, waiting for transfers between devices: 0.01 us -> 2.22 us  [shards(): ha = lax.ppermute(ha, BAND, across)]
    ppermute x1 -> x3, starting transfers between devices: 1.3 us -> 3.24 us  [the longest x1 3.24 us: shards(): recv = lax.ppermute(send, 'xh', [(0, 1), (1, 0)])]
    ppermute x3, starting transfers between devices: 4.38 us -> 5.88 us  [shards(): lax.ppermute(sums, 'y', [(i, (i + k) % 4) for i in range(4)])]
    ppermute x1, starting transfers between devices: 2.32 us -> 3.46 us  [shards(): ha = lax.ppermute(ha, BAND, across)]
    ppermute x1 -> x3, waiting for transfers between devices: 4.92 us -> 4.22 us  [the longest x1 3.14 us: shards(): recv = lax.ppermute(send, 'xh', [(0, 1), (1, 0)])]
    pallas_call x10 -> x11, Pallas kernels: 11.5 us -> 11.1 us  [call(): pl.pallas_call(body, out_shape=[jax.ShapeDtypeStruct(s, d) for s, d in ou...]
  transfers between devices with their start and end apart: 12 -> 14, of which waited for: 6 -> 8; matrix products, arithmetic and copies ran while one was open for 0% -> 0% of each run, Pallas kernels for 4% -> 4%
where the time goes in v4:
time: 94.7 us; the launch traced here: 94.3 us
  blocking collectives  34.2 us (36%)
  starting transfers between devices  28.8 us (30%)
  waiting for transfers between devices  19.5 us (21%)
  Pallas kernels  11.1 us (12%)
    all_to_all x1, blocking collectives, shards(): got = lax.all_to_all(packed, CHAN, 0, 0)  34.2 us
    pallas_call x11, Pallas kernels, call(): pl.pallas_call(body, out_shape=[jax.ShapeDtypeStruct(s, d) for s, d in ou...  11.1 us
    all_to_all x1, waiting for transfers between devices, shards(): kg = lax.all_to_all(kg, CHAN, 0, 0)  8.28 us
    ppermute x3, starting transfers between devices, shards(): lax.ppermute(sums, 'y', [(i, (i + k) % 4) for i in range(4)])  5.88 us
    all_to_all x1, starting transfers between devices, shards(): back = lax.all_to_all(joined, 'z', 0, 0)  4.29 us
    all_to_all x1, starting transfers between devices, shards(): kg = lax.all_to_all(kg, CHAN, 0, 0)  4 us
    ppermute x1, starting transfers between devices, shards(): ha = lax.ppermute(ha, BAND, across)  3.46 us
    ppermute x1, starting transfers between devices, shards(): recv = lax.ppermute(send, 'xh', [(0, 1), (1, 0)])  3.24 us
  transfers between devices with their start and end apart: 14, of which 8 were waited for; matrix products, arithmetic and copies ran while one was open for 0% of the time, Pallas kernels for 4%

profile of v4, /device:TPU:1, one launch (start us, length us, event | category | flops | bytes accessed | tf_op | source)
XLA Modules:
  0.0 94.3 jit_solution(9871314489032267073)
XLA Ops:
  0.6 2.5 %shard_map.59 = bf16[16,184,128]{2,1,0:T(8,128)(2,1)} custom-call(s32[1]{0:T(128)} %bitcast.1.core_ref.refs_0_, bf16[9,16,256]{2,1,0:T(8,128)(2,1)} %bitcast.11, f32[1,16]{1,0:T(1,128)} %bitcast.12, bf16[16,16,384]{2,1,0:T(8,128)(2,1)} %refs_2_.1, bf16[16,16,384]{2,1,0:T(8,128)(2,1)} %refs_3_.1), custom_call_target="tpu_custom_call" | custom-call | tf_op jit(solution)/shard_map/pallas_call | solution.py:37
  3.2 34.2 %all_to_all.15.r_ref = bf16[16,184,128]{2,1,0:T(8,128)(2,1)S(1)} all-to-all(bf16[16,184,128]{2,1,0:T(8,128)(2,1)} %shard_map.59), channel_id=1, replica_groups=mesh['xl'=2,'y'=4,'core'=2,'z'=8,'xh'=2] {'z','xh'}, dimensions={0} | all-to-all | bytes 1507328 | tf_op jit(solution)/shard_map/all_to_all | solution.py:367
  37.4 1.0 %shard_map.60 = (bf16[768,256]{1,0:T(8,128)(2,1)S(1)}, bf16[512,128]{1,0:T(8,128)(2,1)S(1)}, bf16[96,256]{1,0:T(8,128)(2,1)S(1)}, bf16[16,72,128]{2,1,0:T(8,128)(2,1)S(1)}) custom-call(s32[1]{0:T(128)} %bitcast.1.core_ref.refs_0_, bf16[16,184,128]{2,1,0:T(8,128)(2,1)S(1)} %all_to_all.15.r_ref), custom_call_target="tpu_custom_call" | custom-call | tf_op jit(solution)/shard_map/pallas_call | solution.py:37
  38.4 2.7 %collective-permute-start = (bf16[768,256]{1,0:T(8,128)(2,1)S(1)}, bf16[768,256]{1,0:T(8,128)(2,1)S(1)}, u32[]{:S(2)}, u32[]{:S(2)}) collective-permute-start(bf16[768,256]{1,0:T(8,128)(2,1)S(1)} %get-tuple-element.12.refs_1_), channel_id=1, source_target_pairs={{0,16},{16,0},{1,17},{17,1},{2,18},{18,2},{3,19},{19,3},{4,20},{20... | collective-permute-start | bytes 1179656 | tf_op jit(solution)/shard_map/ppermute | solution.py:376
  41.1 0.0 collective-permute-start.3
  41.1 3.5 %collective-permute-start.1 = (bf16[96,256]{1,0:T(8,128)(2,1)S(1)}, bf16[96,256]{1,0:T(8,128)(2,1)S(1)}, u32[]{:S(2)}, u32[]{:S(2)}) collective-permute-start(bf16[96,256]{1,0:T(8,128)(2,1)S(1)} %get-tuple-element.14), channel_id=1, source_target_pairs={{16,32},{48,64},{80,96},{112,128},{144,160},{176,192},{208,224},{3... | collective-permute-start | bytes 147464 | tf_op jit(solution)/shard_map/ppermute | solution.py:377
  44.6 2.2 %collective-permute-done.1.refs_4_ = bf16[96,256]{1,0:T(8,128)(2,1)S(1)} collective-permute-done((bf16[96,256]{1,0:T(8,128)(2,1)S(1)}, bf16[96,256]{1,0:T(8,128)(2,1)S(1)}, u32[]{:S(2)}, u32[]{:S(2)}) %collective-permute-start.1) | collective-permute-done | bytes 49184 | tf_op jit(solution)/shard_map/ppermute | solution.py:377
  46.8 0.0 collective-permute-start.2
  46.8 1.1 %collective-permute-done.3.got_ref = bf16[16,72,128]{2,1,0:T(8,128)(2,1)S(1)} collective-permute-done((bf16[16,72,128]{2,1,0:T(8,128)(2,1)S(1)}, bf16[16,72,128]{2,1,0:T(8,128)(2,1)S(1)}, u32[]{:S(2)}, u32[]{:S(2)}) %collective-permute-start.3) | collective-permute-done | bytes 294944 | tf_op jit(solution)/shard_map/ppermute | solution.py:380
  47.9 0.2 shard_map.61.refs_6_.w_ref
  48.1 0.0 collective-permute-done.2.refs_5_
  48.1 0.0 collective-permute-done.refs_2_
  48.1 3.0 %shard_map.62 = (bf16[16,144,128]{2,1,0:T(8,128)(2,1)}, bf16[1152,128]{1,0:T(8,128)(2,1)S(1)}) custom-call(s32[1]{0:T(128)} %bitcast.1.core_ref.refs_0_, bf16[768,256]{1,0:T(8,128)(2,1)S(1)} %get-tuple-element.12.refs_1_, bf16[768,256]{1,0:T(8,128)(2,1)S(1)} %collective-permute-done.refs_2_, bf16[512,128]{1,0:T(8,128)(2,1)S(1)} %get-tuple-element.13.refs_3_, ...), custom_call_target="tpu_custom_call" | custom-call | tf_op jit(solution)/shard_map/pallas_call | solution.py:37
  51.1 4.0 %all-to-all-start.2 = ((bf16[16,144,128]{2,1,0:T(8,128)(2,1)}), bf16[16,144,128]{2,1,0:T(8,128)(2,1)S(1)}, u32[]{:S(2)}, u32[]{:S(2)}) async-start(bf16[16,144,128]{2,1,0:T(8,128)(2,1)} %get-tuple-element.21), calls=%async_computation.2 | async-start | bytes 1179648 | tf_op jit(solution)/shard_map/all_to_all | solution.py:407
  55.1 1.5 %shard_map.63 = (f32[512,256]{1,0:T(8,128)S(1)}, bf16[512,256]{1,0:T(8,128)(2,1)S(1)}) custom-call(s32[1]{0:T(128)} %bitcast.1.core_ref.refs_0_, bf16[1152,128]{1,0:T(8,128)(2,1)S(1)} %get-tuple-element.16.g_ref, bf16[1152,256]{1,0:T(8,128)(2,1)S(1)} %shard_map.61.refs_6_.w_ref), custom_call_target="tpu_custom_call" | custom-call | tf_op jit(solution)/shard_map/pallas_call | solution.py:37
  56.6 0.5 collective-permute-start.4
  57.2 1.2 %collective-permute-done.4.recv_ref = bf16[512,256]{1,0:T(8,128)(2,1)S(1)} collective-permute-done((bf16[512,256]{1,0:T(8,128)(2,1)S(1)}, bf16[512,256]{1,0:T(8,128)(2,1)S(1)}, u32[]{:S(2)}, u32[]{:S(2)}) %collective-permute-start.4) | collective-permute-done | bytes 262176 | tf_op jit(solution)/shard_map/ppermute | solution.py:416
  58.3 0.4 shard_map.64
  58.7 3.2 %collective-permute-start.5 = (bf16[8,48,128]{2,1,0:T(8,128)(2,1)S(1)}, bf16[8,48,128]{2,1,0:T(8,128)(2,1)S(1)}, u32[]{:S(2)}, u32[]{:S(2)}) collective-permute-start(bf16[8,48,128]{2,1,0:T(8,128)(2,1)S(1)} %get-tuple-element.20), channel_id=1, source_target_pairs={{0,1},{1,0},{2,3},{3,2},{4,5},{5,4},{6,7},{7,6},{8,9},{9,8},{10,11... | collective-permute-start | bytes 294920 | tf_op jit(solution)/shard_map/ppermute | solution.py:426
  61.9 3.1 %collective-permute-done.5.recv_ref = bf16[8,48,128]{2,1,0:T(8,128)(2,1)S(1)} collective-permute-done((bf16[8,48,128]{2,1,0:T(8,128)(2,1)S(1)}, bf16[8,48,128]{2,1,0:T(8,128)(2,1)S(1)}, u32[]{:S(2)}, u32[]{:S(2)}) %collective-permute-start.5) | collective-permute-done | bytes 98336 | tf_op jit(solution)/shard_map/ppermute | solution.py:426
  65.1 0.7 shard_map.65.after_ref
  65.8 8.3 %all-to-all-done.2.r_ref = bf16[16,144,128]{2,1,0:T(8,128)(2,1)S(1)} async-done(((bf16[16,144,128]{2,1,0:T(8,128)(2,1)}), bf16[16,144,128]{2,1,0:T(8,128)(2,1)S(1)}, u32[]{:S(2)}, u32[]{:S(2)}) %all-to-all-start.2) | async-done | bytes 589856 | tf_op jit(solution)/shard_map/all_to_all | solution.py:407
  74.1 4.3 %all-to-all-start.1 = ((bf16[8,96,128]{2,1,0:T(8,128)(2,1)}), bf16[8,96,128]{2,1,0:T(8,128)(2,1)S(1)}, u32[]{:S(2)}, u32[]{:S(2)}) async-start(bf16[8,96,128]{2,1,0:T(8,128)(2,1)} %shard_map.65.after_ref), calls=%async_computation.1 | async-start | bytes 393216 | tf_op jit(solution)/shard_map/all_to_all | solution.py:428
  78.4 0.1 shard_map.67.own_ref
  78.4 3.2 %collective-permute-start.8 = (bf16[144,128]{1,0:T(8,128)(2,1)S(1)}, bf16[144,128]{1,0:T(8,128)(2,1)S(1)}, u32[]{:S(2)}, u32[]{:S(2)}) collective-permute-start(bf16[144,128]{1,0:T(8,128)(2,1)S(1)} %shard_map.67.own_ref), channel_id=1, source_target_pairs={{0,64},{32,96},{64,0},{96,32},{1,65},{33,97},{65,1},{97,33},{2,66}... | collective-permute-start | bytes 110600 | tf_op jit(solution)/shard_map/ppermute | solution.py:433
  81.6 2.0 %collective-permute-start.7 = (bf16[144,128]{1,0:T(8,128)(2,1)S(1)}, bf16[144,128]{1,0:T(8,128)(2,1)S(1)}, u32[]{:S(2)}, u32[]{:S(2)}) collective-permute-start(bf16[144,128]{1,0:T(8,128)(2,1)S(1)} %shard_map.67.own_ref), channel_id=1, source_target_pairs={{0,32},{32,64},{64,96},{96,0},{1,33},{33,65},{65,97},{97,1},{2,34}... | collective-permute-start | bytes 110600 | tf_op jit(solution)/shard_map/ppermute | solution.py:433
  83.7 0.7 collective-permute-start.6
  84.3 0.0 collective-permute-done.8.far_ref
  84.3 1.6 %collective-permute-done.7.prev_ref = bf16[144,128]{1,0:T(8,128)(2,1)S(1)} collective-permute-done((bf16[144,128]{1,0:T(8,128)(2,1)S(1)}, bf16[144,128]{1,0:T(8,128)(2,1)S(1)}, u32[]{:S(2)}, u32[]{:S(2)}) %collective-permute-start.7) | collective-permute-done | bytes 36896 | tf_op jit(solution)/shard_map/ppermute | solution.py:433
  86.0 0.8 collective-permute-done.6.next_ref
  86.8 2.2 %collective-permute-start.11 = (bf16[144,128]{1,0:T(8,128)(2,1)S(1)}, bf16[144,128]{1,0:T(8,128)(2,1)S(1)}, u32[]{:S(2)}, u32[]{:S(2)}) collective-permute-start(bf16[144,128]{1,0:T(8,128)(2,1)S(1)} %shard_map.68.own_ref), channel_id=1, source_target_pairs={{0,144},{16,128},{128,16},{144,0},{1,145},{17,129},{129,17},{145,1... | collective-permute-start | bytes 110600 | tf_op jit(solution)/shard_map/ppermute | solution.py:442
  89.0 1.2 %collective-permute-start.10 = (bf16[144,128]{1,0:T(8,128)(2,1)S(1)}, bf16[144,128]{1,0:T(8,128)(2,1)S(1)}, u32[]{:S(2)}, u32[]{:S(2)}) collective-permute-start(bf16[144,128]{1,0:T(8,128)(2,1)S(1)} %shard_map.68.own_ref), channel_id=1, source_target_pairs={{0,16},{16,0},{1,17},{17,1},{2,18},{18,2},{3,19},{19,3},{4,20},{20... | collective-permute-start | bytes 110600 | tf_op jit(solution)/shard_map/ppermute | solution.py:441
  90.3 1.3 %collective-permute-start.9 = (bf16[144,128]{1,0:T(8,128)(2,1)S(1)}, bf16[144,128]{1,0:T(8,128)(2,1)S(1)}, u32[]{:S(2)}, u32[]{:S(2)}) collective-permute-start(bf16[144,128]{1,0:T(8,128)(2,1)S(1)} %shard_map.68.own_ref), channel_id=1, source_target_pairs={{0,128},{128,0},{1,129},{129,1},{2,130},{130,2},{3,131},{131,3},{4... | collective-permute-start | bytes 110600 | tf_op jit(solution)/shard_map/ppermute | solution.py:440
  91.5 0.0 all-to-all-done.1.r_ref
  91.5 0.9 shard_map.66
  92.5 0.0 collective-permute-done.11.core_xl_ref
  92.5 0.0 collective-permute-done.10.core_own_ref
  92.5 1.1 %collective-permute-done.9.xl_ref = bf16[144,128]{1,0:T(8,128)(2,1)S(1)} collective-permute-done((bf16[144,128]{1,0:T(8,128)(2,1)S(1)}, bf16[144,128]{1,0:T(8,128)(2,1)S(1)}, u32[]{:S(2)}, u32[]{:S(2)}) %collective-permute-start.9) | collective-permute-done | bytes 36896 | tf_op jit(solution)/shard_map/ppermute | solution.py:440
  93.6 0.7 shard_map.69
  (1 shorter events, 0.0 us)
Async XLA Ops:
  38.4 9.6 %collective-permute-start = (bf16[768,256]{1,0:T(8,128)(2,1)S(1)}, bf16[768,256]{1,0:T(8,128)(2,1)S(1)}, u32[]{:S(2)}, u32[]{:S(2)}) collective-permute-start(bf16[768,256]{1,0:T(8,128)(2,1)S(1)} %get-tuple-element.12.refs_1_), channel_id=1, source_target_pairs={{0,16},{16,0},{1,17},{17,1},{2,18},{18,2},{3,19},{19,3},{4,20},{20... | collective-permute-start | bytes 1179656 | tf_op jit(solution)/shard_map/ppermute | solution.py:376
  41.1 6.8 %collective-permute-start.3 = (bf16[16,72,128]{2,1,0:T(8,128)(2,1)S(1)}, bf16[16,72,128]{2,1,0:T(8,128)(2,1)S(1)}, u32[]{:S(2)}, u32[]{:S(2)}) collective-permute-start(bf16[16,72,128]{2,1,0:T(8,128)(2,1)S(1)} %get-tuple-element.15.own_ref), channel_id=1, source_target_pairs={{0,14},{2,0},{4,2},{6,4},{8,6},{10,8},{12,10},{14,12},{16,18},{18,... | collective-permute-start | bytes 884744 | tf_op jit(solution)/shard_map/ppermute | solution.py:380
  41.1 5.7 %collective-permute-start.1 = (bf16[96,256]{1,0:T(8,128)(2,1)S(1)}, bf16[96,256]{1,0:T(8,128)(2,1)S(1)}, u32[]{:S(2)}, u32[]{:S(2)}) collective-permute-start(bf16[96,256]{1,0:T(8,128)(2,1)S(1)} %get-tuple-element.14), channel_id=1, source_target_pairs={{16,32},{48,64},{80,96},{112,128},{144,160},{176,192},{208,224},{3... | collective-permute-start | bytes 147464 | tf_op jit(solution)/shard_map/ppermute | solution.py:377
  46.8 1.3 %collective-permute-start.2 = (bf16[96,256]{1,0:T(8,128)(2,1)S(1)}, bf16[96,256]{1,0:T(8,128)(2,1)S(1)}, u32[]{:S(2)}, u32[]{:S(2)}) collective-permute-start(bf16[96,256]{1,0:T(8,128)(2,1)S(1)} %collective-permute-done.1.refs_4_), channel_id=1, source_target_pairs={{0,16},{16,0},{1,17},{17,1},{2,18},{18,2},{3,19},{19,3},{4,20},{20... | collective-permute-start | bytes 147464 | tf_op jit(solution)/shard_map/ppermute | solution.py:378
  51.1 22.9 %all-to-all-start.2 = ((bf16[16,144,128]{2,1,0:T(8,128)(2,1)}), bf16[16,144,128]{2,1,0:T(8,128)(2,1)S(1)}, u32[]{:S(2)}, u32[]{:S(2)}) async-start(bf16[16,144,128]{2,1,0:T(8,128)(2,1)} %get-tuple-element.21), calls=%async_computation.2 | async-start | bytes 1179648 | tf_op jit(solution)/shard_map/all_to_all | solution.py:407
  56.6 1.7 %collective-permute-start.4 = (bf16[512,256]{1,0:T(8,128)(2,1)S(1)}, bf16[512,256]{1,0:T(8,128)(2,1)S(1)}, u32[]{:S(2)}, u32[]{:S(2)}) collective-permute-start(bf16[512,256]{1,0:T(8,128)(2,1)S(1)} %get-tuple-element.18), channel_id=1, source_target_pairs={{0,16},{16,0},{1,17},{17,1},{2,18},{18,2},{3,19},{19,3},{4,20},{20... | collective-permute-start | bytes 786440 | tf_op jit(solution)/shard_map/ppermute | solution.py:416
  58.7 6.4 %collective-permute-start.5 = (bf16[8,48,128]{2,1,0:T(8,128)(2,1)S(1)}, bf16[8,48,128]{2,1,0:T(8,128)(2,1)S(1)}, u32[]{:S(2)}, u32[]{:S(2)}) collective-permute-start(bf16[8,48,128]{2,1,0:T(8,128)(2,1)S(1)} %get-tuple-element.20), channel_id=1, source_target_pairs={{0,1},{1,0},{2,3},{3,2},{4,5},{5,4},{6,7},{7,6},{8,9},{9,8},{10,11... | collective-permute-start | bytes 294920 | tf_op jit(solution)/shard_map/ppermute | solution.py:426
  74.1 17.5 %all-to-all-start.1 = ((bf16[8,96,128]{2,1,0:T(8,128)(2,1)}), bf16[8,96,128]{2,1,0:T(8,128)(2,1)S(1)}, u32[]{:S(2)}, u32[]{:S(2)}) async-start(bf16[8,96,128]{2,1,0:T(8,128)(2,1)} %shard_map.65.after_ref), calls=%async_computation.1 | async-start | bytes 393216 | tf_op jit(solution)/shard_map/all_to_all | solution.py:428
  78.4 5.9 %collective-permute-start.8 = (bf16[144,128]{1,0:T(8,128)(2,1)S(1)}, bf16[144,128]{1,0:T(8,128)(2,1)S(1)}, u32[]{:S(2)}, u32[]{:S(2)}) collective-permute-start(bf16[144,128]{1,0:T(8,128)(2,1)S(1)} %shard_map.67.own_ref), channel_id=1, source_target_pairs={{0,64},{32,96},{64,0},{96,32},{1,65},{33,97},{65,1},{97,33},{2,66}... | collective-permute-start | bytes 110600 | tf_op jit(solution)/shard_map/ppermute | solution.py:433
  81.6 4.3 %collective-permute-start.7 = (bf16[144,128]{1,0:T(8,128)(2,1)S(1)}, bf16[144,128]{1,0:T(8,128)(2,1)S(1)}, u32[]{:S(2)}, u32[]{:S(2)}) collective-permute-start(bf16[144,128]{1,0:T(8,128)(2,1)S(1)} %shard_map.67.own_ref), channel_id=1, source_target_pairs={{0,32},{32,64},{64,96},{96,0},{1,33},{33,65},{65,97},{97,1},{2,34}... | collective-permute-start | bytes 110600 | tf_op jit(solution)/shard_map/ppermute | solution.py:433
  83.7 3.1 %collective-permute-start.6 = (bf16[144,128]{1,0:T(8,128)(2,1)S(1)}, bf16[144,128]{1,0:T(8,128)(2,1)S(1)}, u32[]{:S(2)}, u32[]{:S(2)}) collective-permute-start(bf16[144,128]{1,0:T(8,128)(2,1)S(1)} %shard_map.67.own_ref), channel_id=1, source_target_pairs={{0,96},{32,0},{64,32},{96,64},{1,97},{33,1},{65,33},{97,65},{2,98}... | collective-permute-start | bytes 110600 | tf_op jit(solution)/shard_map/ppermute | solution.py:433
  86.8 5.7 %collective-permute-start.11 = (bf16[144,128]{1,0:T(8,128)(2,1)S(1)}, bf16[144,128]{1,0:T(8,128)(2,1)S(1)}, u32[]{:S(2)}, u32[]{:S(2)}) collective-permute-start(bf16[144,128]{1,0:T(8,128)(2,1)S(1)} %shard_map.68.own_ref), channel_id=1, source_target_pairs={{0,144},{16,128},{128,16},{144,0},{1,145},{17,129},{129,17},{145,1... | collective-permute-start | bytes 110600 | tf_op jit(solution)/shard_map/ppermute | solution.py:442
  89.0 3.4 %collective-permute-start.10 = (bf16[144,128]{1,0:T(8,128)(2,1)S(1)}, bf16[144,128]{1,0:T(8,128)(2,1)S(1)}, u32[]{:S(2)}, u32[]{:S(2)}) collective-permute-start(bf16[144,128]{1,0:T(8,128)(2,1)S(1)} %shard_map.68.own_ref), channel_id=1, source_target_pairs={{0,16},{16,0},{1,17},{17,1},{2,18},{18,2},{3,19},{19,3},{4,20},{20... | collective-permute-start | bytes 110600 | tf_op jit(solution)/shard_map/ppermute | solution.py:441
  90.3 3.3 %collective-permute-start.9 = (bf16[144,128]{1,0:T(8,128)(2,1)S(1)}, bf16[144,128]{1,0:T(8,128)(2,1)S(1)}, u32[]{:S(2)}, u32[]{:S(2)}) collective-permute-start(bf16[144,128]{1,0:T(8,128)(2,1)S(1)} %shard_map.68.own_ref), channel_id=1, source_target_pairs={{0,128},{128,0},{1,129},{129,1},{2,130},{130,2},{3,131},{131,3},{4... | collective-permute-start | bytes 110600 | tf_op jit(solution)/shard_map/ppermute | solution.py:440

commit v5 on v4

--- a/solution.py
+++ b/solution.py
@@ -114,15 +114,20 @@
     cot_window = window(-1, 26)
 
     copies[0].wait()
-    taps = []
+    upper = iota((8, 256), 0) < 4
+    mine = []
     for t in range(9):
         both = ker_ref[t].astype(F32)
-        taps.append(jnp.where(core == 0, both[0:8], both[8:16]))
-    taps = jnp.concatenate(taps, axis=0).astype(BF)
+        mine.append(jnp.where(core == 0, both[0:8], both[8:16]))
+    halves = []
+    for r in range(2):
+        taps = [mine[t] if (t % 2 == r) else half_up(mine[t]) for t in range(9)] + [mine[8]]
+        pairs = [jnp.where(upper, taps[t], taps[t + 1]) for t in range(0, 10, 2)]
+        halves.append(jnp.concatenate(pairs, axis=0).astype(BF))
     for j in range(16):
         lane = (j // 2 % 2) * 128
-        buffer[j, 112:184, :] = taps[:, lane : lane + 128]
-    sent = [copy_rows(buffer, out_hbm, 112, 184, out_sems.at[0])]
+        buffer[j, 112:152, :] = halves[j // 4 % 2][:, lane : lane + 128]
+    sent = [copy_rows(buffer, out_hbm, 112, 152, out_sems.at[0])]
 
     copies[1].wait()
     bias = jnp.broadcast_to(bias_ref[...], (8, 16))
@@ -181,17 +186,24 @@
     ha_ref[64:96, 0:128] = jnp.where(first, oth[0], oth[15])
     ha_ref[64:96, 128:256] = jnp.where(first, own[0], own[15])
     for k in range(16):
-        w_ref[k] = r_ref[SOURCES[k], 112:184, :]
-
-
-def weight_kernel(half_ref, own_ref, got_ref, w_ref):
-    low = half_ref[0] == 0
-    own = own_ref[...].astype(F32)
-    got = got_ref[...].astype(F32)
-    for ih, field in enumerate((jnp.where(low, own, got), jnp.where(low, got, own))):
+        w_ref[k] = r_ref[SOURCES[k], 112:152, :]
+
+
+def weight_kernel(z_ref, own_ref, below_ref, above_ref, far_ref, w_ref, quarters):
+    for ref, offset in ((own_ref, 0), (below_ref, 3), (above_ref, 1), (far_ref, 2)):
+        quarters[(z_ref[0] + offset) & 3] = ref[...]
+    upper = iota((16, 8, 128), 1) < 4
+    for ih in range(2):
+        first, second = quarters[ih].astype(F32), quarters[2 + ih].astype(F32)
         for t in range(9):
-            tap = field[:, t * 8 : t * 8 + 8].reshape(128, 128)
-            w_ref[t * 128 : t * 128 + 128, ih * 128 : ih * 128 + 128] = tap.astype(BF)
+            rows = slice((t // 2) * 8, (t // 2) * 8 + 8)
+            if t % 2 == 0:
+                tap = jnp.where(upper, first[:, rows], half_up(second[:, rows]))
+            else:
+                tap = jnp.where(upper, half_up(first[:, rows]), second[:, rows])
+            w_ref[t * 128 : t * 128 + 128, ih * 128 : ih * 128 + 128] = tap.reshape(
+                128, 128
+            ).astype(BF)
 
 
 def grad_kernel(scale, core_ref, xo_ref, xr_ref, co_ref, ha_ref, hb_ref, w_ref, *refs):
@@ -342,10 +354,9 @@
     core, z, xh = (
         lax.axis_index(n).astype(jnp.int32).reshape(1) for n in ("core", "z", "xh")
     )
-    half = z & 1
     (packed,) = call(
         pack_kernel,
-        [((16, 184, 128), BF)],
+        [((16, 152, 128), BF)],
         core,
         kernel.reshape(16, 9, 256).transpose(1, 0, 2),
         channel_bias.reshape(1, 16),
@@ -359,15 +370,15 @@
             pltpu.VMEM((1, 16), F32),
             pltpu.VMEM((16, 16, 384), BF),
             pltpu.VMEM((16, 16, 384), BF),
-            pltpu.VMEM((16, 184, 128), BF),
+            pltpu.VMEM((16, 152, 128), BF),
             pltpu.SemaphoreType.DMA((4,)),
             pltpu.SemaphoreType.DMA((3,)),
         ],
     )
     got = lax.all_to_all(packed, CHAN, 0, 0)
-    xo, co, ha, w_half = call(
+    xo, co, ha, w_part = call(
         unpack_kernel,
-        [((768, 256), BF), ((512, 128), BF), ((96, 256), BF), ((16, 72, 128), BF)],
+        [((768, 256), BF), ((512, 128), BF), ((96, 256), BF), ((16, 40, 128), BF)],
         core,
         got,
     )
@@ -376,9 +387,17 @@
     xr = lax.ppermute(xo, "core", [(0, 1), (1, 0)])
     ha = lax.ppermute(ha, BAND, across)
     hb = lax.ppermute(ha, "core", [(0, 1), (1, 0)])
-    ring = [(i, (i + 7) % 8) for i in range(8)] + [(8 + i, 8 + (i + 1) % 8) for i in range(8)]
-    w_rest = lax.ppermute(w_half, ("core", "z"), ring)
-    (w,) = call(weight_kernel, [((1152, 256), BF)], half, w_half, w_rest)
+    far = [(i, (i + 2) % 8) for i in range(8)] + [(8 + i, 8 + (i + 6) % 8) for i in range(8)]
+    (w,) = call(
+        weight_kernel,
+        [((1152, 256), BF)],
+        z,
+        w_part,
+        lax.ppermute(w_part, "z", [(i, (i + 1) % 8) for i in range(8)]),
+        lax.ppermute(w_part, "z", [(i, (i + 7) % 8) for i in range(8)]),
+        lax.ppermute(w_part, ("core", "z"), far),
+        scratch=[pltpu.VMEM((4, 16, 40, 128), BF)],
+    )
     scale = 1.0 / math.sqrt(256 * 384)
 
     def grads(*refs):

time: 94.7 us -> 94.6 us (level)
  starting transfers between devices: 28.8 us -> 31.9 us
  blocking collectives: 34.2 us -> 32.4 us
  waiting for transfers between devices: 19.5 us -> 18.1 us
    all_to_all x1, waiting for transfers between devices: 8.28 us -> 6.24 us  [shards(): kg = lax.all_to_all(kg, CHAN, 0, 0)]
    ppermute x1 -> x3, starting transfers between devices: 0.01 us -> 1.9 us  [the longest x1 1.25 us: shards(): lax.ppermute(w_part, 'z', [(i, (i + 1) % 8) for i in range(8)])]
    all_to_all x1, blocking collectives: 34.2 us -> 32.4 us  [shards(): got = lax.all_to_all(packed, CHAN, 0, 0)]
    ppermute x1, starting transfers between devices: 0.52 us -> 1.8 us  [shards(): recv = lax.ppermute(send, 'core', [(0, 1), (1, 0)])]
  transfers between devices with their start and end apart: 14 -> 16, of which waited for: 8 -> 10; matrix products, arithmetic and copies ran while one was open for 0% -> 0% of each run, Pallas kernels for 4% -> 4%
where the time goes in v5:
time: 94.6 us; the launch traced here: 94.2 us
  blocking collectives  32.4 us (34%)
  starting transfers between devices  31.9 us (34%)
  waiting for transfers between devices  18.1 us (19%)
  Pallas kernels  11.2 us (12%)
    all_to_all x1, blocking collectives, shards(): got = lax.all_to_all(packed, CHAN, 0, 0)  32.4 us
    pallas_call x11, Pallas kernels, call(): pl.pallas_call(body, out_shape=[jax.ShapeDtypeStruct(s, d) for s, d in ou...  11.2 us
    all_to_all x1, waiting for transfers between devices, shards(): kg = lax.all_to_all(kg, CHAN, 0, 0)  6.24 us
    ppermute x3, starting transfers between devices, shards(): lax.ppermute(sums, 'y', [(i, (i + k) % 4) for i in range(4)])  5.69 us
    all_to_all x1, starting transfers between devices, shards(): back = lax.all_to_all(joined, 'z', 0, 0)  4.41 us
    ppermute x1, starting transfers between devices, shards(): ha = lax.ppermute(ha, BAND, across)  4.39 us
    all_to_all x1, starting transfers between devices, shards(): kg = lax.all_to_all(kg, CHAN, 0, 0)  3.82 us
    ppermute x1, waiting for transfers between devices, shards(): recv = lax.ppermute(send, 'xh', [(0, 1), (1, 0)])  3.38 us
  transfers between devices with their start and end apart: 16, of which 10 were waited for; matrix products, arithmetic and copies ran while one was open for 0% of the time, Pallas kernels for 4%

profile of v5, /device:TPU:1, one launch (start us, length us, event | category | flops | bytes accessed | tf_op | source)
XLA Modules:
  0.0 94.2 jit_solution(903516466181138236)
XLA Ops:
  0.6 2.5 %shard_map.59 = bf16[16,152,128]{2,1,0:T(8,128)(2,1)} custom-call(s32[1]{0:T(128)} %bitcast.1.core_ref.refs_0_, bf16[9,16,256]{2,1,0:T(8,128)(2,1)} %bitcast.11, f32[1,16]{1,0:T(1,128)} %bitcast.12, bf16[16,16,384]{2,1,0:T(8,128)(2,1)} %refs_2_.1, bf16[16,16,384]{2,1,0:T(8,128)(2,1)} %refs_3_.1), custom_call_target="tpu_custom_call" | custom-call | tf_op jit(solution)/shard_map/pallas_call | solution.py:37
  3.2 32.4 %all_to_all.15.r_ref = bf16[16,152,128]{2,1,0:T(8,128)(2,1)S(1)} all-to-all(bf16[16,152,128]{2,1,0:T(8,128)(2,1)} %shard_map.59), channel_id=1, replica_groups=mesh['xl'=2,'y'=4,'core'=2,'z'=8,'xh'=2] {'z','xh'}, dimensions={0} | all-to-all | bytes 1245184 | tf_op jit(solution)/shard_map/all_to_all | solution.py:378
  35.6 1.0 %shard_map.60 = (bf16[768,256]{1,0:T(8,128)(2,1)S(1)}, bf16[512,128]{1,0:T(8,128)(2,1)S(1)}, bf16[96,256]{1,0:T(8,128)(2,1)S(1)}, bf16[16,40,128]{2,1,0:T(8,128)(2,1)S(1)}) custom-call(s32[1]{0:T(128)} %bitcast.1.core_ref.refs_0_, bf16[16,152,128]{2,1,0:T(8,128)(2,1)S(1)} %all_to_all.15.r_ref), custom_call_target="tpu_custom_call" | custom-call | tf_op jit(solution)/shard_map/pallas_call | solution.py:37
  36.6 2.0 %collective-permute-start = (bf16[768,256]{1,0:T(8,128)(2,1)S(1)}, bf16[768,256]{1,0:T(8,128)(2,1)S(1)}, u32[]{:S(2)}, u32[]{:S(2)}) collective-permute-start(bf16[768,256]{1,0:T(8,128)(2,1)S(1)} %get-tuple-element.12.refs_1_), channel_id=1, source_target_pairs={{0,16},{16,0},{1,17},{17,1},{2,18},{18,2},{3,19},{19,3},{4,20},{20... | collective-permute-start | bytes 1179656 | tf_op jit(solution)/shard_map/ppermute | solution.py:387
  38.6 0.4 collective-permute-start.5
  39.0 0.2 collective-permute-start.4
  39.2 1.3 %collective-permute-start.3 = (bf16[16,40,128]{2,1,0:T(8,128)(2,1)S(1)}, bf16[16,40,128]{2,1,0:T(8,128)(2,1)S(1)}, u32[]{:S(2)}, u32[]{:S(2)}) collective-permute-start(bf16[16,40,128]{2,1,0:T(8,128)(2,1)S(1)} %get-tuple-element.15.own_ref), channel_id=1, source_target_pairs={{0,2},{2,4},{4,6},{6,8},{8,10},{10,12},{12,14},{14,0},{1,3},{3,5},... | collective-permute-start | bytes 491528 | tf_op jit(solution)/shard_map/ppermute | solution.py:396
  40.5 4.4 %collective-permute-start.1 = (bf16[96,256]{1,0:T(8,128)(2,1)S(1)}, bf16[96,256]{1,0:T(8,128)(2,1)S(1)}, u32[]{:S(2)}, u32[]{:S(2)}) collective-permute-start(bf16[96,256]{1,0:T(8,128)(2,1)S(1)} %get-tuple-element.14), channel_id=1, source_target_pairs={{16,32},{48,64},{80,96},{112,128},{144,160},{176,192},{208,224},{3... | collective-permute-start | bytes 147464 | tf_op jit(solution)/shard_map/ppermute | solution.py:388
  44.9 2.1 %collective-permute-done.1.refs_4_ = bf16[96,256]{1,0:T(8,128)(2,1)S(1)} collective-permute-done((bf16[96,256]{1,0:T(8,128)(2,1)S(1)}, bf16[96,256]{1,0:T(8,128)(2,1)S(1)}, u32[]{:S(2)}, u32[]{:S(2)}) %collective-permute-start.1) | collective-permute-done | bytes 49184 | tf_op jit(solution)/shard_map/ppermute | solution.py:388
  46.9 0.0 collective-permute-start.2
  46.9 0.4 collective-permute-done.5.far_ref
  47.3 0.8 collective-permute-done.4.above_ref
  48.1 0.3 collective-permute-done.3.below_ref
  48.4 0.3 shard_map.61.refs_6_.w_ref
  48.7 0.0 collective-permute-done.2.refs_5_
  48.7 0.0 collective-permute-done.refs_2_
  48.7 3.0 %shard_map.62 = (bf16[16,144,128]{2,1,0:T(8,128)(2,1)}, bf16[1152,128]{1,0:T(8,128)(2,1)S(1)}) custom-call(s32[1]{0:T(128)} %bitcast.1.core_ref.refs_0_, bf16[768,256]{1,0:T(8,128)(2,1)S(1)} %get-tuple-element.12.refs_1_, bf16[768,256]{1,0:T(8,128)(2,1)S(1)} %collective-permute-done.refs_2_, bf16[512,128]{1,0:T(8,128)(2,1)S(1)} %get-tuple-element.13.refs_3_, ...), custom_call_target="tpu_custom_call" | custom-call | tf_op jit(solution)/shard_map/pallas_call | solution.py:37
  51.7 3.8 %all-to-all-start.2 = ((bf16[16,144,128]{2,1,0:T(8,128)(2,1)}), bf16[16,144,128]{2,1,0:T(8,128)(2,1)S(1)}, u32[]{:S(2)}, u32[]{:S(2)}) async-start(bf16[16,144,128]{2,1,0:T(8,128)(2,1)} %get-tuple-element.21), calls=%async_computation.2 | async-start | bytes 1179648 | tf_op jit(solution)/shard_map/all_to_all | solution.py:426
  55.6 1.5 %shard_map.63 = (f32[512,256]{1,0:T(8,128)S(1)}, bf16[512,256]{1,0:T(8,128)(2,1)S(1)}) custom-call(s32[1]{0:T(128)} %bitcast.1.core_ref.refs_0_, bf16[1152,128]{1,0:T(8,128)(2,1)S(1)} %get-tuple-element.16.g_ref, bf16[1152,256]{1,0:T(8,128)(2,1)S(1)} %shard_map.61.refs_6_.w_ref), custom_call_target="tpu_custom_call" | custom-call | tf_op jit(solution)/shard_map/pallas_call | solution.py:37
  57.1 1.8 %collective-permute-start.6 = (bf16[512,256]{1,0:T(8,128)(2,1)S(1)}, bf16[512,256]{1,0:T(8,128)(2,1)S(1)}, u32[]{:S(2)}, u32[]{:S(2)}) collective-permute-start(bf16[512,256]{1,0:T(8,128)(2,1)S(1)} %get-tuple-element.18), channel_id=1, source_target_pairs={{0,16},{16,0},{1,17},{17,1},{2,18},{18,2},{3,19},{19,3},{4,20},{20... | collective-permute-start | bytes 786440 | tf_op jit(solution)/shard_map/ppermute | solution.py:435
  58.9 1.2 %collective-permute-done.6.recv_ref = bf16[512,256]{1,0:T(8,128)(2,1)S(1)} collective-permute-done((bf16[512,256]{1,0:T(8,128)(2,1)S(1)}, bf16[512,256]{1,0:T(8,128)(2,1)S(1)}, u32[]{:S(2)}, u32[]{:S(2)}) %collective-permute-start.6) | collective-permute-done | bytes 262176 | tf_op jit(solution)/shard_map/ppermute | solution.py:435
  60.0 0.4 shard_map.64
  60.4 3.1 %collective-permute-start.7 = (bf16[8,48,128]{2,1,0:T(8,128)(2,1)S(1)}, bf16[8,48,128]{2,1,0:T(8,128)(2,1)S(1)}, u32[]{:S(2)}, u32[]{:S(2)}) collective-permute-start(bf16[8,48,128]{2,1,0:T(8,128)(2,1)S(1)} %get-tuple-element.20), channel_id=1, source_target_pairs={{0,1},{1,0},{2,3},{3,2},{4,5},{5,4},{6,7},{7,6},{8,9},{9,8},{10,11... | collective-permute-start | bytes 294920 | tf_op jit(solution)/shard_map/ppermute | solution.py:445
  63.5 3.4 %collective-permute-done.7.recv_ref = bf16[8,48,128]{2,1,0:T(8,128)(2,1)S(1)} collective-permute-done((bf16[8,48,128]{2,1,0:T(8,128)(2,1)S(1)}, bf16[8,48,128]{2,1,0:T(8,128)(2,1)S(1)}, u32[]{:S(2)}, u32[]{:S(2)}) %collective-permute-start.7) | collective-permute-done | bytes 98336 | tf_op jit(solution)/shard_map/ppermute | solution.py:445
  66.9 0.7 shard_map.65.after_ref
  67.6 6.2 %all-to-all-done.2.r_ref = bf16[16,144,128]{2,1,0:T(8,128)(2,1)S(1)} async-done(((bf16[16,144,128]{2,1,0:T(8,128)(2,1)}), bf16[16,144,128]{2,1,0:T(8,128)(2,1)S(1)}, u32[]{:S(2)}, u32[]{:S(2)}) %all-to-all-start.2) | async-done | bytes 589856 | tf_op jit(solution)/shard_map/all_to_all | solution.py:426
  73.8 4.4 %all-to-all-start.1 = ((bf16[8,96,128]{2,1,0:T(8,128)(2,1)}), bf16[8,96,128]{2,1,0:T(8,128)(2,1)S(1)}, u32[]{:S(2)}, u32[]{:S(2)}) async-start(bf16[8,96,128]{2,1,0:T(8,128)(2,1)} %shard_map.65.after_ref), calls=%async_computation.1 | async-start | bytes 393216 | tf_op jit(solution)/shard_map/all_to_all | solution.py:447
  78.2 0.1 shard_map.67.own_ref
  78.3 3.0 %collective-permute-start.10 = (bf16[144,128]{1,0:T(8,128)(2,1)S(1)}, bf16[144,128]{1,0:T(8,128)(2,1)S(1)}, u32[]{:S(2)}, u32[]{:S(2)}) collective-permute-start(bf16[144,128]{1,0:T(8,128)(2,1)S(1)} %shard_map.67.own_ref), channel_id=1, source_target_pairs={{0,64},{32,96},{64,0},{96,32},{1,65},{33,97},{65,1},{97,33},{2,66}... | collective-permute-start | bytes 110600 | tf_op jit(solution)/shard_map/ppermute | solution.py:452
  81.3 2.2 %collective-permute-start.9 = (bf16[144,128]{1,0:T(8,128)(2,1)S(1)}, bf16[144,128]{1,0:T(8,128)(2,1)S(1)}, u32[]{:S(2)}, u32[]{:S(2)}) collective-permute-start(bf16[144,128]{1,0:T(8,128)(2,1)S(1)} %shard_map.67.own_ref), channel_id=1, source_target_pairs={{0,32},{32,64},{64,96},{96,0},{1,33},{33,65},{65,97},{97,1},{2,34}... | collective-permute-start | bytes 110600 | tf_op jit(solution)/shard_map/ppermute | solution.py:452
  83.6 0.4 collective-permute-start.8
  84.0 0.0 collective-permute-done.10.far_ref
  84.0 1.6 %collective-permute-done.9.prev_ref = bf16[144,128]{1,0:T(8,128)(2,1)S(1)} collective-permute-done((bf16[144,128]{1,0:T(8,128)(2,1)S(1)}, bf16[144,128]{1,0:T(8,128)(2,1)S(1)}, u32[]{:S(2)}, u32[]{:S(2)}) %collective-permute-start.9) | collective-permute-done | bytes 36896 | tf_op jit(solution)/shard_map/ppermute | solution.py:452
  85.7 1.0 %collective-permute-done.8.next_ref = bf16[144,128]{1,0:T(8,128)(2,1)S(1)} collective-permute-done((bf16[144,128]{1,0:T(8,128)(2,1)S(1)}, bf16[144,128]{1,0:T(8,128)(2,1)S(1)}, u32[]{:S(2)}, u32[]{:S(2)}) %collective-permute-start.8) | collective-permute-done | bytes 36896 | tf_op jit(solution)/shard_map/ppermute | solution.py:452
  86.7 2.2 %collective-permute-start.13 = (bf16[144,128]{1,0:T(8,128)(2,1)S(1)}, bf16[144,128]{1,0:T(8,128)(2,1)S(1)}, u32[]{:S(2)}, u32[]{:S(2)}) collective-permute-start(bf16[144,128]{1,0:T(8,128)(2,1)S(1)} %shard_map.68.own_ref), channel_id=1, source_target_pairs={{0,144},{16,128},{128,16},{144,0},{1,145},{17,129},{129,17},{145,1... | collective-permute-start | bytes 110600 | tf_op jit(solution)/shard_map/ppermute | solution.py:461
  88.9 1.3 %collective-permute-start.12 = (bf16[144,128]{1,0:T(8,128)(2,1)S(1)}, bf16[144,128]{1,0:T(8,128)(2,1)S(1)}, u32[]{:S(2)}, u32[]{:S(2)}) collective-permute-start(bf16[144,128]{1,0:T(8,128)(2,1)S(1)} %shard_map.68.own_ref), channel_id=1, source_target_pairs={{0,16},{16,0},{1,17},{17,1},{2,18},{18,2},{3,19},{19,3},{4,20},{20... | collective-permute-start | bytes 110600 | tf_op jit(solution)/shard_map/ppermute | solution.py:460
  90.2 1.3 %collective-permute-start.11 = (bf16[144,128]{1,0:T(8,128)(2,1)S(1)}, bf16[144,128]{1,0:T(8,128)(2,1)S(1)}, u32[]{:S(2)}, u32[]{:S(2)}) collective-permute-start(bf16[144,128]{1,0:T(8,128)(2,1)S(1)} %shard_map.68.own_ref), channel_id=1, source_target_pairs={{0,128},{128,0},{1,129},{129,1},{2,130},{130,2},{3,131},{131,3},{4... | collective-permute-start | bytes 110600 | tf_op jit(solution)/shard_map/ppermute | solution.py:459
  91.4 0.0 all-to-all-done.1.r_ref
  91.4 0.9 shard_map.66
  92.4 0.0 collective-permute-done.13.core_xl_ref
  92.4 0.0 collective-permute-done.12.core_own_ref
  92.4 1.1 %collective-permute-done.11.xl_ref = bf16[144,128]{1,0:T(8,128)(2,1)S(1)} collective-permute-done((bf16[144,128]{1,0:T(8,128)(2,1)S(1)}, bf16[144,128]{1,0:T(8,128)(2,1)S(1)}, u32[]{:S(2)}, u32[]{:S(2)}) %collective-permute-start.11) | collective-permute-done | bytes 36896 | tf_op jit(solution)/shard_map/ppermute | solution.py:459
  93.5 0.7 shard_map.69
  (1 shorter events, 0.0 us)
Async XLA Ops:
  36.6 12.1 %collective-permute-start = (bf16[768,256]{1,0:T(8,128)(2,1)S(1)}, bf16[768,256]{1,0:T(8,128)(2,1)S(1)}, u32[]{:S(2)}, u32[]{:S(2)}) collective-permute-start(bf16[768,256]{1,0:T(8,128)(2,1)S(1)} %get-tuple-element.12.refs_1_), channel_id=1, source_target_pairs={{0,16},{16,0},{1,17},{17,1},{2,18},{18,2},{3,19},{19,3},{4,20},{20... | collective-permute-start | bytes 1179656 | tf_op jit(solution)/shard_map/ppermute | solution.py:387
  38.6 8.7 %collective-permute-start.5 = (bf16[16,40,128]{2,1,0:T(8,128)(2,1)S(1)}, bf16[16,40,128]{2,1,0:T(8,128)(2,1)S(1)}, u32[]{:S(2)}, u32[]{:S(2)}) collective-permute-start(bf16[16,40,128]{2,1,0:T(8,128)(2,1)S(1)} %get-tuple-element.15.own_ref), channel_id=1, source_target_pairs={{0,4},{2,6},{4,8},{6,10},{8,12},{10,14},{12,0},{14,2},{16,28},{18,... | collective-permute-start | bytes 491528 | tf_op jit(solution)/shard_map/ppermute | solution.py:398
  39.0 9.1 %collective-permute-start.4 = (bf16[16,40,128]{2,1,0:T(8,128)(2,1)S(1)}, bf16[16,40,128]{2,1,0:T(8,128)(2,1)S(1)}, u32[]{:S(2)}, u32[]{:S(2)}) collective-permute-start(bf16[16,40,128]{2,1,0:T(8,128)(2,1)S(1)} %get-tuple-element.15.own_ref), channel_id=1, source_target_pairs={{0,14},{2,0},{4,2},{6,4},{8,6},{10,8},{12,10},{14,12},{1,15},{3,1}... | collective-permute-start | bytes 491528 | tf_op jit(solution)/shard_map/ppermute | solution.py:397
  39.2 9.2 %collective-permute-start.3 = (bf16[16,40,128]{2,1,0:T(8,128)(2,1)S(1)}, bf16[16,40,128]{2,1,0:T(8,128)(2,1)S(1)}, u32[]{:S(2)}, u32[]{:S(2)}) collective-permute-start(bf16[16,40,128]{2,1,0:T(8,128)(2,1)S(1)} %get-tuple-element.15.own_ref), channel_id=1, source_target_pairs={{0,2},{2,4},{4,6},{6,8},{8,10},{10,12},{12,14},{14,0},{1,3},{3,5},... | collective-permute-start | bytes 491528 | tf_op jit(solution)/shard_map/ppermute | solution.py:396
  40.5 6.4 %collective-permute-start.1 = (bf16[96,256]{1,0:T(8,128)(2,1)S(1)}, bf16[96,256]{1,0:T(8,128)(2,1)S(1)}, u32[]{:S(2)}, u32[]{:S(2)}) collective-permute-start(bf16[96,256]{1,0:T(8,128)(2,1)S(1)} %get-tuple-element.14), channel_id=1, source_target_pairs={{16,32},{48,64},{80,96},{112,128},{144,160},{176,192},{208,224},{3... | collective-permute-start | bytes 147464 | tf_op jit(solution)/shard_map/ppermute | solution.py:388
  46.9 1.7 %collective-permute-start.2 = (bf16[96,256]{1,0:T(8,128)(2,1)S(1)}, bf16[96,256]{1,0:T(8,128)(2,1)S(1)}, u32[]{:S(2)}, u32[]{:S(2)}) collective-permute-start(bf16[96,256]{1,0:T(8,128)(2,1)S(1)} %collective-permute-done.1.refs_4_), channel_id=1, source_target_pairs={{0,16},{16,0},{1,17},{17,1},{2,18},{18,2},{3,19},{19,3},{4,20},{20... | collective-permute-start | bytes 147464 | tf_op jit(solution)/shard_map/ppermute | solution.py:389
  51.7 22.1 %all-to-all-start.2 = ((bf16[16,144,128]{2,1,0:T(8,128)(2,1)}), bf16[16,144,128]{2,1,0:T(8,128)(2,1)S(1)}, u32[]{:S(2)}, u32[]{:S(2)}) async-start(bf16[16,144,128]{2,1,0:T(8,128)(2,1)} %get-tuple-element.21), calls=%async_computation.2 | async-start | bytes 1179648 | tf_op jit(solution)/shard_map/all_to_all | solution.py:426
  57.1 3.0 %collective-permute-start.6 = (bf16[512,256]{1,0:T(8,128)(2,1)S(1)}, bf16[512,256]{1,0:T(8,128)(2,1)S(1)}, u32[]{:S(2)}, u32[]{:S(2)}) collective-permute-start(bf16[512,256]{1,0:T(8,128)(2,1)S(1)} %get-tuple-element.18), channel_id=1, source_target_pairs={{0,16},{16,0},{1,17},{17,1},{2,18},{18,2},{3,19},{19,3},{4,20},{20... | collective-permute-start | bytes 786440 | tf_op jit(solution)/shard_map/ppermute | solution.py:435
  60.4 6.5 %collective-permute-start.7 = (bf16[8,48,128]{2,1,0:T(8,128)(2,1)S(1)}, bf16[8,48,128]{2,1,0:T(8,128)(2,1)S(1)}, u32[]{:S(2)}, u32[]{:S(2)}) collective-permute-start(bf16[8,48,128]{2,1,0:T(8,128)(2,1)S(1)} %get-tuple-element.20), channel_id=1, source_target_pairs={{0,1},{1,0},{2,3},{3,2},{4,5},{5,4},{6,7},{7,6},{8,9},{9,8},{10,11... | collective-permute-start | bytes 294920 | tf_op jit(solution)/shard_map/ppermute | solution.py:445
  73.8 17.6 %all-to-all-start.1 = ((bf16[8,96,128]{2,1,0:T(8,128)(2,1)}), bf16[8,96,128]{2,1,0:T(8,128)(2,1)S(1)}, u32[]{:S(2)}, u32[]{:S(2)}) async-start(bf16[8,96,128]{2,1,0:T(8,128)(2,1)} %shard_map.65.after_ref), calls=%async_computation.1 | async-start | bytes 393216 | tf_op jit(solution)/shard_map/all_to_all | solution.py:447
  78.3 5.7 %collective-permute-start.10 = (bf16[144,128]{1,0:T(8,128)(2,1)S(1)}, bf16[144,128]{1,0:T(8,128)(2,1)S(1)}, u32[]{:S(2)}, u32[]{:S(2)}) collective-permute-start(bf16[144,128]{1,0:T(8,128)(2,1)S(1)} %shard_map.67.own_ref), channel_id=1, source_target_pairs={{0,64},{32,96},{64,0},{96,32},{1,65},{33,97},{65,1},{97,33},{2,66}... | collective-permute-start | bytes 110600 | tf_op jit(solution)/shard_map/ppermute | solution.py:452
  81.3 4.3 %collective-permute-start.9 = (bf16[144,128]{1,0:T(8,128)(2,1)S(1)}, bf16[144,128]{1,0:T(8,128)(2,1)S(1)}, u32[]{:S(2)}, u32[]{:S(2)}) collective-permute-start(bf16[144,128]{1,0:T(8,128)(2,1)S(1)} %shard_map.67.own_ref), channel_id=1, source_target_pairs={{0,32},{32,64},{64,96},{96,0},{1,33},{33,65},{65,97},{97,1},{2,34}... | collective-permute-start | bytes 110600 | tf_op jit(solution)/shard_map/ppermute | solution.py:452
  83.6 3.1 %collective-permute-start.8 = (bf16[144,128]{1,0:T(8,128)(2,1)S(1)}, bf16[144,128]{1,0:T(8,128)(2,1)S(1)}, u32[]{:S(2)}, u32[]{:S(2)}) collective-permute-start(bf16[144,128]{1,0:T(8,128)(2,1)S(1)} %shard_map.67.own_ref), channel_id=1, source_target_pairs={{0,96},{32,0},{64,32},{96,64},{1,97},{33,1},{65,33},{97,65},{2,98}... | collective-permute-start | bytes 110600 | tf_op jit(solution)/shard_map/ppermute | solution.py:452
  86.7 5.7 %collective-permute-start.13 = (bf16[144,128]{1,0:T(8,128)(2,1)S(1)}, bf16[144,128]{1,0:T(8,128)(2,1)S(1)}, u32[]{:S(2)}, u32[]{:S(2)}) collective-permute-start(bf16[144,128]{1,0:T(8,128)(2,1)S(1)} %shard_map.68.own_ref), channel_id=1, source_target_pairs={{0,144},{16,128},{128,16},{144,0},{1,145},{17,129},{129,17},{145,1... | collective-permute-start | bytes 110600 | tf_op jit(solution)/shard_map/ppermute | solution.py:461
  88.9 3.5 %collective-permute-start.12 = (bf16[144,128]{1,0:T(8,128)(2,1)S(1)}, bf16[144,128]{1,0:T(8,128)(2,1)S(1)}, u32[]{:S(2)}, u32[]{:S(2)}) collective-permute-start(bf16[144,128]{1,0:T(8,128)(2,1)S(1)} %shard_map.68.own_ref), channel_id=1, source_target_pairs={{0,16},{16,0},{1,17},{17,1},{2,18},{18,2},{3,19},{19,3},{4,20},{20... | collective-permute-start | bytes 110600 | tf_op jit(solution)/shard_map/ppermute | solution.py:460
  90.2 3.3 %collective-permute-start.11 = (bf16[144,128]{1,0:T(8,128)(2,1)S(1)}, bf16[144,128]{1,0:T(8,128)(2,1)S(1)}, u32[]{:S(2)}, u32[]{:S(2)}) collective-permute-start(bf16[144,128]{1,0:T(8,128)(2,1)S(1)} %shard_map.68.own_ref), channel_id=1, source_target_pairs={{0,128},{128,0},{1,129},{129,1},{2,130},{130,2},{3,131},{131,3},{4... | collective-permute-start | bytes 110600 | tf_op jit(solution)/shard_map/ppermute | solution.py:459

commit v6 on v5

--- a/solution.py
+++ b/solution.py
@@ -123,12 +123,7 @@
     for r in range(2):
         taps = [mine[t] if (t % 2 == r) else half_up(mine[t]) for t in range(9)] + [mine[8]]
         pairs = [jnp.where(upper, taps[t], taps[t + 1]) for t in range(0, 10, 2)]
-        halves.append(jnp.concatenate(pairs, axis=0).astype(BF))
-    for j in range(16):
-        lane = (j // 2 % 2) * 128
-        buffer[j, 112:152, :] = halves[j // 4 % 2][:, lane : lane + 128]
-    sent = [copy_rows(buffer, out_hbm, 112, 152, out_sems.at[0])]
-
+        halves.append(jnp.concatenate(pairs, axis=0))
     copies[1].wait()
     bias = jnp.broadcast_to(bias_ref[...], (8, 16))
     hi = bias.astype(BF).astype(F32)
@@ -143,14 +138,20 @@
     copies[3].wait()
     x = dot(to_h_ch, x_ref[...].reshape(256, 384)).astype(BF)
     x = fold(dot(x_window, x, NT).reshape(16, 32, 256))
-    buffer[:, 0:48, :] = jnp.concatenate(x[:2], axis=1).astype(BF)
-    sent.append(copy_rows(buffer, out_hbm, 0, 48, out_sems.at[1]))
-
     c = dot(to_half, cot_ref[...].reshape(256, 384)).astype(BF)
     c = fold(dot(cot_window, c, NT).reshape(16, 32, 256))
     c[2] = c[2] + pieces[None]
-    buffer[:, 48:112, :] = jnp.concatenate([x[2]] + c, axis=1).astype(BF)
-    sent.append(copy_rows(buffer, out_hbm, 48, 112, out_sems.at[2]))
+    field = jnp.concatenate(x + c, axis=1)
+    sent = []
+    for first in range(0, 16, 4):
+        for j in range(first, first + 4):
+            lane = (j // 2 % 2) * 128
+            quarter = halves[j // 4 % 2][:, lane : lane + 128]
+            buffer[j] = jnp.concatenate([field[j], quarter], axis=0).astype(BF)
+        slabs = pl.ds(first, 4)
+        copy = pltpu.make_async_copy(buffer.at[slabs], out_hbm.at[slabs], out_sems.at[first // 4])
+        copy.start()
+        sent.append(copy)
     for copy in sent:
         copy.wait()
 
@@ -161,7 +162,7 @@
 def unpack_kernel(core_ref, r_ref, xo_ref, co_ref, ha_ref, w_ref):
     core = core_ref[0]
     edge = []
-    chunks = [r_ref[s, 0:112, :].astype(F32) for s in range(16)]
+    chunks = [r_ref[s].astype(F32) for s in range(16)]
     fields = [unfold(chunk[0:56]) for chunk in chunks]
     for hh in range(2):
         halves = []
@@ -186,7 +187,7 @@
     ha_ref[64:96, 0:128] = jnp.where(first, oth[0], oth[15])
     ha_ref[64:96, 128:256] = jnp.where(first, own[0], own[15])
     for k in range(16):
-        w_ref[k] = r_ref[SOURCES[k], 112:152, :]
+        w_ref[k] = chunks[SOURCES[k]][112:152].astype(BF)
 
 
 def weight_kernel(z_ref, own_ref, below_ref, above_ref, far_ref, w_ref, quarters):
@@ -372,7 +373,7 @@
             pltpu.VMEM((16, 16, 384), BF),
             pltpu.VMEM((16, 152, 128), BF),
             pltpu.SemaphoreType.DMA((4,)),
-            pltpu.SemaphoreType.DMA((3,)),
+            pltpu.SemaphoreType.DMA((4,)),
         ],
     )
     got = lax.all_to_all(packed, CHAN, 0, 0)

time: 94.6 us -> 94.7 us (level)
  no operation moved by 1% of the time
where the time goes in v6:
time: 94.7 us; the launch traced here: 94.3 us
  blocking collectives  32.4 us (34%)
  starting transfers between devices  31.9 us (34%)
  waiting for transfers between devices  18.1 us (19%)
  Pallas kernels  11.2 us (12%)
    all_to_all x1, blocking collectives, shards(): got = lax.all_to_all(packed, CHAN, 0, 0)  32.4 us
    pallas_call x11, Pallas kernels, call(): pl.pallas_call(body, out_shape=[jax.ShapeDtypeStruct(s, d) for s, d in ou...  11.2 us
    all_to_all x1, waiting for transfers between devices, shards(): kg = lax.all_to_all(kg, CHAN, 0, 0)  6.24 us
    ppermute x3, starting transfers between devices, shards(): lax.ppermute(sums, 'y', [(i, (i + k) % 4) for i in range(4)])  5.69 us
    all_to_all x1, starting transfers between devices, shards(): back = lax.all_to_all(joined, 'z', 0, 0)  4.41 us
    ppermute x1, starting transfers between devices, shards(): ha = lax.ppermute(ha, BAND, across)  4.39 us
    all_to_all x1, starting transfers between devices, shards(): kg = lax.all_to_all(kg, CHAN, 0, 0)  3.82 us
    ppermute x1, waiting for transfers between devices, shards(): recv = lax.ppermute(send, 'xh', [(0, 1), (1, 0)])  3.38 us
  transfers between devices with their start and end apart: 16, of which 10 were waited for; matrix products, arithmetic and copies ran while one was open for 0% of the time, Pallas kernels for 4%

profile of v6, /device:TPU:1, one launch (start us, length us, event | category | flops | bytes accessed | tf_op | source)
XLA Modules:
  0.0 94.3 jit_solution(6321933324870537833)
XLA Ops:
  0.6 2.6 %shard_map.59 = bf16[16,152,128]{2,1,0:T(8,128)(2,1)} custom-call(s32[1]{0:T(128)} %bitcast.1.core_ref.refs_0_, bf16[9,16,256]{2,1,0:T(8,128)(2,1)} %bitcast.11, f32[1,16]{1,0:T(1,128)} %bitcast.12, bf16[16,16,384]{2,1,0:T(8,128)(2,1)} %refs_2_.1, bf16[16,16,384]{2,1,0:T(8,128)(2,1)} %refs_3_.1), custom_call_target="tpu_custom_call" | custom-call | tf_op jit(solution)/shard_map/pallas_call | solution.py:37
  3.3 32.4 %all_to_all.15.r_ref = bf16[16,152,128]{2,1,0:T(8,128)(2,1)S(1)} all-to-all(bf16[16,152,128]{2,1,0:T(8,128)(2,1)} %shard_map.59), channel_id=1, replica_groups=mesh['xl'=2,'y'=4,'core'=2,'z'=8,'xh'=2] {'z','xh'}, dimensions={0} | all-to-all | bytes 1245184 | tf_op jit(solution)/shard_map/all_to_all | solution.py:379
  35.7 1.0 %shard_map.60 = (bf16[768,256]{1,0:T(8,128)(2,1)S(1)}, bf16[512,128]{1,0:T(8,128)(2,1)S(1)}, bf16[96,256]{1,0:T(8,128)(2,1)S(1)}, bf16[16,40,128]{2,1,0:T(8,128)(2,1)S(1)}) custom-call(s32[1]{0:T(128)} %bitcast.1.core_ref.refs_0_, bf16[16,152,128]{2,1,0:T(8,128)(2,1)S(1)} %all_to_all.15.r_ref), custom_call_target="tpu_custom_call" | custom-call | tf_op jit(solution)/shard_map/pallas_call | solution.py:37
  36.7 2.0 %collective-permute-start = (bf16[768,256]{1,0:T(8,128)(2,1)S(1)}, bf16[768,256]{1,0:T(8,128)(2,1)S(1)}, u32[]{:S(2)}, u32[]{:S(2)}) collective-permute-start(bf16[768,256]{1,0:T(8,128)(2,1)S(1)} %get-tuple-element.12.refs_1_), channel_id=1, source_target_pairs={{0,16},{16,0},{1,17},{17,1},{2,18},{18,2},{3,19},{19,3},{4,20},{20... | collective-permute-start | bytes 1179656 | tf_op jit(solution)/shard_map/ppermute | solution.py:388
  38.7 0.4 collective-permute-start.5
  39.1 0.2 collective-permute-start.4
  39.3 1.3 %collective-permute-start.3 = (bf16[16,40,128]{2,1,0:T(8,128)(2,1)S(1)}, bf16[16,40,128]{2,1,0:T(8,128)(2,1)S(1)}, u32[]{:S(2)}, u32[]{:S(2)}) collective-permute-start(bf16[16,40,128]{2,1,0:T(8,128)(2,1)S(1)} %get-tuple-element.15.own_ref), channel_id=1, source_target_pairs={{0,2},{2,4},{4,6},{6,8},{8,10},{10,12},{12,14},{14,0},{1,3},{3,5},... | collective-permute-start | bytes 491528 | tf_op jit(solution)/shard_map/ppermute | solution.py:397
  40.6 4.4 %collective-permute-start.1 = (bf16[96,256]{1,0:T(8,128)(2,1)S(1)}, bf16[96,256]{1,0:T(8,128)(2,1)S(1)}, u32[]{:S(2)}, u32[]{:S(2)}) collective-permute-start(bf16[96,256]{1,0:T(8,128)(2,1)S(1)} %get-tuple-element.14), channel_id=1, source_target_pairs={{16,32},{48,64},{80,96},{112,128},{144,160},{176,192},{208,224},{3... | collective-permute-start | bytes 147464 | tf_op jit(solution)/shard_map/ppermute | solution.py:389
  45.0 2.1 %collective-permute-done.1.refs_4_ = bf16[96,256]{1,0:T(8,128)(2,1)S(1)} collective-permute-done((bf16[96,256]{1,0:T(8,128)(2,1)S(1)}, bf16[96,256]{1,0:T(8,128)(2,1)S(1)}, u32[]{:S(2)}, u32[]{:S(2)}) %collective-permute-start.1) | collective-permute-done | bytes 49184 | tf_op jit(solution)/shard_map/ppermute | solution.py:389
  47.0 0.0 collective-permute-start.2
  47.0 0.4 collective-permute-done.5.far_ref
  47.4 0.8 collective-permute-done.4.above_ref
  48.2 0.3 collective-permute-done.3.below_ref
  48.5 0.3 shard_map.61.refs_6_.w_ref
  48.7 0.0 collective-permute-done.2.refs_5_
  48.8 0.0 collective-permute-done.refs_2_
  48.8 3.0 %shard_map.62 = (bf16[16,144,128]{2,1,0:T(8,128)(2,1)}, bf16[1152,128]{1,0:T(8,128)(2,1)S(1)}) custom-call(s32[1]{0:T(128)} %bitcast.1.core_ref.refs_0_, bf16[768,256]{1,0:T(8,128)(2,1)S(1)} %get-tuple-element.12.refs_1_, bf16[768,256]{1,0:T(8,128)(2,1)S(1)} %collective-permute-done.refs_2_, bf16[512,128]{1,0:T(8,128)(2,1)S(1)} %get-tuple-element.13.refs_3_, ...), custom_call_target="tpu_custom_call" | custom-call | tf_op jit(solution)/shard_map/pallas_call | solution.py:37
  51.8 3.8 %all-to-all-start.2 = ((bf16[16,144,128]{2,1,0:T(8,128)(2,1)}), bf16[16,144,128]{2,1,0:T(8,128)(2,1)S(1)}, u32[]{:S(2)}, u32[]{:S(2)}) async-start(bf16[16,144,128]{2,1,0:T(8,128)(2,1)} %get-tuple-element.21), calls=%async_computation.2 | async-start | bytes 1179648 | tf_op jit(solution)/shard_map/all_to_all | solution.py:427
  55.6 1.5 %shard_map.63 = (f32[512,256]{1,0:T(8,128)S(1)}, bf16[512,256]{1,0:T(8,128)(2,1)S(1)}) custom-call(s32[1]{0:T(128)} %bitcast.1.core_ref.refs_0_, bf16[1152,128]{1,0:T(8,128)(2,1)S(1)} %get-tuple-element.16.g_ref, bf16[1152,256]{1,0:T(8,128)(2,1)S(1)} %shard_map.61.refs_6_.w_ref), custom_call_target="tpu_custom_call" | custom-call | tf_op jit(solution)/shard_map/pallas_call | solution.py:37
  57.2 1.8 %collective-permute-start.6 = (bf16[512,256]{1,0:T(8,128)(2,1)S(1)}, bf16[512,256]{1,0:T(8,128)(2,1)S(1)}, u32[]{:S(2)}, u32[]{:S(2)}) collective-permute-start(bf16[512,256]{1,0:T(8,128)(2,1)S(1)} %get-tuple-element.18), channel_id=1, source_target_pairs={{0,16},{16,0},{1,17},{17,1},{2,18},{18,2},{3,19},{19,3},{4,20},{20... | collective-permute-start | bytes 786440 | tf_op jit(solution)/shard_map/ppermute | solution.py:436
  58.9 1.2 %collective-permute-done.6.recv_ref = bf16[512,256]{1,0:T(8,128)(2,1)S(1)} collective-permute-done((bf16[512,256]{1,0:T(8,128)(2,1)S(1)}, bf16[512,256]{1,0:T(8,128)(2,1)S(1)}, u32[]{:S(2)}, u32[]{:S(2)}) %collective-permute-start.6) | collective-permute-done | bytes 262176 | tf_op jit(solution)/shard_map/ppermute | solution.py:436
  60.1 0.4 shard_map.64
  60.5 3.1 %collective-permute-start.7 = (bf16[8,48,128]{2,1,0:T(8,128)(2,1)S(1)}, bf16[8,48,128]{2,1,0:T(8,128)(2,1)S(1)}, u32[]{:S(2)}, u32[]{:S(2)}) collective-permute-start(bf16[8,48,128]{2,1,0:T(8,128)(2,1)S(1)} %get-tuple-element.20), channel_id=1, source_target_pairs={{0,1},{1,0},{2,3},{3,2},{4,5},{5,4},{6,7},{7,6},{8,9},{9,8},{10,11... | collective-permute-start | bytes 294920 | tf_op jit(solution)/shard_map/ppermute | solution.py:446
  63.6 3.4 %collective-permute-done.7.recv_ref = bf16[8,48,128]{2,1,0:T(8,128)(2,1)S(1)} collective-permute-done((bf16[8,48,128]{2,1,0:T(8,128)(2,1)S(1)}, bf16[8,48,128]{2,1,0:T(8,128)(2,1)S(1)}, u32[]{:S(2)}, u32[]{:S(2)}) %collective-permute-start.7) | collective-permute-done | bytes 98336 | tf_op jit(solution)/shard_map/ppermute | solution.py:446
  67.0 0.7 shard_map.65.after_ref
  67.7 6.2 %all-to-all-done.2.r_ref = bf16[16,144,128]{2,1,0:T(8,128)(2,1)S(1)} async-done(((bf16[16,144,128]{2,1,0:T(8,128)(2,1)}), bf16[16,144,128]{2,1,0:T(8,128)(2,1)S(1)}, u32[]{:S(2)}, u32[]{:S(2)}) %all-to-all-start.2) | async-done | bytes 589856 | tf_op jit(solution)/shard_map/all_to_all | solution.py:427
  73.9 4.4 %all-to-all-start.1 = ((bf16[8,96,128]{2,1,0:T(8,128)(2,1)}), bf16[8,96,128]{2,1,0:T(8,128)(2,1)S(1)}, u32[]{:S(2)}, u32[]{:S(2)}) async-start(bf16[8,96,128]{2,1,0:T(8,128)(2,1)} %shard_map.65.after_ref), calls=%async_computation.1 | async-start | bytes 393216 | tf_op jit(solution)/shard_map/all_to_all | solution.py:448
  78.3 0.1 shard_map.67.own_ref
  78.4 3.0 %collective-permute-start.10 = (bf16[144,128]{1,0:T(8,128)(2,1)S(1)}, bf16[144,128]{1,0:T(8,128)(2,1)S(1)}, u32[]{:S(2)}, u32[]{:S(2)}) collective-permute-start(bf16[144,128]{1,0:T(8,128)(2,1)S(1)} %shard_map.67.own_ref), channel_id=1, source_target_pairs={{0,64},{32,96},{64,0},{96,32},{1,65},{33,97},{65,1},{97,33},{2,66}... | collective-permute-start | bytes 110600 | tf_op jit(solution)/shard_map/ppermute | solution.py:453
  81.4 2.2 %collective-permute-start.9 = (bf16[144,128]{1,0:T(8,128)(2,1)S(1)}, bf16[144,128]{1,0:T(8,128)(2,1)S(1)}, u32[]{:S(2)}, u32[]{:S(2)}) collective-permute-start(bf16[144,128]{1,0:T(8,128)(2,1)S(1)} %shard_map.67.own_ref), channel_id=1, source_target_pairs={{0,32},{32,64},{64,96},{96,0},{1,33},{33,65},{65,97},{97,1},{2,34}... | collective-permute-start | bytes 110600 | tf_op jit(solution)/shard_map/ppermute | solution.py:453
  83.7 0.5 collective-permute-start.8
  84.1 0.0 collective-permute-done.10.far_ref
  84.1 1.6 %collective-permute-done.9.prev_ref = bf16[144,128]{1,0:T(8,128)(2,1)S(1)} collective-permute-done((bf16[144,128]{1,0:T(8,128)(2,1)S(1)}, bf16[144,128]{1,0:T(8,128)(2,1)S(1)}, u32[]{:S(2)}, u32[]{:S(2)}) %collective-permute-start.9) | collective-permute-done | bytes 36896 | tf_op jit(solution)/shard_map/ppermute | solution.py:453
  85.8 1.0 %collective-permute-done.8.next_ref = bf16[144,128]{1,0:T(8,128)(2,1)S(1)} collective-permute-done((bf16[144,128]{1,0:T(8,128)(2,1)S(1)}, bf16[144,128]{1,0:T(8,128)(2,1)S(1)}, u32[]{:S(2)}, u32[]{:S(2)}) %collective-permute-start.8) | collective-permute-done | bytes 36896 | tf_op jit(solution)/shard_map/ppermute | solution.py:453
  86.8 2.2 %collective-permute-start.13 = (bf16[144,128]{1,0:T(8,128)(2,1)S(1)}, bf16[144,128]{1,0:T(8,128)(2,1)S(1)}, u32[]{:S(2)}, u32[]{:S(2)}) collective-permute-start(bf16[144,128]{1,0:T(8,128)(2,1)S(1)} %shard_map.68.own_ref), channel_id=1, source_target_pairs={{0,144},{16,128},{128,16},{144,0},{1,145},{17,129},{129,17},{145,1... | collective-permute-start | bytes 110600 | tf_op jit(solution)/shard_map/ppermute | solution.py:462
  89.0 1.3 %collective-permute-start.12 = (bf16[144,128]{1,0:T(8,128)(2,1)S(1)}, bf16[144,128]{1,0:T(8,128)(2,1)S(1)}, u32[]{:S(2)}, u32[]{:S(2)}) collective-permute-start(bf16[144,128]{1,0:T(8,128)(2,1)S(1)} %shard_map.68.own_ref), channel_id=1, source_target_pairs={{0,16},{16,0},{1,17},{17,1},{2,18},{18,2},{3,19},{19,3},{4,20},{20... | collective-permute-start | bytes 110600 | tf_op jit(solution)/shard_map/ppermute | solution.py:461
  90.3 1.3 %collective-permute-start.11 = (bf16[144,128]{1,0:T(8,128)(2,1)S(1)}, bf16[144,128]{1,0:T(8,128)(2,1)S(1)}, u32[]{:S(2)}, u32[]{:S(2)}) collective-permute-start(bf16[144,128]{1,0:T(8,128)(2,1)S(1)} %shard_map.68.own_ref), channel_id=1, source_target_pairs={{0,128},{128,0},{1,129},{129,1},{2,130},{130,2},{3,131},{131,3},{4... | collective-permute-start | bytes 110600 | tf_op jit(solution)/shard_map/ppermute | solution.py:460
  91.5 0.0 all-to-all-done.1.r_ref
  91.5 0.9 shard_map.66
  92.5 0.0 collective-permute-done.13.core_xl_ref
  92.5 0.0 collective-permute-done.12.core_own_ref
  92.5 1.1 %collective-permute-done.11.xl_ref = bf16[144,128]{1,0:T(8,128)(2,1)S(1)} collective-permute-done((bf16[144,128]{1,0:T(8,128)(2,1)S(1)}, bf16[144,128]{1,0:T(8,128)(2,1)S(1)}, u32[]{:S(2)}, u32[]{:S(2)}) %collective-permute-start.11) | collective-permute-done | bytes 36896 | tf_op jit(solution)/shard_map/ppermute | solution.py:460
  93.6 0.7 shard_map.69
  (1 shorter events, 0.0 us)
Async XLA Ops:
  36.7 12.1 %collective-permute-start = (bf16[768,256]{1,0:T(8,128)(2,1)S(1)}, bf16[768,256]{1,0:T(8,128)(2,1)S(1)}, u32[]{:S(2)}, u32[]{:S(2)}) collective-permute-start(bf16[768,256]{1,0:T(8,128)(2,1)S(1)} %get-tuple-element.12.refs_1_), channel_id=1, source_target_pairs={{0,16},{16,0},{1,17},{17,1},{2,18},{18,2},{3,19},{19,3},{4,20},{20... | collective-permute-start | bytes 1179656 | tf_op jit(solution)/shard_map/ppermute | solution.py:388
  38.7 8.7 %collective-permute-start.5 = (bf16[16,40,128]{2,1,0:T(8,128)(2,1)S(1)}, bf16[16,40,128]{2,1,0:T(8,128)(2,1)S(1)}, u32[]{:S(2)}, u32[]{:S(2)}) collective-permute-start(bf16[16,40,128]{2,1,0:T(8,128)(2,1)S(1)} %get-tuple-element.15.own_ref), channel_id=1, source_target_pairs={{0,4},{2,6},{4,8},{6,10},{8,12},{10,14},{12,0},{14,2},{16,28},{18,... | collective-permute-start | bytes 491528 | tf_op jit(solution)/shard_map/ppermute | solution.py:399
  39.1 9.1 %collective-permute-start.4 = (bf16[16,40,128]{2,1,0:T(8,128)(2,1)S(1)}, bf16[16,40,128]{2,1,0:T(8,128)(2,1)S(1)}, u32[]{:S(2)}, u32[]{:S(2)}) collective-permute-start(bf16[16,40,128]{2,1,0:T(8,128)(2,1)S(1)} %get-tuple-element.15.own_ref), channel_id=1, source_target_pairs={{0,14},{2,0},{4,2},{6,4},{8,6},{10,8},{12,10},{14,12},{1,15},{3,1}... | collective-permute-start | bytes 491528 | tf_op jit(solution)/shard_map/ppermute | solution.py:398
  39.3 9.2 %collective-permute-start.3 = (bf16[16,40,128]{2,1,0:T(8,128)(2,1)S(1)}, bf16[16,40,128]{2,1,0:T(8,128)(2,1)S(1)}, u32[]{:S(2)}, u32[]{:S(2)}) collective-permute-start(bf16[16,40,128]{2,1,0:T(8,128)(2,1)S(1)} %get-tuple-element.15.own_ref), channel_id=1, source_target_pairs={{0,2},{2,4},{4,6},{6,8},{8,10},{10,12},{12,14},{14,0},{1,3},{3,5},... | collective-permute-start | bytes 491528 | tf_op jit(solution)/shard_map/ppermute | solution.py:397
  40.6 6.4 %collective-permute-start.1 = (bf16[96,256]{1,0:T(8,128)(2,1)S(1)}, bf16[96,256]{1,0:T(8,128)(2,1)S(1)}, u32[]{:S(2)}, u32[]{:S(2)}) collective-permute-start(bf16[96,256]{1,0:T(8,128)(2,1)S(1)} %get-tuple-element.14), channel_id=1, source_target_pairs={{16,32},{48,64},{80,96},{112,128},{144,160},{176,192},{208,224},{3... | collective-permute-start | bytes 147464 | tf_op jit(solution)/shard_map/ppermute | solution.py:389
  47.0 1.7 %collective-permute-start.2 = (bf16[96,256]{1,0:T(8,128)(2,1)S(1)}, bf16[96,256]{1,0:T(8,128)(2,1)S(1)}, u32[]{:S(2)}, u32[]{:S(2)}) collective-permute-start(bf16[96,256]{1,0:T(8,128)(2,1)S(1)} %collective-permute-done.1.refs_4_), channel_id=1, source_target_pairs={{0,16},{16,0},{1,17},{17,1},{2,18},{18,2},{3,19},{19,3},{4,20},{20... | collective-permute-start | bytes 147464 | tf_op jit(solution)/shard_map/ppermute | solution.py:390
  51.8 22.1 %all-to-all-start.2 = ((bf16[16,144,128]{2,1,0:T(8,128)(2,1)}), bf16[16,144,128]{2,1,0:T(8,128)(2,1)S(1)}, u32[]{:S(2)}, u32[]{:S(2)}) async-start(bf16[16,144,128]{2,1,0:T(8,128)(2,1)} %get-tuple-element.21), calls=%async_computation.2 | async-start | bytes 1179648 | tf_op jit(solution)/shard_map/all_to_all | solution.py:427
  57.2 3.0 %collective-permute-start.6 = (bf16[512,256]{1,0:T(8,128)(2,1)S(1)}, bf16[512,256]{1,0:T(8,128)(2,1)S(1)}, u32[]{:S(2)}, u32[]{:S(2)}) collective-permute-start(bf16[512,256]{1,0:T(8,128)(2,1)S(1)} %get-tuple-element.18), channel_id=1, source_target_pairs={{0,16},{16,0},{1,17},{17,1},{2,18},{18,2},{3,19},{19,3},{4,20},{20... | collective-permute-start | bytes 786440 | tf_op jit(solution)/shard_map/ppermute | solution.py:436
  60.5 6.5 %collective-permute-start.7 = (bf16[8,48,128]{2,1,0:T(8,128)(2,1)S(1)}, bf16[8,48,128]{2,1,0:T(8,128)(2,1)S(1)}, u32[]{:S(2)}, u32[]{:S(2)}) collective-permute-start(bf16[8,48,128]{2,1,0:T(8,128)(2,1)S(1)} %get-tuple-element.20), channel_id=1, source_target_pairs={{0,1},{1,0},{2,3},{3,2},{4,5},{5,4},{6,7},{7,6},{8,9},{9,8},{10,11... | collective-permute-start | bytes 294920 | tf_op jit(solution)/shard_map/ppermute | solution.py:446
  73.9 17.6 %all-to-all-start.1 = ((bf16[8,96,128]{2,1,0:T(8,128)(2,1)}), bf16[8,96,128]{2,1,0:T(8,128)(2,1)S(1)}, u32[]{:S(2)}, u32[]{:S(2)}) async-start(bf16[8,96,128]{2,1,0:T(8,128)(2,1)} %shard_map.65.after_ref), calls=%async_computation.1 | async-start | bytes 393216 | tf_op jit(solution)/shard_map/all_to_all | solution.py:448
  78.4 5.7 %collective-permute-start.10 = (bf16[144,128]{1,0:T(8,128)(2,1)S(1)}, bf16[144,128]{1,0:T(8,128)(2,1)S(1)}, u32[]{:S(2)}, u32[]{:S(2)}) collective-permute-start(bf16[144,128]{1,0:T(8,128)(2,1)S(1)} %shard_map.67.own_ref), channel_id=1, source_target_pairs={{0,64},{32,96},{64,0},{96,32},{1,65},{33,97},{65,1},{97,33},{2,66}... | collective-permute-start | bytes 110600 | tf_op jit(solution)/shard_map/ppermute | solution.py:453
  81.4 4.3 %collective-permute-start.9 = (bf16[144,128]{1,0:T(8,128)(2,1)S(1)}, bf16[144,128]{1,0:T(8,128)(2,1)S(1)}, u32[]{:S(2)}, u32[]{:S(2)}) collective-permute-start(bf16[144,128]{1,0:T(8,128)(2,1)S(1)} %shard_map.67.own_ref), channel_id=1, source_target_pairs={{0,32},{32,64},{64,96},{96,0},{1,33},{33,65},{65,97},{97,1},{2,34}... | collective-permute-start | bytes 110600 | tf_op jit(solution)/shard_map/ppermute | solution.py:453
  83.7 3.1 %collective-permute-start.8 = (bf16[144,128]{1,0:T(8,128)(2,1)S(1)}, bf16[144,128]{1,0:T(8,128)(2,1)S(1)}, u32[]{:S(2)}, u32[]{:S(2)}) collective-permute-start(bf16[144,128]{1,0:T(8,128)(2,1)S(1)} %shard_map.67.own_ref), channel_id=1, source_target_pairs={{0,96},{32,0},{64,32},{96,64},{1,97},{33,1},{65,33},{97,65},{2,98}... | collective-permute-start | bytes 110600 | tf_op jit(solution)/shard_map/ppermute | solution.py:453
  86.8 5.7 %collective-permute-start.13 = (bf16[144,128]{1,0:T(8,128)(2,1)S(1)}, bf16[144,128]{1,0:T(8,128)(2,1)S(1)}, u32[]{:S(2)}, u32[]{:S(2)}) collective-permute-start(bf16[144,128]{1,0:T(8,128)(2,1)S(1)} %shard_map.68.own_ref), channel_id=1, source_target_pairs={{0,144},{16,128},{128,16},{144,0},{1,145},{17,129},{129,17},{145,1... | collective-permute-start | bytes 110600 | tf_op jit(solution)/shard_map/ppermute | solution.py:462
  89.0 3.5 %collective-permute-start.12 = (bf16[144,128]{1,0:T(8,128)(2,1)S(1)}, bf16[144,128]{1,0:T(8,128)(2,1)S(1)}, u32[]{:S(2)}, u32[]{:S(2)}) collective-permute-start(bf16[144,128]{1,0:T(8,128)(2,1)S(1)} %shard_map.68.own_ref), channel_id=1, source_target_pairs={{0,16},{16,0},{1,17},{17,1},{2,18},{18,2},{3,19},{19,3},{4,20},{20... | collective-permute-start | bytes 110600 | tf_op jit(solution)/shard_map/ppermute | solution.py:461
  90.3 3.3 %collective-permute-start.11 = (bf16[144,128]{1,0:T(8,128)(2,1)S(1)}, bf16[144,128]{1,0:T(8,128)(2,1)S(1)}, u32[]{:S(2)}, u32[]{:S(2)}) collective-permute-start(bf16[144,128]{1,0:T(8,128)(2,1)S(1)} %shard_map.68.own_ref), channel_id=1, source_target_pairs={{0,128},{128,0},{1,129},{129,1},{2,130},{130,2},{3,131},{131,3},{4... | collective-permute-start | bytes 110600 | tf_op jit(solution)/shard_map/ppermute | solution.py:460

commit v7 on v6

--- a/solution.py
+++ b/solution.py
@@ -11,6 +11,7 @@
 BF = jnp.bfloat16
 F32 = jnp.float32
 CHAN = ("z", "xh")
+SLOTS = ("xh", "z")
 BAND = ("xl", "y", "core")
 PITCH = 32
 NCOL = 24
@@ -144,10 +145,11 @@
     field = jnp.concatenate(x + c, axis=1)
     sent = []
     for first in range(0, 16, 4):
-        for j in range(first, first + 4):
+        for k in range(first, first + 4):
+            j = SOURCES[k]
             lane = (j // 2 % 2) * 128
             quarter = halves[j // 4 % 2][:, lane : lane + 128]
-            buffer[j] = jnp.concatenate([field[j], quarter], axis=0).astype(BF)
+            buffer[k] = jnp.concatenate([field[j], quarter], axis=0).astype(BF)
         slabs = pl.ds(first, 4)
         copy = pltpu.make_async_copy(buffer.at[slabs], out_hbm.at[slabs], out_sems.at[first // 4])
         copy.start()
@@ -162,7 +164,7 @@
 def unpack_kernel(core_ref, r_ref, xo_ref, co_ref, ha_ref, w_ref):
     core = core_ref[0]
     edge = []
-    chunks = [r_ref[s].astype(F32) for s in range(16)]
+    chunks = [r_ref[s % 2 * 8 + s // 2].astype(F32) for s in range(16)]
     fields = [unfold(chunk[0:56]) for chunk in chunks]
     for hh in range(2):
         halves = []
@@ -264,7 +266,7 @@
             for b in range(3):
                 tap = block[128 * b + 8 * k : 128 * b + 8 * k + 8]
                 rows += [tap[:, 0:128], tap[:, 128:256]]
-            buffer[SOURCES[k], 48 * a : 48 * a + 48, :] = jnp.concatenate(rows, axis=0).astype(BF)
+            buffer[k, 48 * a : 48 * a + 48, :] = jnp.concatenate(rows, axis=0).astype(BF)
         sent.append(copy_rows(buffer, kg_hbm, 48 * a, 48 * a + 48, sems.at[a]))
     for copy in sent:
         copy.wait()
@@ -376,7 +378,7 @@
             pltpu.SemaphoreType.DMA((4,)),
         ],
     )
-    got = lax.all_to_all(packed, CHAN, 0, 0)
+    got = lax.all_to_all(packed, SLOTS, 0, 0)
     xo, co, ha, w_part = call(
         unpack_kernel,
         [((768, 256), BF), ((512, 128), BF), ((96, 256), BF), ((16, 40, 128), BF)],
@@ -424,7 +426,7 @@
         ],
         copied=(0,),
     )
-    kg = lax.all_to_all(kg, CHAN, 0, 0)
+    kg = lax.all_to_all(kg, SLOTS, 0, 0)
     own, send = call(
         input_kernel,
         [((512, 256), F32), ((512, 256), BF)],

time: 94.7 us -> 92.5 us (0.977)
  blocking collectives: 32.4 us -> 30.4 us
  waiting for transfers between devices: 18.1 us -> 16.5 us
  starting transfers between devices: 31.9 us -> 33 us
    all_to_all x1, waiting for transfers between devices: 6.24 us -> 2.03 us  [shards(): kg = lax.all_to_all(kg, SLOTS, 0, 0)]
    ppermute x1, waiting for transfers between devices: 3.38 us -> 5.9 us  [shards(): recv = lax.ppermute(send, 'xh', [(0, 1), (1, 0)])]
    all_to_all x1, blocking collectives: 32.4 us -> 30.4 us  [shards(): got = lax.all_to_all(packed, SLOTS, 0, 0)]
    ppermute x1, starting transfers between devices: 1.29 us -> 0.12 us  [shards(): lax.ppermute(sums, 'core', [(0, 1), (1, 0)])]
    ppermute x1, starting transfers between devices: 1.97 us -> 3.09 us  [shards(): xr = lax.ppermute(xo, 'core', [(0, 1), (1, 0)])]
  transfers between devices with their start and end apart: 16 -> 16, of which waited for: 10 -> 9; matrix products, arithmetic and copies ran while one was open for 0% -> 0% of each run, Pallas kernels for 4% -> 4%
where the time goes in v7:
time: 92.5 us; the launch traced here: 91.9 us
  starting transfers between devices  33 us (36%)
  blocking collectives  30.4 us (33%)
  waiting for transfers between devices  16.5 us (18%)
  Pallas kernels  11.3 us (12%)
    all_to_all x1, blocking collectives, shards(): got = lax.all_to_all(packed, SLOTS, 0, 0)  30.4 us
    pallas_call x11, Pallas kernels, call(): pl.pallas_call(body, out_shape=[jax.ShapeDtypeStruct(s, d) for s, d in ou...  11.3 us
    ppermute x1, waiting for transfers between devices, shards(): recv = lax.ppermute(send, 'xh', [(0, 1), (1, 0)])  5.9 us
    ppermute x3, starting transfers between devices, shards(): lax.ppermute(sums, 'y', [(i, (i + k) % 4) for i in range(4)])  5.67 us
    all_to_all x1, starting transfers between devices, shards(): back = lax.all_to_all(joined, 'z', 0, 0)  5.07 us
    ppermute x1, starting transfers between devices, shards(): ha = lax.ppermute(ha, BAND, across)  4.48 us
    all_to_all x1, starting transfers between devices, shards(): kg = lax.all_to_all(kg, SLOTS, 0, 0)  4.1 us
    ppermute x1, starting transfers between devices, shards(): recv = lax.ppermute(send, 'xh', [(0, 1), (1, 0)])  3.16 us
  transfers between devices with their start and end apart: 16, of which 9 were waited for; matrix products, arithmetic and copies ran while one was open for 0% of the time, Pallas kernels for 4%

profile of v7, /device:TPU:1, one launch (start us, length us, event | category | flops | bytes accessed | tf_op | source)
XLA Modules:
  0.0 91.9 jit_solution(12644327997421097867)
XLA Ops:
  0.6 2.7 %shard_map.59 = bf16[16,152,128]{2,1,0:T(8,128)(2,1)} custom-call(s32[1]{0:T(128)} %bitcast.1.core_ref.refs_0_, bf16[9,16,256]{2,1,0:T(8,128)(2,1)} %bitcast.11, f32[1,16]{1,0:T(1,128)} %bitcast.12, bf16[16,16,384]{2,1,0:T(8,128)(2,1)} %refs_2_.1, bf16[16,16,384]{2,1,0:T(8,128)(2,1)} %refs_3_.1), custom_call_target="tpu_custom_call" | custom-call | tf_op jit(solution)/shard_map/pallas_call | solution.py:38
  3.3 30.4 %all_to_all.15.r_ref = bf16[16,152,128]{2,1,0:T(8,128)(2,1)S(1)} all-to-all(bf16[16,152,128]{2,1,0:T(8,128)(2,1)} %shard_map.59), channel_id=1, replica_groups=mesh['xl'=2,'y'=4,'core'=2,'z'=8,'xh'=2] {'xh','z'}, dimensions={0} | all-to-all | bytes 1245184 | tf_op jit(solution)/shard_map/all_to_all | solution.py:381
  33.7 1.0 %shard_map.60 = (bf16[768,256]{1,0:T(8,128)(2,1)S(1)}, bf16[512,128]{1,0:T(8,128)(2,1)S(1)}, bf16[96,256]{1,0:T(8,128)(2,1)S(1)}, bf16[16,40,128]{2,1,0:T(8,128)(2,1)S(1)}) custom-call(s32[1]{0:T(128)} %bitcast.1.core_ref.refs_0_, bf16[16,152,128]{2,1,0:T(8,128)(2,1)S(1)} %all_to_all.15.r_ref), custom_call_target="tpu_custom_call" | custom-call | tf_op jit(solution)/shard_map/pallas_call | solution.py:38
  34.7 3.1 %collective-permute-start = (bf16[768,256]{1,0:T(8,128)(2,1)S(1)}, bf16[768,256]{1,0:T(8,128)(2,1)S(1)}, u32[]{:S(2)}, u32[]{:S(2)}) collective-permute-start(bf16[768,256]{1,0:T(8,128)(2,1)S(1)} %get-tuple-element.12.refs_1_), channel_id=1, source_target_pairs={{0,16},{16,0},{1,17},{17,1},{2,18},{18,2},{3,19},{19,3},{4,20},{20... | collective-permute-start | bytes 1179656 | tf_op jit(solution)/shard_map/ppermute | solution.py:390
  37.8 1.1 %collective-permute-start.5 = (bf16[16,40,128]{2,1,0:T(8,128)(2,1)S(1)}, bf16[16,40,128]{2,1,0:T(8,128)(2,1)S(1)}, u32[]{:S(2)}, u32[]{:S(2)}) collective-permute-start(bf16[16,40,128]{2,1,0:T(8,128)(2,1)S(1)} %get-tuple-element.15.own_ref), channel_id=1, source_target_pairs={{0,4},{2,6},{4,8},{6,10},{8,12},{10,14},{12,0},{14,2},{16,28},{18,... | collective-permute-start | bytes 491528 | tf_op jit(solution)/shard_map/ppermute | solution.py:401
  38.9 0.5 collective-permute-start.4
  39.4 1.0 %collective-permute-start.3 = (bf16[16,40,128]{2,1,0:T(8,128)(2,1)S(1)}, bf16[16,40,128]{2,1,0:T(8,128)(2,1)S(1)}, u32[]{:S(2)}, u32[]{:S(2)}) collective-permute-start(bf16[16,40,128]{2,1,0:T(8,128)(2,1)S(1)} %get-tuple-element.15.own_ref), channel_id=1, source_target_pairs={{0,2},{2,4},{4,6},{6,8},{8,10},{10,12},{12,14},{14,0},{1,3},{3,5},... | collective-permute-start | bytes 491528 | tf_op jit(solution)/shard_map/ppermute | solution.py:399
  40.4 4.5 %collective-permute-start.1 = (bf16[96,256]{1,0:T(8,128)(2,1)S(1)}, bf16[96,256]{1,0:T(8,128)(2,1)S(1)}, u32[]{:S(2)}, u32[]{:S(2)}) collective-permute-start(bf16[96,256]{1,0:T(8,128)(2,1)S(1)} %get-tuple-element.14), channel_id=1, source_target_pairs={{16,32},{48,64},{80,96},{112,128},{144,160},{176,192},{208,224},{3... | collective-permute-start | bytes 147464 | tf_op jit(solution)/shard_map/ppermute | solution.py:391
  44.9 2.1 %collective-permute-done.1.refs_4_ = bf16[96,256]{1,0:T(8,128)(2,1)S(1)} collective-permute-done((bf16[96,256]{1,0:T(8,128)(2,1)S(1)}, bf16[96,256]{1,0:T(8,128)(2,1)S(1)}, u32[]{:S(2)}, u32[]{:S(2)}) %collective-permute-start.1) | collective-permute-done | bytes 49184 | tf_op jit(solution)/shard_map/ppermute | solution.py:391
  46.9 0.0 collective-permute-start.2
  46.9 0.0 collective-permute-done.5.far_ref
  46.9 1.4 %collective-permute-done.4.above_ref = bf16[16,40,128]{2,1,0:T(8,128)(2,1)S(1)} collective-permute-done((bf16[16,40,128]{2,1,0:T(8,128)(2,1)S(1)}, bf16[16,40,128]{2,1,0:T(8,128)(2,1)S(1)}, u32[]{:S(2)}, u32[]{:S(2)}) %collective-permute-start.4) | collective-permute-done | bytes 163872 | tf_op jit(solution)/shard_map/ppermute | solution.py:400
  48.3 0.2 collective-permute-done.3.below_ref
  48.5 0.3 shard_map.61.refs_6_.w_ref
  48.8 0.0 collective-permute-done.2.refs_5_
  48.8 0.0 collective-permute-done.refs_2_
  48.8 3.0 %shard_map.62 = (bf16[16,144,128]{2,1,0:T(8,128)(2,1)}, bf16[1152,128]{1,0:T(8,128)(2,1)S(1)}) custom-call(s32[1]{0:T(128)} %bitcast.1.core_ref.refs_0_, bf16[768,256]{1,0:T(8,128)(2,1)S(1)} %get-tuple-element.12.refs_1_, bf16[768,256]{1,0:T(8,128)(2,1)S(1)} %collective-permute-done.refs_2_, bf16[512,128]{1,0:T(8,128)(2,1)S(1)} %get-tuple-element.13.refs_3_, ...), custom_call_target="tpu_custom_call" | custom-call | tf_op jit(solution)/shard_map/pallas_call | solution.py:38
  51.8 4.1 %all-to-all-start.2 = ((bf16[16,144,128]{2,1,0:T(8,128)(2,1)}), bf16[16,144,128]{2,1,0:T(8,128)(2,1)S(1)}, u32[]{:S(2)}, u32[]{:S(2)}) async-start(bf16[16,144,128]{2,1,0:T(8,128)(2,1)} %get-tuple-element.21), calls=%async_computation.2 | async-start | bytes 1179648 | tf_op jit(solution)/shard_map/all_to_all | solution.py:429
  56.0 1.5 %shard_map.63 = (f32[512,256]{1,0:T(8,128)S(1)}, bf16[512,256]{1,0:T(8,128)(2,1)S(1)}) custom-call(s32[1]{0:T(128)} %bitcast.1.core_ref.refs_0_, bf16[1152,128]{1,0:T(8,128)(2,1)S(1)} %get-tuple-element.16.g_ref, bf16[1152,256]{1,0:T(8,128)(2,1)S(1)} %shard_map.61.refs_6_.w_ref), custom_call_target="tpu_custom_call" | custom-call | tf_op jit(solution)/shard_map/pallas_call | solution.py:38
  57.5 1.4 %collective-permute-start.6 = (bf16[512,256]{1,0:T(8,128)(2,1)S(1)}, bf16[512,256]{1,0:T(8,128)(2,1)S(1)}, u32[]{:S(2)}, u32[]{:S(2)}) collective-permute-start(bf16[512,256]{1,0:T(8,128)(2,1)S(1)} %get-tuple-element.18), channel_id=1, source_target_pairs={{0,16},{16,0},{1,17},{17,1},{2,18},{18,2},{3,19},{19,3},{4,20},{20... | collective-permute-start | bytes 786440 | tf_op jit(solution)/shard_map/ppermute | solution.py:438
  58.8 1.2 %collective-permute-done.6.recv_ref = bf16[512,256]{1,0:T(8,128)(2,1)S(1)} collective-permute-done((bf16[512,256]{1,0:T(8,128)(2,1)S(1)}, bf16[512,256]{1,0:T(8,128)(2,1)S(1)}, u32[]{:S(2)}, u32[]{:S(2)}) %collective-permute-start.6) | collective-permute-done | bytes 262176 | tf_op jit(solution)/shard_map/ppermute | solution.py:438
  60.0 0.4 shard_map.64
  60.4 3.2 %collective-permute-start.7 = (bf16[8,48,128]{2,1,0:T(8,128)(2,1)S(1)}, bf16[8,48,128]{2,1,0:T(8,128)(2,1)S(1)}, u32[]{:S(2)}, u32[]{:S(2)}) collective-permute-start(bf16[8,48,128]{2,1,0:T(8,128)(2,1)S(1)} %get-tuple-element.20), channel_id=1, source_target_pairs={{0,1},{1,0},{2,3},{3,2},{4,5},{5,4},{6,7},{7,6},{8,9},{9,8},{10,11... | collective-permute-start | bytes 294920 | tf_op jit(solution)/shard_map/ppermute | solution.py:448
  63.5 5.9 %collective-permute-done.7.recv_ref = bf16[8,48,128]{2,1,0:T(8,128)(2,1)S(1)} collective-permute-done((bf16[8,48,128]{2,1,0:T(8,128)(2,1)S(1)}, bf16[8,48,128]{2,1,0:T(8,128)(2,1)S(1)}, u32[]{:S(2)}, u32[]{:S(2)}) %collective-permute-start.7) | collective-permute-done | bytes 98336 | tf_op jit(solution)/shard_map/ppermute | solution.py:448
  69.4 0.7 shard_map.65.after_ref
  70.2 2.0 %all-to-all-done.2.r_ref = bf16[16,144,128]{2,1,0:T(8,128)(2,1)S(1)} async-done(((bf16[16,144,128]{2,1,0:T(8,128)(2,1)}), bf16[16,144,128]{2,1,0:T(8,128)(2,1)S(1)}, u32[]{:S(2)}, u32[]{:S(2)}) %all-to-all-start.2) | async-done | bytes 589856 | tf_op jit(solution)/shard_map/all_to_all | solution.py:429
  72.2 5.1 %all-to-all-start.1 = ((bf16[8,96,128]{2,1,0:T(8,128)(2,1)}), bf16[8,96,128]{2,1,0:T(8,128)(2,1)S(1)}, u32[]{:S(2)}, u32[]{:S(2)}) async-start(bf16[8,96,128]{2,1,0:T(8,128)(2,1)} %shard_map.65.after_ref), calls=%async_computation.1 | async-start | bytes 393216 | tf_op jit(solution)/shard_map/all_to_all | solution.py:450
  77.2 0.1 shard_map.67.own_ref
  77.3 3.0 %collective-permute-start.10 = (bf16[144,128]{1,0:T(8,128)(2,1)S(1)}, bf16[144,128]{1,0:T(8,128)(2,1)S(1)}, u32[]{:S(2)}, u32[]{:S(2)}) collective-permute-start(bf16[144,128]{1,0:T(8,128)(2,1)S(1)} %shard_map.67.own_ref), channel_id=1, source_target_pairs={{0,64},{32,96},{64,0},{96,32},{1,65},{33,97},{65,1},{97,33},{2,66}... | collective-permute-start | bytes 110600 | tf_op jit(solution)/shard_map/ppermute | solution.py:455
  80.3 2.3 %collective-permute-start.9 = (bf16[144,128]{1,0:T(8,128)(2,1)S(1)}, bf16[144,128]{1,0:T(8,128)(2,1)S(1)}, u32[]{:S(2)}, u32[]{:S(2)}) collective-permute-start(bf16[144,128]{1,0:T(8,128)(2,1)S(1)} %shard_map.67.own_ref), channel_id=1, source_target_pairs={{0,32},{32,64},{64,96},{96,0},{1,33},{33,65},{65,97},{97,1},{2,34}... | collective-permute-start | bytes 110600 | tf_op jit(solution)/shard_map/ppermute | solution.py:455
  82.6 0.4 collective-permute-start.8
  83.0 0.0 collective-permute-done.10.far_ref
  83.0 1.9 %collective-permute-done.9.prev_ref = bf16[144,128]{1,0:T(8,128)(2,1)S(1)} collective-permute-done((bf16[144,128]{1,0:T(8,128)(2,1)S(1)}, bf16[144,128]{1,0:T(8,128)(2,1)S(1)}, u32[]{:S(2)}, u32[]{:S(2)}) %collective-permute-start.9) | collective-permute-done | bytes 36896 | tf_op jit(solution)/shard_map/ppermute | solution.py:455
  84.9 1.1 %collective-permute-done.8.next_ref = bf16[144,128]{1,0:T(8,128)(2,1)S(1)} collective-permute-done((bf16[144,128]{1,0:T(8,128)(2,1)S(1)}, bf16[144,128]{1,0:T(8,128)(2,1)S(1)}, u32[]{:S(2)}, u32[]{:S(2)}) %collective-permute-start.8) | collective-permute-done | bytes 36896 | tf_op jit(solution)/shard_map/ppermute | solution.py:455
  86.0 2.1 %collective-permute-start.13 = (bf16[144,128]{1,0:T(8,128)(2,1)S(1)}, bf16[144,128]{1,0:T(8,128)(2,1)S(1)}, u32[]{:S(2)}, u32[]{:S(2)}) collective-permute-start(bf16[144,128]{1,0:T(8,128)(2,1)S(1)} %shard_map.68.own_ref), channel_id=1, source_target_pairs={{0,144},{16,128},{128,16},{144,0},{1,145},{17,129},{129,17},{145,1... | collective-permute-start | bytes 110600 | tf_op jit(solution)/shard_map/ppermute | solution.py:464
  88.1 0.1 collective-permute-start.12
  88.2 1.3 %collective-permute-start.11 = (bf16[144,128]{1,0:T(8,128)(2,1)S(1)}, bf16[144,128]{1,0:T(8,128)(2,1)S(1)}, u32[]{:S(2)}, u32[]{:S(2)}) collective-permute-start(bf16[144,128]{1,0:T(8,128)(2,1)S(1)} %shard_map.68.own_ref), channel_id=1, source_target_pairs={{0,128},{128,0},{1,129},{129,1},{2,130},{130,2},{3,131},{131,3},{4... | collective-permute-start | bytes 110600 | tf_op jit(solution)/shard_map/ppermute | solution.py:462
  89.5 0.0 all-to-all-done.1.r_ref
  89.5 0.9 %shard_map.66 = bf16[16,16,384]{2,1,0:T(8,128)(2,1)} custom-call(bf16[8,96,128]{2,1,0:T(8,128)(2,1)S(1)} %all-to-all-done.1.r_ref), custom_call_target="tpu_custom_call" | custom-call | tf_op jit(solution)/shard_map/pallas_call | solution.py:38
  90.4 0.0 collective-permute-done.13.core_xl_ref
  90.4 0.0 collective-permute-done.12.core_own_ref
  90.4 0.8 collective-permute-done.11.xl_ref
  91.2 0.7 shard_map.69
  (1 shorter events, 0.0 us)
Async XLA Ops:
  34.7 14.1 %collective-permute-start = (bf16[768,256]{1,0:T(8,128)(2,1)S(1)}, bf16[768,256]{1,0:T(8,128)(2,1)S(1)}, u32[]{:S(2)}, u32[]{:S(2)}) collective-permute-start(bf16[768,256]{1,0:T(8,128)(2,1)S(1)} %get-tuple-element.12.refs_1_), channel_id=1, source_target_pairs={{0,16},{16,0},{1,17},{17,1},{2,18},{18,2},{3,19},{19,3},{4,20},{20... | collective-permute-start | bytes 1179656 | tf_op jit(solution)/shard_map/ppermute | solution.py:390
  37.8 9.1 %collective-permute-start.5 = (bf16[16,40,128]{2,1,0:T(8,128)(2,1)S(1)}, bf16[16,40,128]{2,1,0:T(8,128)(2,1)S(1)}, u32[]{:S(2)}, u32[]{:S(2)}) collective-permute-start(bf16[16,40,128]{2,1,0:T(8,128)(2,1)S(1)} %get-tuple-element.15.own_ref), channel_id=1, source_target_pairs={{0,4},{2,6},{4,8},{6,10},{8,12},{10,14},{12,0},{14,2},{16,28},{18,... | collective-permute-start | bytes 491528 | tf_op jit(solution)/shard_map/ppermute | solution.py:401
  38.9 9.4 %collective-permute-start.4 = (bf16[16,40,128]{2,1,0:T(8,128)(2,1)S(1)}, bf16[16,40,128]{2,1,0:T(8,128)(2,1)S(1)}, u32[]{:S(2)}, u32[]{:S(2)}) collective-permute-start(bf16[16,40,128]{2,1,0:T(8,128)(2,1)S(1)} %get-tuple-element.15.own_ref), channel_id=1, source_target_pairs={{0,14},{2,0},{4,2},{6,4},{8,6},{10,8},{12,10},{14,12},{1,15},{3,1}... | collective-permute-start | bytes 491528 | tf_op jit(solution)/shard_map/ppermute | solution.py:400
  39.4 9.1 %collective-permute-start.3 = (bf16[16,40,128]{2,1,0:T(8,128)(2,1)S(1)}, bf16[16,40,128]{2,1,0:T(8,128)(2,1)S(1)}, u32[]{:S(2)}, u32[]{:S(2)}) collective-permute-start(bf16[16,40,128]{2,1,0:T(8,128)(2,1)S(1)} %get-tuple-element.15.own_ref), channel_id=1, source_target_pairs={{0,2},{2,4},{4,6},{6,8},{8,10},{10,12},{12,14},{14,0},{1,3},{3,5},... | collective-permute-start | bytes 491528 | tf_op jit(solution)/shard_map/ppermute | solution.py:399
  40.4 6.5 %collective-permute-start.1 = (bf16[96,256]{1,0:T(8,128)(2,1)S(1)}, bf16[96,256]{1,0:T(8,128)(2,1)S(1)}, u32[]{:S(2)}, u32[]{:S(2)}) collective-permute-start(bf16[96,256]{1,0:T(8,128)(2,1)S(1)} %get-tuple-element.14), channel_id=1, source_target_pairs={{16,32},{48,64},{80,96},{112,128},{144,160},{176,192},{208,224},{3... | collective-permute-start | bytes 147464 | tf_op jit(solution)/shard_map/ppermute | solution.py:391
  46.9 1.9 %collective-permute-start.2 = (bf16[96,256]{1,0:T(8,128)(2,1)S(1)}, bf16[96,256]{1,0:T(8,128)(2,1)S(1)}, u32[]{:S(2)}, u32[]{:S(2)}) collective-permute-start(bf16[96,256]{1,0:T(8,128)(2,1)S(1)} %collective-permute-done.1.refs_4_), channel_id=1, source_target_pairs={{0,16},{16,0},{1,17},{17,1},{2,18},{18,2},{3,19},{19,3},{4,20},{20... | collective-permute-start | bytes 147464 | tf_op jit(solution)/shard_map/ppermute | solution.py:392
  51.8 20.3 %all-to-all-start.2 = ((bf16[16,144,128]{2,1,0:T(8,128)(2,1)}), bf16[16,144,128]{2,1,0:T(8,128)(2,1)S(1)}, u32[]{:S(2)}, u32[]{:S(2)}) async-start(bf16[16,144,128]{2,1,0:T(8,128)(2,1)} %get-tuple-element.21), calls=%async_computation.2 | async-start | bytes 1179648 | tf_op jit(solution)/shard_map/all_to_all | solution.py:429
  57.5 2.5 %collective-permute-start.6 = (bf16[512,256]{1,0:T(8,128)(2,1)S(1)}, bf16[512,256]{1,0:T(8,128)(2,1)S(1)}, u32[]{:S(2)}, u32[]{:S(2)}) collective-permute-start(bf16[512,256]{1,0:T(8,128)(2,1)S(1)} %get-tuple-element.18), channel_id=1, source_target_pairs={{0,16},{16,0},{1,17},{17,1},{2,18},{18,2},{3,19},{19,3},{4,20},{20... | collective-permute-start | bytes 786440 | tf_op jit(solution)/shard_map/ppermute | solution.py:438
  60.4 9.1 %collective-permute-start.7 = (bf16[8,48,128]{2,1,0:T(8,128)(2,1)S(1)}, bf16[8,48,128]{2,1,0:T(8,128)(2,1)S(1)}, u32[]{:S(2)}, u32[]{:S(2)}) collective-permute-start(bf16[8,48,128]{2,1,0:T(8,128)(2,1)S(1)} %get-tuple-element.20), channel_id=1, source_target_pairs={{0,1},{1,0},{2,3},{3,2},{4,5},{5,4},{6,7},{7,6},{8,9},{9,8},{10,11... | collective-permute-start | bytes 294920 | tf_op jit(solution)/shard_map/ppermute | solution.py:448
  72.2 17.3 %all-to-all-start.1 = ((bf16[8,96,128]{2,1,0:T(8,128)(2,1)}), bf16[8,96,128]{2,1,0:T(8,128)(2,1)S(1)}, u32[]{:S(2)}, u32[]{:S(2)}) async-start(bf16[8,96,128]{2,1,0:T(8,128)(2,1)} %shard_map.65.after_ref), calls=%async_computation.1 | async-start | bytes 393216 | tf_op jit(solution)/shard_map/all_to_all | solution.py:450
  77.3 5.7 %collective-permute-start.10 = (bf16[144,128]{1,0:T(8,128)(2,1)S(1)}, bf16[144,128]{1,0:T(8,128)(2,1)S(1)}, u32[]{:S(2)}, u32[]{:S(2)}) collective-permute-start(bf16[144,128]{1,0:T(8,128)(2,1)S(1)} %shard_map.67.own_ref), channel_id=1, source_target_pairs={{0,64},{32,96},{64,0},{96,32},{1,65},{33,97},{65,1},{97,33},{2,66}... | collective-permute-start | bytes 110600 | tf_op jit(solution)/shard_map/ppermute | solution.py:455
  80.3 4.5 %collective-permute-start.9 = (bf16[144,128]{1,0:T(8,128)(2,1)S(1)}, bf16[144,128]{1,0:T(8,128)(2,1)S(1)}, u32[]{:S(2)}, u32[]{:S(2)}) collective-permute-start(bf16[144,128]{1,0:T(8,128)(2,1)S(1)} %shard_map.67.own_ref), channel_id=1, source_target_pairs={{0,32},{32,64},{64,96},{96,0},{1,33},{33,65},{65,97},{97,1},{2,34}... | collective-permute-start | bytes 110600 | tf_op jit(solution)/shard_map/ppermute | solution.py:455
  82.6 3.3 %collective-permute-start.8 = (bf16[144,128]{1,0:T(8,128)(2,1)S(1)}, bf16[144,128]{1,0:T(8,128)(2,1)S(1)}, u32[]{:S(2)}, u32[]{:S(2)}) collective-permute-start(bf16[144,128]{1,0:T(8,128)(2,1)S(1)} %shard_map.67.own_ref), channel_id=1, source_target_pairs={{0,96},{32,0},{64,32},{96,64},{1,97},{33,1},{65,33},{97,65},{2,98}... | collective-permute-start | bytes 110600 | tf_op jit(solution)/shard_map/ppermute | solution.py:455
  86.0 4.4 %collective-permute-start.13 = (bf16[144,128]{1,0:T(8,128)(2,1)S(1)}, bf16[144,128]{1,0:T(8,128)(2,1)S(1)}, u32[]{:S(2)}, u32[]{:S(2)}) collective-permute-start(bf16[144,128]{1,0:T(8,128)(2,1)S(1)} %shard_map.68.own_ref), channel_id=1, source_target_pairs={{0,144},{16,128},{128,16},{144,0},{1,145},{17,129},{129,17},{145,1... | collective-permute-start | bytes 110600 | tf_op jit(solution)/shard_map/ppermute | solution.py:464
  88.1 2.3 %collective-permute-start.12 = (bf16[144,128]{1,0:T(8,128)(2,1)S(1)}, bf16[144,128]{1,0:T(8,128)(2,1)S(1)}, u32[]{:S(2)}, u32[]{:S(2)}) collective-permute-start(bf16[144,128]{1,0:T(8,128)(2,1)S(1)} %shard_map.68.own_ref), channel_id=1, source_target_pairs={{0,16},{16,0},{1,17},{17,1},{2,18},{18,2},{3,19},{19,3},{4,20},{20... | collective-permute-start | bytes 110600 | tf_op jit(solution)/shard_map/ppermute | solution.py:463
  88.2 3.0 %collective-permute-start.11 = (bf16[144,128]{1,0:T(8,128)(2,1)S(1)}, bf16[144,128]{1,0:T(8,128)(2,1)S(1)}, u32[]{:S(2)}, u32[]{:S(2)}) collective-permute-start(bf16[144,128]{1,0:T(8,128)(2,1)S(1)} %shard_map.68.own_ref), channel_id=1, source_target_pairs={{0,128},{128,0},{1,129},{129,1},{2,130},{130,2},{3,131},{131,3},{4... | collective-permute-start | bytes 110600 | tf_op jit(solution)/shard_map/ppermute | solution.py:462

commit v8 on v7

--- a/solution.py
+++ b/solution.py
@@ -261,13 +261,15 @@
     sent = []
     for a in range(3):
         block = dot(shifted, x[32 * a : 32 * a + PX, :], TN) * scale
-        for k in range(16):
-            rows = []
-            for b in range(3):
-                tap = block[128 * b + 8 * k : 128 * b + 8 * k + 8]
-                rows += [tap[:, 0:128], tap[:, 128:256]]
-            buffer[k, 48 * a : 48 * a + 48, :] = jnp.concatenate(rows, axis=0).astype(BF)
-        sent.append(copy_rows(buffer, kg_hbm, 48 * a, 48 * a + 48, sems.at[a]))
+        for group in ((0, 1, 2),) if a < 2 else ((0,), (1,), (2,)):
+            first, last = 48 * a + 16 * group[0], 48 * a + 16 * group[-1] + 16
+            for k in range(16):
+                rows = []
+                for b in group:
+                    tap = block[128 * b + 8 * k : 128 * b + 8 * k + 8]
+                    rows += [tap[:, 0:128], tap[:, 128:256]]
+                buffer[k, first:last, :] = jnp.concatenate(rows, axis=0).astype(BF)
+            sent.append(copy_rows(buffer, kg_hbm, first, last, sems.at[len(sent)]))
     for copy in sent:
         copy.wait()
 
@@ -422,7 +424,7 @@
             pltpu.VMEM((PX, 384), F32),
             pltpu.VMEM((PX + 16, 128), F32),
             pltpu.VMEM((16, 144, 128), BF),
-            pltpu.SemaphoreType.DMA((3,)),
+            pltpu.SemaphoreType.DMA((5,)),
         ],
         copied=(0,),
     )

time: 92.5 us -> 92.5 us (level)
  no operation moved by 1% of the time
where the time goes in v8:
time: 92.5 us; the launch traced here: 91.9 us
  starting transfers between devices  33 us (36%)
  blocking collectives  30.4 us (33%)
  waiting for transfers between devices  16.5 us (18%)
  Pallas kernels  11.3 us (12%)
    all_to_all x1, blocking collectives, shards(): got = lax.all_to_all(packed, SLOTS, 0, 0)  30.4 us
    pallas_call x11, Pallas kernels, call(): pl.pallas_call(body, out_shape=[jax.ShapeDtypeStruct(s, d) for s, d in ou...  11.3 us
    ppermute x1, waiting for transfers between devices, shards(): recv = lax.ppermute(send, 'xh', [(0, 1), (1, 0)])  5.79 us
    ppermute x3, starting transfers between devices, shards(): lax.ppermute(sums, 'y', [(i, (i + k) % 4) for i in range(4)])  5.67 us
    all_to_all x1, starting transfers between devices, shards(): back = lax.all_to_all(joined, 'z', 0, 0)  5.07 us
    ppermute x1, starting transfers between devices, shards(): ha = lax.ppermute(ha, BAND, across)  4.48 us
    all_to_all x1, starting transfers between devices, shards(): kg = lax.all_to_all(kg, SLOTS, 0, 0)  4.1 us
    ppermute x1, starting transfers between devices, shards(): recv = lax.ppermute(send, 'xh', [(0, 1), (1, 0)])  3.16 us
  transfers between devices with their start and end apart: 16, of which 9 were waited for; matrix products, arithmetic and copies ran while one was open for 0% of the time, Pallas kernels for 4%

profile of v8, /device:TPU:1, one launch (start us, length us, event | category | flops | bytes accessed | tf_op | source)
XLA Modules:
  0.0 91.9 jit_solution(13709698140495981695)
XLA Ops:
  0.6 2.7 %shard_map.59 = bf16[16,152,128]{2,1,0:T(8,128)(2,1)} custom-call(s32[1]{0:T(128)} %bitcast.1.core_ref.refs_0_, bf16[9,16,256]{2,1,0:T(8,128)(2,1)} %bitcast.11, f32[1,16]{1,0:T(1,128)} %bitcast.12, bf16[16,16,384]{2,1,0:T(8,128)(2,1)} %refs_2_.1, bf16[16,16,384]{2,1,0:T(8,128)(2,1)} %refs_3_.1), custom_call_target="tpu_custom_call" | custom-call | tf_op jit(solution)/shard_map/pallas_call | solution.py:38
  3.3 30.4 %all_to_all.15.r_ref = bf16[16,152,128]{2,1,0:T(8,128)(2,1)S(1)} all-to-all(bf16[16,152,128]{2,1,0:T(8,128)(2,1)} %shard_map.59), channel_id=1, replica_groups=mesh['xl'=2,'y'=4,'core'=2,'z'=8,'xh'=2] {'xh','z'}, dimensions={0} | all-to-all | bytes 1245184 | tf_op jit(solution)/shard_map/all_to_all | solution.py:383
  33.7 1.0 %shard_map.60 = (bf16[768,256]{1,0:T(8,128)(2,1)S(1)}, bf16[512,128]{1,0:T(8,128)(2,1)S(1)}, bf16[96,256]{1,0:T(8,128)(2,1)S(1)}, bf16[16,40,128]{2,1,0:T(8,128)(2,1)S(1)}) custom-call(s32[1]{0:T(128)} %bitcast.1.core_ref.refs_0_, bf16[16,152,128]{2,1,0:T(8,128)(2,1)S(1)} %all_to_all.15.r_ref), custom_call_target="tpu_custom_call" | custom-call | tf_op jit(solution)/shard_map/pallas_call | solution.py:38
  34.7 3.1 %collective-permute-start = (bf16[768,256]{1,0:T(8,128)(2,1)S(1)}, bf16[768,256]{1,0:T(8,128)(2,1)S(1)}, u32[]{:S(2)}, u32[]{:S(2)}) collective-permute-start(bf16[768,256]{1,0:T(8,128)(2,1)S(1)} %get-tuple-element.12.refs_1_), channel_id=1, source_target_pairs={{0,16},{16,0},{1,17},{17,1},{2,18},{18,2},{3,19},{19,3},{4,20},{20... | collective-permute-start | bytes 1179656 | tf_op jit(solution)/shard_map/ppermute | solution.py:392
  37.8 1.1 %collective-permute-start.5 = (bf16[16,40,128]{2,1,0:T(8,128)(2,1)S(1)}, bf16[16,40,128]{2,1,0:T(8,128)(2,1)S(1)}, u32[]{:S(2)}, u32[]{:S(2)}) collective-permute-start(bf16[16,40,128]{2,1,0:T(8,128)(2,1)S(1)} %get-tuple-element.15.own_ref), channel_id=1, source_target_pairs={{0,4},{2,6},{4,8},{6,10},{8,12},{10,14},{12,0},{14,2},{16,28},{18,... | collective-permute-start | bytes 491528 | tf_op jit(solution)/shard_map/ppermute | solution.py:403
  38.9 0.5 collective-permute-start.4
  39.4 1.0 %collective-permute-start.3 = (bf16[16,40,128]{2,1,0:T(8,128)(2,1)S(1)}, bf16[16,40,128]{2,1,0:T(8,128)(2,1)S(1)}, u32[]{:S(2)}, u32[]{:S(2)}) collective-permute-start(bf16[16,40,128]{2,1,0:T(8,128)(2,1)S(1)} %get-tuple-element.15.own_ref), channel_id=1, source_target_pairs={{0,2},{2,4},{4,6},{6,8},{8,10},{10,12},{12,14},{14,0},{1,3},{3,5},... | collective-permute-start | bytes 491528 | tf_op jit(solution)/shard_map/ppermute | solution.py:401
  40.4 4.5 %collective-permute-start.1 = (bf16[96,256]{1,0:T(8,128)(2,1)S(1)}, bf16[96,256]{1,0:T(8,128)(2,1)S(1)}, u32[]{:S(2)}, u32[]{:S(2)}) collective-permute-start(bf16[96,256]{1,0:T(8,128)(2,1)S(1)} %get-tuple-element.14), channel_id=1, source_target_pairs={{16,32},{48,64},{80,96},{112,128},{144,160},{176,192},{208,224},{3... | collective-permute-start | bytes 147464 | tf_op jit(solution)/shard_map/ppermute | solution.py:393
  44.9 2.1 %collective-permute-done.1.refs_4_ = bf16[96,256]{1,0:T(8,128)(2,1)S(1)} collective-permute-done((bf16[96,256]{1,0:T(8,128)(2,1)S(1)}, bf16[96,256]{1,0:T(8,128)(2,1)S(1)}, u32[]{:S(2)}, u32[]{:S(2)}) %collective-permute-start.1) | collective-permute-done | bytes 49184 | tf_op jit(solution)/shard_map/ppermute | solution.py:393
  46.9 0.0 collective-permute-start.2
  46.9 0.0 collective-permute-done.5.far_ref
  46.9 1.4 %collective-permute-done.4.above_ref = bf16[16,40,128]{2,1,0:T(8,128)(2,1)S(1)} collective-permute-done((bf16[16,40,128]{2,1,0:T(8,128)(2,1)S(1)}, bf16[16,40,128]{2,1,0:T(8,128)(2,1)S(1)}, u32[]{:S(2)}, u32[]{:S(2)}) %collective-permute-start.4) | collective-permute-done | bytes 163872 | tf_op jit(solution)/shard_map/ppermute | solution.py:402
  48.3 0.2 collective-permute-done.3.below_ref
  48.5 0.3 shard_map.61.refs_6_.w_ref
  48.8 0.0 collective-permute-done.2.refs_5_
  48.8 0.0 collective-permute-done.refs_2_
  48.8 3.0 %shard_map.62 = (bf16[16,144,128]{2,1,0:T(8,128)(2,1)}, bf16[1152,128]{1,0:T(8,128)(2,1)S(1)}) custom-call(s32[1]{0:T(128)} %bitcast.1.core_ref.refs_0_, bf16[768,256]{1,0:T(8,128)(2,1)S(1)} %get-tuple-element.12.refs_1_, bf16[768,256]{1,0:T(8,128)(2,1)S(1)} %collective-permute-done.refs_2_, bf16[512,128]{1,0:T(8,128)(2,1)S(1)} %get-tuple-element.13.refs_3_, ...), custom_call_target="tpu_custom_call" | custom-call | tf_op jit(solution)/shard_map/pallas_call | solution.py:38
  51.8 4.1 %all-to-all-start.2 = ((bf16[16,144,128]{2,1,0:T(8,128)(2,1)}), bf16[16,144,128]{2,1,0:T(8,128)(2,1)S(1)}, u32[]{:S(2)}, u32[]{:S(2)}) async-start(bf16[16,144,128]{2,1,0:T(8,128)(2,1)} %get-tuple-element.21), calls=%async_computation.2 | async-start | bytes 1179648 | tf_op jit(solution)/shard_map/all_to_all | solution.py:431
  55.9 1.5 %shard_map.63 = (f32[512,256]{1,0:T(8,128)S(1)}, bf16[512,256]{1,0:T(8,128)(2,1)S(1)}) custom-call(s32[1]{0:T(128)} %bitcast.1.core_ref.refs_0_, bf16[1152,128]{1,0:T(8,128)(2,1)S(1)} %get-tuple-element.16.g_ref, bf16[1152,256]{1,0:T(8,128)(2,1)S(1)} %shard_map.61.refs_6_.w_ref), custom_call_target="tpu_custom_call" | custom-call | tf_op jit(solution)/shard_map/pallas_call | solution.py:38
  57.4 1.4 %collective-permute-start.6 = (bf16[512,256]{1,0:T(8,128)(2,1)S(1)}, bf16[512,256]{1,0:T(8,128)(2,1)S(1)}, u32[]{:S(2)}, u32[]{:S(2)}) collective-permute-start(bf16[512,256]{1,0:T(8,128)(2,1)S(1)} %get-tuple-element.18), channel_id=1, source_target_pairs={{0,16},{16,0},{1,17},{17,1},{2,18},{18,2},{3,19},{19,3},{4,20},{20... | collective-permute-start | bytes 786440 | tf_op jit(solution)/shard_map/ppermute | solution.py:440
  58.8 1.2 %collective-permute-done.6.recv_ref = bf16[512,256]{1,0:T(8,128)(2,1)S(1)} collective-permute-done((bf16[512,256]{1,0:T(8,128)(2,1)S(1)}, bf16[512,256]{1,0:T(8,128)(2,1)S(1)}, u32[]{:S(2)}, u32[]{:S(2)}) %collective-permute-start.6) | collective-permute-done | bytes 262176 | tf_op jit(solution)/shard_map/ppermute | solution.py:440
  60.0 0.4 shard_map.64
  60.4 3.2 %collective-permute-start.7 = (bf16[8,48,128]{2,1,0:T(8,128)(2,1)S(1)}, bf16[8,48,128]{2,1,0:T(8,128)(2,1)S(1)}, u32[]{:S(2)}, u32[]{:S(2)}) collective-permute-start(bf16[8,48,128]{2,1,0:T(8,128)(2,1)S(1)} %get-tuple-element.20), channel_id=1, source_target_pairs={{0,1},{1,0},{2,3},{3,2},{4,5},{5,4},{6,7},{7,6},{8,9},{9,8},{10,11... | collective-permute-start | bytes 294920 | tf_op jit(solution)/shard_map/ppermute | solution.py:450
  63.5 5.8 %collective-permute-done.7.recv_ref = bf16[8,48,128]{2,1,0:T(8,128)(2,1)S(1)} collective-permute-done((bf16[8,48,128]{2,1,0:T(8,128)(2,1)S(1)}, bf16[8,48,128]{2,1,0:T(8,128)(2,1)S(1)}, u32[]{:S(2)}, u32[]{:S(2)}) %collective-permute-start.7) | collective-permute-done | bytes 98336 | tf_op jit(solution)/shard_map/ppermute | solution.py:450
  69.3 0.7 shard_map.65.after_ref
  70.0 2.1 %all-to-all-done.2.r_ref = bf16[16,144,128]{2,1,0:T(8,128)(2,1)S(1)} async-done(((bf16[16,144,128]{2,1,0:T(8,128)(2,1)}), bf16[16,144,128]{2,1,0:T(8,128)(2,1)S(1)}, u32[]{:S(2)}, u32[]{:S(2)}) %all-to-all-start.2) | async-done | bytes 589856 | tf_op jit(solution)/shard_map/all_to_all | solution.py:431
  72.2 5.1 %all-to-all-start.1 = ((bf16[8,96,128]{2,1,0:T(8,128)(2,1)}), bf16[8,96,128]{2,1,0:T(8,128)(2,1)S(1)}, u32[]{:S(2)}, u32[]{:S(2)}) async-start(bf16[8,96,128]{2,1,0:T(8,128)(2,1)} %shard_map.65.after_ref), calls=%async_computation.1 | async-start | bytes 393216 | tf_op jit(solution)/shard_map/all_to_all | solution.py:452
  77.2 0.1 shard_map.67.own_ref
  77.3 3.0 %collective-permute-start.10 = (bf16[144,128]{1,0:T(8,128)(2,1)S(1)}, bf16[144,128]{1,0:T(8,128)(2,1)S(1)}, u32[]{:S(2)}, u32[]{:S(2)}) collective-permute-start(bf16[144,128]{1,0:T(8,128)(2,1)S(1)} %shard_map.67.own_ref), channel_id=1, source_target_pairs={{0,64},{32,96},{64,0},{96,32},{1,65},{33,97},{65,1},{97,33},{2,66}... | collective-permute-start | bytes 110600 | tf_op jit(solution)/shard_map/ppermute | solution.py:457
  80.3 2.3 %collective-permute-start.9 = (bf16[144,128]{1,0:T(8,128)(2,1)S(1)}, bf16[144,128]{1,0:T(8,128)(2,1)S(1)}, u32[]{:S(2)}, u32[]{:S(2)}) collective-permute-start(bf16[144,128]{1,0:T(8,128)(2,1)S(1)} %shard_map.67.own_ref), channel_id=1, source_target_pairs={{0,32},{32,64},{64,96},{96,0},{1,33},{33,65},{65,97},{97,1},{2,34}... | collective-permute-start | bytes 110600 | tf_op jit(solution)/shard_map/ppermute | solution.py:457
  82.6 0.4 collective-permute-start.8
  83.0 0.0 collective-permute-done.10.far_ref
  83.0 1.9 %collective-permute-done.9.prev_ref = bf16[144,128]{1,0:T(8,128)(2,1)S(1)} collective-permute-done((bf16[144,128]{1,0:T(8,128)(2,1)S(1)}, bf16[144,128]{1,0:T(8,128)(2,1)S(1)}, u32[]{:S(2)}, u32[]{:S(2)}) %collective-permute-start.9) | collective-permute-done | bytes 36896 | tf_op jit(solution)/shard_map/ppermute | solution.py:457
  84.9 1.1 %collective-permute-done.8.next_ref = bf16[144,128]{1,0:T(8,128)(2,1)S(1)} collective-permute-done((bf16[144,128]{1,0:T(8,128)(2,1)S(1)}, bf16[144,128]{1,0:T(8,128)(2,1)S(1)}, u32[]{:S(2)}, u32[]{:S(2)}) %collective-permute-start.8) | collective-permute-done | bytes 36896 | tf_op jit(solution)/shard_map/ppermute | solution.py:457
  86.0 2.1 %collective-permute-start.13 = (bf16[144,128]{1,0:T(8,128)(2,1)S(1)}, bf16[144,128]{1,0:T(8,128)(2,1)S(1)}, u32[]{:S(2)}, u32[]{:S(2)}) collective-permute-start(bf16[144,128]{1,0:T(8,128)(2,1)S(1)} %shard_map.68.own_ref), channel_id=1, source_target_pairs={{0,144},{16,128},{128,16},{144,0},{1,145},{17,129},{129,17},{145,1... | collective-permute-start | bytes 110600 | tf_op jit(solution)/shard_map/ppermute | solution.py:466
  88.1 0.1 collective-permute-start.12
  88.2 1.3 %collective-permute-start.11 = (bf16[144,128]{1,0:T(8,128)(2,1)S(1)}, bf16[144,128]{1,0:T(8,128)(2,1)S(1)}, u32[]{:S(2)}, u32[]{:S(2)}) collective-permute-start(bf16[144,128]{1,0:T(8,128)(2,1)S(1)} %shard_map.68.own_ref), channel_id=1, source_target_pairs={{0,128},{128,0},{1,129},{129,1},{2,130},{130,2},{3,131},{131,3},{4... | collective-permute-start | bytes 110600 | tf_op jit(solution)/shard_map/ppermute | solution.py:464
  89.4 0.0 all-to-all-done.1.r_ref
  89.4 0.9 %shard_map.66 = bf16[16,16,384]{2,1,0:T(8,128)(2,1)} custom-call(bf16[8,96,128]{2,1,0:T(8,128)(2,1)S(1)} %all-to-all-done.1.r_ref), custom_call_target="tpu_custom_call" | custom-call | tf_op jit(solution)/shard_map/pallas_call | solution.py:38
  90.4 0.0 collective-permute-done.13.core_xl_ref
  90.4 0.0 collective-permute-done.12.core_own_ref
  90.4 0.8 collective-permute-done.11.xl_ref
  91.2 0.7 shard_map.69
  (1 shorter events, 0.0 us)
Async XLA Ops:
  34.7 14.1 %collective-permute-start = (bf16[768,256]{1,0:T(8,128)(2,1)S(1)}, bf16[768,256]{1,0:T(8,128)(2,1)S(1)}, u32[]{:S(2)}, u32[]{:S(2)}) collective-permute-start(bf16[768,256]{1,0:T(8,128)(2,1)S(1)} %get-tuple-element.12.refs_1_), channel_id=1, source_target_pairs={{0,16},{16,0},{1,17},{17,1},{2,18},{18,2},{3,19},{19,3},{4,20},{20... | collective-permute-start | bytes 1179656 | tf_op jit(solution)/shard_map/ppermute | solution.py:392
  37.8 9.1 %collective-permute-start.5 = (bf16[16,40,128]{2,1,0:T(8,128)(2,1)S(1)}, bf16[16,40,128]{2,1,0:T(8,128)(2,1)S(1)}, u32[]{:S(2)}, u32[]{:S(2)}) collective-permute-start(bf16[16,40,128]{2,1,0:T(8,128)(2,1)S(1)} %get-tuple-element.15.own_ref), channel_id=1, source_target_pairs={{0,4},{2,6},{4,8},{6,10},{8,12},{10,14},{12,0},{14,2},{16,28},{18,... | collective-permute-start | bytes 491528 | tf_op jit(solution)/shard_map/ppermute | solution.py:403
  38.9 9.4 %collective-permute-start.4 = (bf16[16,40,128]{2,1,0:T(8,128)(2,1)S(1)}, bf16[16,40,128]{2,1,0:T(8,128)(2,1)S(1)}, u32[]{:S(2)}, u32[]{:S(2)}) collective-permute-start(bf16[16,40,128]{2,1,0:T(8,128)(2,1)S(1)} %get-tuple-element.15.own_ref), channel_id=1, source_target_pairs={{0,14},{2,0},{4,2},{6,4},{8,6},{10,8},{12,10},{14,12},{1,15},{3,1}... | collective-permute-start | bytes 491528 | tf_op jit(solution)/shard_map/ppermute | solution.py:402
  39.4 9.1 %collective-permute-start.3 = (bf16[16,40,128]{2,1,0:T(8,128)(2,1)S(1)}, bf16[16,40,128]{2,1,0:T(8,128)(2,1)S(1)}, u32[]{:S(2)}, u32[]{:S(2)}) collective-permute-start(bf16[16,40,128]{2,1,0:T(8,128)(2,1)S(1)} %get-tuple-element.15.own_ref), channel_id=1, source_target_pairs={{0,2},{2,4},{4,6},{6,8},{8,10},{10,12},{12,14},{14,0},{1,3},{3,5},... | collective-permute-start | bytes 491528 | tf_op jit(solution)/shard_map/ppermute | solution.py:401
  40.4 6.5 %collective-permute-start.1 = (bf16[96,256]{1,0:T(8,128)(2,1)S(1)}, bf16[96,256]{1,0:T(8,128)(2,1)S(1)}, u32[]{:S(2)}, u32[]{:S(2)}) collective-permute-start(bf16[96,256]{1,0:T(8,128)(2,1)S(1)} %get-tuple-element.14), channel_id=1, source_target_pairs={{16,32},{48,64},{80,96},{112,128},{144,160},{176,192},{208,224},{3... | collective-permute-start | bytes 147464 | tf_op jit(solution)/shard_map/ppermute | solution.py:393
  46.9 1.9 %collective-permute-start.2 = (bf16[96,256]{1,0:T(8,128)(2,1)S(1)}, bf16[96,256]{1,0:T(8,128)(2,1)S(1)}, u32[]{:S(2)}, u32[]{:S(2)}) collective-permute-start(bf16[96,256]{1,0:T(8,128)(2,1)S(1)} %collective-permute-done.1.refs_4_), channel_id=1, source_target_pairs={{0,16},{16,0},{1,17},{17,1},{2,18},{18,2},{3,19},{19,3},{4,20},{20... | collective-permute-start | bytes 147464 | tf_op jit(solution)/shard_map/ppermute | solution.py:394
  51.8 20.3 %all-to-all-start.2 = ((bf16[16,144,128]{2,1,0:T(8,128)(2,1)}), bf16[16,144,128]{2,1,0:T(8,128)(2,1)S(1)}, u32[]{:S(2)}, u32[]{:S(2)}) async-start(bf16[16,144,128]{2,1,0:T(8,128)(2,1)} %get-tuple-element.21), calls=%async_computation.2 | async-start | bytes 1179648 | tf_op jit(solution)/shard_map/all_to_all | solution.py:431
  57.4 2.6 %collective-permute-start.6 = (bf16[512,256]{1,0:T(8,128)(2,1)S(1)}, bf16[512,256]{1,0:T(8,128)(2,1)S(1)}, u32[]{:S(2)}, u32[]{:S(2)}) collective-permute-start(bf16[512,256]{1,0:T(8,128)(2,1)S(1)} %get-tuple-element.18), channel_id=1, source_target_pairs={{0,16},{16,0},{1,17},{17,1},{2,18},{18,2},{3,19},{19,3},{4,20},{20... | collective-permute-start | bytes 786440 | tf_op jit(solution)/shard_map/ppermute | solution.py:440
  60.4 9.0 %collective-permute-start.7 = (bf16[8,48,128]{2,1,0:T(8,128)(2,1)S(1)}, bf16[8,48,128]{2,1,0:T(8,128)(2,1)S(1)}, u32[]{:S(2)}, u32[]{:S(2)}) collective-permute-start(bf16[8,48,128]{2,1,0:T(8,128)(2,1)S(1)} %get-tuple-element.20), channel_id=1, source_target_pairs={{0,1},{1,0},{2,3},{3,2},{4,5},{5,4},{6,7},{7,6},{8,9},{9,8},{10,11... | collective-permute-start | bytes 294920 | tf_op jit(solution)/shard_map/ppermute | solution.py:450
  72.2 17.3 %all-to-all-start.1 = ((bf16[8,96,128]{2,1,0:T(8,128)(2,1)}), bf16[8,96,128]{2,1,0:T(8,128)(2,1)S(1)}, u32[]{:S(2)}, u32[]{:S(2)}) async-start(bf16[8,96,128]{2,1,0:T(8,128)(2,1)} %shard_map.65.after_ref), calls=%async_computation.1 | async-start | bytes 393216 | tf_op jit(solution)/shard_map/all_to_all | solution.py:452
  77.3 5.7 %collective-permute-start.10 = (bf16[144,128]{1,0:T(8,128)(2,1)S(1)}, bf16[144,128]{1,0:T(8,128)(2,1)S(1)}, u32[]{:S(2)}, u32[]{:S(2)}) collective-permute-start(bf16[144,128]{1,0:T(8,128)(2,1)S(1)} %shard_map.67.own_ref), channel_id=1, source_target_pairs={{0,64},{32,96},{64,0},{96,32},{1,65},{33,97},{65,1},{97,33},{2,66}... | collective-permute-start | bytes 110600 | tf_op jit(solution)/shard_map/ppermute | solution.py:457
  80.3 4.5 %collective-permute-start.9 = (bf16[144,128]{1,0:T(8,128)(2,1)S(1)}, bf16[144,128]{1,0:T(8,128)(2,1)S(1)}, u32[]{:S(2)}, u32[]{:S(2)}) collective-permute-start(bf16[144,128]{1,0:T(8,128)(2,1)S(1)} %shard_map.67.own_ref), channel_id=1, source_target_pairs={{0,32},{32,64},{64,96},{96,0},{1,33},{33,65},{65,97},{97,1},{2,34}... | collective-permute-start | bytes 110600 | tf_op jit(solution)/shard_map/ppermute | solution.py:457
  82.6 3.3 %collective-permute-start.8 = (bf16[144,128]{1,0:T(8,128)(2,1)S(1)}, bf16[144,128]{1,0:T(8,128)(2,1)S(1)}, u32[]{:S(2)}, u32[]{:S(2)}) collective-permute-start(bf16[144,128]{1,0:T(8,128)(2,1)S(1)} %shard_map.67.own_ref), channel_id=1, source_target_pairs={{0,96},{32,0},{64,32},{96,64},{1,97},{33,1},{65,33},{97,65},{2,98}... | collective-permute-start | bytes 110600 | tf_op jit(solution)/shard_map/ppermute | solution.py:457
  86.0 4.4 %collective-permute-start.13 = (bf16[144,128]{1,0:T(8,128)(2,1)S(1)}, bf16[144,128]{1,0:T(8,128)(2,1)S(1)}, u32[]{:S(2)}, u32[]{:S(2)}) collective-permute-start(bf16[144,128]{1,0:T(8,128)(2,1)S(1)} %shard_map.68.own_ref), channel_id=1, source_target_pairs={{0,144},{16,128},{128,16},{144,0},{1,145},{17,129},{129,17},{145,1... | collective-permute-start | bytes 110600 | tf_op jit(solution)/shard_map/ppermute | solution.py:466
  88.1 2.3 %collective-permute-start.12 = (bf16[144,128]{1,0:T(8,128)(2,1)S(1)}, bf16[144,128]{1,0:T(8,128)(2,1)S(1)}, u32[]{:S(2)}, u32[]{:S(2)}) collective-permute-start(bf16[144,128]{1,0:T(8,128)(2,1)S(1)} %shard_map.68.own_ref), channel_id=1, source_target_pairs={{0,16},{16,0},{1,17},{17,1},{2,18},{18,2},{3,19},{19,3},{4,20},{20... | collective-permute-start | bytes 110600 | tf_op jit(solution)/shard_map/ppermute | solution.py:465
  88.2 3.0 %collective-permute-start.11 = (bf16[144,128]{1,0:T(8,128)(2,1)S(1)}, bf16[144,128]{1,0:T(8,128)(2,1)S(1)}, u32[]{:S(2)}, u32[]{:S(2)}) collective-permute-start(bf16[144,128]{1,0:T(8,128)(2,1)S(1)} %shard_map.68.own_ref), channel_id=1, source_target_pairs={{0,128},{128,0},{1,129},{129,1},{2,130},{130,2},{3,131},{131,3},{4... | collective-permute-start | bytes 110600 | tf_op jit(solution)/shard_map/ppermute | solution.py:464

commit v9 on v8

--- a/solution.py
+++ b/solution.py
@@ -101,7 +101,7 @@
 def pack_kernel(core_ref, *refs):
     out_hbm, buffer, sems, out_sems = refs[4], refs[9], refs[10], refs[11]
     copies = [pltpu.make_async_copy(refs[k], refs[5 + k], sems.at[k]) for k in range(4)]
-    for copy in copies:
+    for copy in copies[2:] + copies[:2]:
         copy.start()
     ker_ref, bias_ref, x_ref, cot_ref = refs[5:9]
     core = core_ref[0]

time: 92.5 us -> 92.6 us (level)
  no operation moved by 1% of the time
where the time goes in v9:
time: 92.6 us; the launch traced here: 92 us
  starting transfers between devices  33 us (36%)
  blocking collectives  30.4 us (33%)
  waiting for transfers between devices  16.5 us (18%)
  Pallas kernels  11.4 us (12%)
    all_to_all x1, blocking collectives, shards(): got = lax.all_to_all(packed, SLOTS, 0, 0)  30.4 us
    pallas_call x11, Pallas kernels, call(): pl.pallas_call(body, out_shape=[jax.ShapeDtypeStruct(s, d) for s, d in ou...  11.4 us
    ppermute x1, waiting for transfers between devices, shards(): recv = lax.ppermute(send, 'xh', [(0, 1), (1, 0)])  5.9 us
    ppermute x3, starting transfers between devices, shards(): lax.ppermute(sums, 'y', [(i, (i + k) % 4) for i in range(4)])  5.68 us
    all_to_all x1, starting transfers between devices, shards(): back = lax.all_to_all(joined, 'z', 0, 0)  5.06 us
    ppermute x1, starting transfers between devices, shards(): ha = lax.ppermute(ha, BAND, across)  4.48 us
    all_to_all x1, starting transfers between devices, shards(): kg = lax.all_to_all(kg, SLOTS, 0, 0)  4.1 us
    ppermute x1, starting transfers between devices, shards(): recv = lax.ppermute(send, 'xh', [(0, 1), (1, 0)])  3.16 us
  transfers between devices with their start and end apart: 16, of which 9 were waited for; matrix products, arithmetic and copies ran while one was open for 0% of the time, Pallas kernels for 4%

profile of v9, /device:TPU:1, one launch (start us, length us, event | category | flops | bytes accessed | tf_op | source)
XLA Modules:
  0.0 92.0 jit_solution(11129005261371383573)
XLA Ops:
  0.6 2.8 %shard_map.59 = bf16[16,152,128]{2,1,0:T(8,128)(2,1)} custom-call(s32[1]{0:T(128)} %bitcast.1.core_ref.refs_0_, bf16[9,16,256]{2,1,0:T(8,128)(2,1)} %bitcast.11, f32[1,16]{1,0:T(1,128)} %bitcast.12, bf16[16,16,384]{2,1,0:T(8,128)(2,1)} %refs_2_.1, bf16[16,16,384]{2,1,0:T(8,128)(2,1)} %refs_3_.1), custom_call_target="tpu_custom_call" | custom-call | tf_op jit(solution)/shard_map/pallas_call | solution.py:38
  3.5 30.4 %all_to_all.15.r_ref = bf16[16,152,128]{2,1,0:T(8,128)(2,1)S(1)} all-to-all(bf16[16,152,128]{2,1,0:T(8,128)(2,1)} %shard_map.59), channel_id=1, replica_groups=mesh['xl'=2,'y'=4,'core'=2,'z'=8,'xh'=2] {'xh','z'}, dimensions={0} | all-to-all | bytes 1245184 | tf_op jit(solution)/shard_map/all_to_all | solution.py:383
  33.9 1.0 %shard_map.60 = (bf16[768,256]{1,0:T(8,128)(2,1)S(1)}, bf16[512,128]{1,0:T(8,128)(2,1)S(1)}, bf16[96,256]{1,0:T(8,128)(2,1)S(1)}, bf16[16,40,128]{2,1,0:T(8,128)(2,1)S(1)}) custom-call(s32[1]{0:T(128)} %bitcast.1.core_ref.refs_0_, bf16[16,152,128]{2,1,0:T(8,128)(2,1)S(1)} %all_to_all.15.r_ref), custom_call_target="tpu_custom_call" | custom-call | tf_op jit(solution)/shard_map/pallas_call | solution.py:38
  34.9 3.1 %collective-permute-start = (bf16[768,256]{1,0:T(8,128)(2,1)S(1)}, bf16[768,256]{1,0:T(8,128)(2,1)S(1)}, u32[]{:S(2)}, u32[]{:S(2)}) collective-permute-start(bf16[768,256]{1,0:T(8,128)(2,1)S(1)} %get-tuple-element.12.refs_1_), channel_id=1, source_target_pairs={{0,16},{16,0},{1,17},{17,1},{2,18},{18,2},{3,19},{19,3},{4,20},{20... | collective-permute-start | bytes 1179656 | tf_op jit(solution)/shard_map/ppermute | solution.py:392
  38.0 1.1 %collective-permute-start.5 = (bf16[16,40,128]{2,1,0:T(8,128)(2,1)S(1)}, bf16[16,40,128]{2,1,0:T(8,128)(2,1)S(1)}, u32[]{:S(2)}, u32[]{:S(2)}) collective-permute-start(bf16[16,40,128]{2,1,0:T(8,128)(2,1)S(1)} %get-tuple-element.15.own_ref), channel_id=1, source_target_pairs={{0,4},{2,6},{4,8},{6,10},{8,12},{10,14},{12,0},{14,2},{16,28},{18,... | collective-permute-start | bytes 491528 | tf_op jit(solution)/shard_map/ppermute | solution.py:403
  39.0 0.5 collective-permute-start.4
  39.5 1.0 %collective-permute-start.3 = (bf16[16,40,128]{2,1,0:T(8,128)(2,1)S(1)}, bf16[16,40,128]{2,1,0:T(8,128)(2,1)S(1)}, u32[]{:S(2)}, u32[]{:S(2)}) collective-permute-start(bf16[16,40,128]{2,1,0:T(8,128)(2,1)S(1)} %get-tuple-element.15.own_ref), channel_id=1, source_target_pairs={{0,2},{2,4},{4,6},{6,8},{8,10},{10,12},{12,14},{14,0},{1,3},{3,5},... | collective-permute-start | bytes 491528 | tf_op jit(solution)/shard_map/ppermute | solution.py:401
  40.5 4.5 %collective-permute-start.1 = (bf16[96,256]{1,0:T(8,128)(2,1)S(1)}, bf16[96,256]{1,0:T(8,128)(2,1)S(1)}, u32[]{:S(2)}, u32[]{:S(2)}) collective-permute-start(bf16[96,256]{1,0:T(8,128)(2,1)S(1)} %get-tuple-element.14), channel_id=1, source_target_pairs={{16,32},{48,64},{80,96},{112,128},{144,160},{176,192},{208,224},{3... | collective-permute-start | bytes 147464 | tf_op jit(solution)/shard_map/ppermute | solution.py:393
  45.0 2.1 %collective-permute-done.1.refs_4_ = bf16[96,256]{1,0:T(8,128)(2,1)S(1)} collective-permute-done((bf16[96,256]{1,0:T(8,128)(2,1)S(1)}, bf16[96,256]{1,0:T(8,128)(2,1)S(1)}, u32[]{:S(2)}, u32[]{:S(2)}) %collective-permute-start.1) | collective-permute-done | bytes 49184 | tf_op jit(solution)/shard_map/ppermute | solution.py:393
  47.1 0.0 collective-permute-start.2
  47.1 0.0 collective-permute-done.5.far_ref
  47.1 1.4 %collective-permute-done.4.above_ref = bf16[16,40,128]{2,1,0:T(8,128)(2,1)S(1)} collective-permute-done((bf16[16,40,128]{2,1,0:T(8,128)(2,1)S(1)}, bf16[16,40,128]{2,1,0:T(8,128)(2,1)S(1)}, u32[]{:S(2)}, u32[]{:S(2)}) %collective-permute-start.4) | collective-permute-done | bytes 163872 | tf_op jit(solution)/shard_map/ppermute | solution.py:402
  48.4 0.2 collective-permute-done.3.below_ref
  48.7 0.3 shard_map.61.refs_6_.w_ref
  48.9 0.0 collective-permute-done.2.refs_5_
  48.9 0.0 collective-permute-done.refs_2_
  48.9 3.0 %shard_map.62 = (bf16[16,144,128]{2,1,0:T(8,128)(2,1)}, bf16[1152,128]{1,0:T(8,128)(2,1)S(1)}) custom-call(s32[1]{0:T(128)} %bitcast.1.core_ref.refs_0_, bf16[768,256]{1,0:T(8,128)(2,1)S(1)} %get-tuple-element.12.refs_1_, bf16[768,256]{1,0:T(8,128)(2,1)S(1)} %collective-permute-done.refs_2_, bf16[512,128]{1,0:T(8,128)(2,1)S(1)} %get-tuple-element.13.refs_3_, ...), custom_call_target="tpu_custom_call" | custom-call | tf_op jit(solution)/shard_map/pallas_call | solution.py:38
  52.0 4.1 %all-to-all-start.2 = ((bf16[16,144,128]{2,1,0:T(8,128)(2,1)}), bf16[16,144,128]{2,1,0:T(8,128)(2,1)S(1)}, u32[]{:S(2)}, u32[]{:S(2)}) async-start(bf16[16,144,128]{2,1,0:T(8,128)(2,1)} %get-tuple-element.21), calls=%async_computation.2 | async-start | bytes 1179648 | tf_op jit(solution)/shard_map/all_to_all | solution.py:431
  56.1 1.5 %shard_map.63 = (f32[512,256]{1,0:T(8,128)S(1)}, bf16[512,256]{1,0:T(8,128)(2,1)S(1)}) custom-call(s32[1]{0:T(128)} %bitcast.1.core_ref.refs_0_, bf16[1152,128]{1,0:T(8,128)(2,1)S(1)} %get-tuple-element.16.g_ref, bf16[1152,256]{1,0:T(8,128)(2,1)S(1)} %shard_map.61.refs_6_.w_ref), custom_call_target="tpu_custom_call" | custom-call | tf_op jit(solution)/shard_map/pallas_call | solution.py:38
  57.6 1.4 %collective-permute-start.6 = (bf16[512,256]{1,0:T(8,128)(2,1)S(1)}, bf16[512,256]{1,0:T(8,128)(2,1)S(1)}, u32[]{:S(2)}, u32[]{:S(2)}) collective-permute-start(bf16[512,256]{1,0:T(8,128)(2,1)S(1)} %get-tuple-element.18), channel_id=1, source_target_pairs={{0,16},{16,0},{1,17},{17,1},{2,18},{18,2},{3,19},{19,3},{4,20},{20... | collective-permute-start | bytes 786440 | tf_op jit(solution)/shard_map/ppermute | solution.py:440
  59.0 1.2 %collective-permute-done.6.recv_ref = bf16[512,256]{1,0:T(8,128)(2,1)S(1)} collective-permute-done((bf16[512,256]{1,0:T(8,128)(2,1)S(1)}, bf16[512,256]{1,0:T(8,128)(2,1)S(1)}, u32[]{:S(2)}, u32[]{:S(2)}) %collective-permute-start.6) | collective-permute-done | bytes 262176 | tf_op jit(solution)/shard_map/ppermute | solution.py:440
  60.1 0.4 shard_map.64
  60.5 3.2 %collective-permute-start.7 = (bf16[8,48,128]{2,1,0:T(8,128)(2,1)S(1)}, bf16[8,48,128]{2,1,0:T(8,128)(2,1)S(1)}, u32[]{:S(2)}, u32[]{:S(2)}) collective-permute-start(bf16[8,48,128]{2,1,0:T(8,128)(2,1)S(1)} %get-tuple-element.20), channel_id=1, source_target_pairs={{0,1},{1,0},{2,3},{3,2},{4,5},{5,4},{6,7},{7,6},{8,9},{9,8},{10,11... | collective-permute-start | bytes 294920 | tf_op jit(solution)/shard_map/ppermute | solution.py:450
  63.7 5.9 %collective-permute-done.7.recv_ref = bf16[8,48,128]{2,1,0:T(8,128)(2,1)S(1)} collective-permute-done((bf16[8,48,128]{2,1,0:T(8,128)(2,1)S(1)}, bf16[8,48,128]{2,1,0:T(8,128)(2,1)S(1)}, u32[]{:S(2)}, u32[]{:S(2)}) %collective-permute-start.7) | collective-permute-done | bytes 98336 | tf_op jit(solution)/shard_map/ppermute | solution.py:450
  69.6 0.7 shard_map.65.after_ref
  70.3 2.0 %all-to-all-done.2.r_ref = bf16[16,144,128]{2,1,0:T(8,128)(2,1)S(1)} async-done(((bf16[16,144,128]{2,1,0:T(8,128)(2,1)}), bf16[16,144,128]{2,1,0:T(8,128)(2,1)S(1)}, u32[]{:S(2)}, u32[]{:S(2)}) %all-to-all-start.2) | async-done | bytes 589856 | tf_op jit(solution)/shard_map/all_to_all | solution.py:431
  72.3 5.1 %all-to-all-start.1 = ((bf16[8,96,128]{2,1,0:T(8,128)(2,1)}), bf16[8,96,128]{2,1,0:T(8,128)(2,1)S(1)}, u32[]{:S(2)}, u32[]{:S(2)}) async-start(bf16[8,96,128]{2,1,0:T(8,128)(2,1)} %shard_map.65.after_ref), calls=%async_computation.1 | async-start | bytes 393216 | tf_op jit(solution)/shard_map/all_to_all | solution.py:452
  77.4 0.1 shard_map.67.own_ref
  77.5 3.0 %collective-permute-start.10 = (bf16[144,128]{1,0:T(8,128)(2,1)S(1)}, bf16[144,128]{1,0:T(8,128)(2,1)S(1)}, u32[]{:S(2)}, u32[]{:S(2)}) collective-permute-start(bf16[144,128]{1,0:T(8,128)(2,1)S(1)} %shard_map.67.own_ref), channel_id=1, source_target_pairs={{0,64},{32,96},{64,0},{96,32},{1,65},{33,97},{65,1},{97,33},{2,66}... | collective-permute-start | bytes 110600 | tf_op jit(solution)/shard_map/ppermute | solution.py:457
  80.5 2.3 %collective-permute-start.9 = (bf16[144,128]{1,0:T(8,128)(2,1)S(1)}, bf16[144,128]{1,0:T(8,128)(2,1)S(1)}, u32[]{:S(2)}, u32[]{:S(2)}) collective-permute-start(bf16[144,128]{1,0:T(8,128)(2,1)S(1)} %shard_map.67.own_ref), channel_id=1, source_target_pairs={{0,32},{32,64},{64,96},{96,0},{1,33},{33,65},{65,97},{97,1},{2,34}... | collective-permute-start | bytes 110600 | tf_op jit(solution)/shard_map/ppermute | solution.py:457
  82.8 0.4 collective-permute-start.8
  83.1 0.0 collective-permute-done.10.far_ref
  83.1 1.9 %collective-permute-done.9.prev_ref = bf16[144,128]{1,0:T(8,128)(2,1)S(1)} collective-permute-done((bf16[144,128]{1,0:T(8,128)(2,1)S(1)}, bf16[144,128]{1,0:T(8,128)(2,1)S(1)}, u32[]{:S(2)}, u32[]{:S(2)}) %collective-permute-start.9) | collective-permute-done | bytes 36896 | tf_op jit(solution)/shard_map/ppermute | solution.py:457
  85.0 1.1 %collective-permute-done.8.next_ref = bf16[144,128]{1,0:T(8,128)(2,1)S(1)} collective-permute-done((bf16[144,128]{1,0:T(8,128)(2,1)S(1)}, bf16[144,128]{1,0:T(8,128)(2,1)S(1)}, u32[]{:S(2)}, u32[]{:S(2)}) %collective-permute-start.8) | collective-permute-done | bytes 36896 | tf_op jit(solution)/shard_map/ppermute | solution.py:457
  86.1 2.1 %collective-permute-start.13 = (bf16[144,128]{1,0:T(8,128)(2,1)S(1)}, bf16[144,128]{1,0:T(8,128)(2,1)S(1)}, u32[]{:S(2)}, u32[]{:S(2)}) collective-permute-start(bf16[144,128]{1,0:T(8,128)(2,1)S(1)} %shard_map.68.own_ref), channel_id=1, source_target_pairs={{0,144},{16,128},{128,16},{144,0},{1,145},{17,129},{129,17},{145,1... | collective-permute-start | bytes 110600 | tf_op jit(solution)/shard_map/ppermute | solution.py:466
  88.2 0.1 collective-permute-start.12
  88.3 1.3 %collective-permute-start.11 = (bf16[144,128]{1,0:T(8,128)(2,1)S(1)}, bf16[144,128]{1,0:T(8,128)(2,1)S(1)}, u32[]{:S(2)}, u32[]{:S(2)}) collective-permute-start(bf16[144,128]{1,0:T(8,128)(2,1)S(1)} %shard_map.68.own_ref), channel_id=1, source_target_pairs={{0,128},{128,0},{1,129},{129,1},{2,130},{130,2},{3,131},{131,3},{4... | collective-permute-start | bytes 110600 | tf_op jit(solution)/shard_map/ppermute | solution.py:464
  89.6 0.0 all-to-all-done.1.r_ref
  89.6 0.9 %shard_map.66 = bf16[16,16,384]{2,1,0:T(8,128)(2,1)} custom-call(bf16[8,96,128]{2,1,0:T(8,128)(2,1)S(1)} %all-to-all-done.1.r_ref), custom_call_target="tpu_custom_call" | custom-call | tf_op jit(solution)/shard_map/pallas_call | solution.py:38
  90.5 0.0 collective-permute-done.13.core_xl_ref
  90.5 0.0 collective-permute-done.12.core_own_ref
  90.5 0.8 collective-permute-done.11.xl_ref
  91.3 0.7 shard_map.69
  (1 shorter events, 0.0 us)
Async XLA Ops:
  34.9 14.1 %collective-permute-start = (bf16[768,256]{1,0:T(8,128)(2,1)S(1)}, bf16[768,256]{1,0:T(8,128)(2,1)S(1)}, u32[]{:S(2)}, u32[]{:S(2)}) collective-permute-start(bf16[768,256]{1,0:T(8,128)(2,1)S(1)} %get-tuple-element.12.refs_1_), channel_id=1, source_target_pairs={{0,16},{16,0},{1,17},{17,1},{2,18},{18,2},{3,19},{19,3},{4,20},{20... | collective-permute-start | bytes 1179656 | tf_op jit(solution)/shard_map/ppermute | solution.py:392
  38.0 9.1 %collective-permute-start.5 = (bf16[16,40,128]{2,1,0:T(8,128)(2,1)S(1)}, bf16[16,40,128]{2,1,0:T(8,128)(2,1)S(1)}, u32[]{:S(2)}, u32[]{:S(2)}) collective-permute-start(bf16[16,40,128]{2,1,0:T(8,128)(2,1)S(1)} %get-tuple-element.15.own_ref), channel_id=1, source_target_pairs={{0,4},{2,6},{4,8},{6,10},{8,12},{10,14},{12,0},{14,2},{16,28},{18,... | collective-permute-start | bytes 491528 | tf_op jit(solution)/shard_map/ppermute | solution.py:403
  39.0 9.4 %collective-permute-start.4 = (bf16[16,40,128]{2,1,0:T(8,128)(2,1)S(1)}, bf16[16,40,128]{2,1,0:T(8,128)(2,1)S(1)}, u32[]{:S(2)}, u32[]{:S(2)}) collective-permute-start(bf16[16,40,128]{2,1,0:T(8,128)(2,1)S(1)} %get-tuple-element.15.own_ref), channel_id=1, source_target_pairs={{0,14},{2,0},{4,2},{6,4},{8,6},{10,8},{12,10},{14,12},{1,15},{3,1}... | collective-permute-start | bytes 491528 | tf_op jit(solution)/shard_map/ppermute | solution.py:402
  39.5 9.1 %collective-permute-start.3 = (bf16[16,40,128]{2,1,0:T(8,128)(2,1)S(1)}, bf16[16,40,128]{2,1,0:T(8,128)(2,1)S(1)}, u32[]{:S(2)}, u32[]{:S(2)}) collective-permute-start(bf16[16,40,128]{2,1,0:T(8,128)(2,1)S(1)} %get-tuple-element.15.own_ref), channel_id=1, source_target_pairs={{0,2},{2,4},{4,6},{6,8},{8,10},{10,12},{12,14},{14,0},{1,3},{3,5},... | collective-permute-start | bytes 491528 | tf_op jit(solution)/shard_map/ppermute | solution.py:401
  40.5 6.5 %collective-permute-start.1 = (bf16[96,256]{1,0:T(8,128)(2,1)S(1)}, bf16[96,256]{1,0:T(8,128)(2,1)S(1)}, u32[]{:S(2)}, u32[]{:S(2)}) collective-permute-start(bf16[96,256]{1,0:T(8,128)(2,1)S(1)} %get-tuple-element.14), channel_id=1, source_target_pairs={{16,32},{48,64},{80,96},{112,128},{144,160},{176,192},{208,224},{3... | collective-permute-start | bytes 147464 | tf_op jit(solution)/shard_map/ppermute | solution.py:393
  47.1 1.9 %collective-permute-start.2 = (bf16[96,256]{1,0:T(8,128)(2,1)S(1)}, bf16[96,256]{1,0:T(8,128)(2,1)S(1)}, u32[]{:S(2)}, u32[]{:S(2)}) collective-permute-start(bf16[96,256]{1,0:T(8,128)(2,1)S(1)} %collective-permute-done.1.refs_4_), channel_id=1, source_target_pairs={{0,16},{16,0},{1,17},{17,1},{2,18},{18,2},{3,19},{19,3},{4,20},{20... | collective-permute-start | bytes 147464 | tf_op jit(solution)/shard_map/ppermute | solution.py:394
  52.0 20.3 %all-to-all-start.2 = ((bf16[16,144,128]{2,1,0:T(8,128)(2,1)}), bf16[16,144,128]{2,1,0:T(8,128)(2,1)S(1)}, u32[]{:S(2)}, u32[]{:S(2)}) async-start(bf16[16,144,128]{2,1,0:T(8,128)(2,1)} %get-tuple-element.21), calls=%async_computation.2 | async-start | bytes 1179648 | tf_op jit(solution)/shard_map/all_to_all | solution.py:431
  57.6 2.6 %collective-permute-start.6 = (bf16[512,256]{1,0:T(8,128)(2,1)S(1)}, bf16[512,256]{1,0:T(8,128)(2,1)S(1)}, u32[]{:S(2)}, u32[]{:S(2)}) collective-permute-start(bf16[512,256]{1,0:T(8,128)(2,1)S(1)} %get-tuple-element.18), channel_id=1, source_target_pairs={{0,16},{16,0},{1,17},{17,1},{2,18},{18,2},{3,19},{19,3},{4,20},{20... | collective-permute-start | bytes 786440 | tf_op jit(solution)/shard_map/ppermute | solution.py:440
  60.5 9.1 %collective-permute-start.7 = (bf16[8,48,128]{2,1,0:T(8,128)(2,1)S(1)}, bf16[8,48,128]{2,1,0:T(8,128)(2,1)S(1)}, u32[]{:S(2)}, u32[]{:S(2)}) collective-permute-start(bf16[8,48,128]{2,1,0:T(8,128)(2,1)S(1)} %get-tuple-element.20), channel_id=1, source_target_pairs={{0,1},{1,0},{2,3},{3,2},{4,5},{5,4},{6,7},{7,6},{8,9},{9,8},{10,11... | collective-permute-start | bytes 294920 | tf_op jit(solution)/shard_map/ppermute | solution.py:450
  72.3 17.3 %all-to-all-start.1 = ((bf16[8,96,128]{2,1,0:T(8,128)(2,1)}), bf16[8,96,128]{2,1,0:T(8,128)(2,1)S(1)}, u32[]{:S(2)}, u32[]{:S(2)}) async-start(bf16[8,96,128]{2,1,0:T(8,128)(2,1)} %shard_map.65.after_ref), calls=%async_computation.1 | async-start | bytes 393216 | tf_op jit(solution)/shard_map/all_to_all | solution.py:452
  77.5 5.7 %collective-permute-start.10 = (bf16[144,128]{1,0:T(8,128)(2,1)S(1)}, bf16[144,128]{1,0:T(8,128)(2,1)S(1)}, u32[]{:S(2)}, u32[]{:S(2)}) collective-permute-start(bf16[144,128]{1,0:T(8,128)(2,1)S(1)} %shard_map.67.own_ref), channel_id=1, source_target_pairs={{0,64},{32,96},{64,0},{96,32},{1,65},{33,97},{65,1},{97,33},{2,66}... | collective-permute-start | bytes 110600 | tf_op jit(solution)/shard_map/ppermute | solution.py:457
  80.5 4.5 %collective-permute-start.9 = (bf16[144,128]{1,0:T(8,128)(2,1)S(1)}, bf16[144,128]{1,0:T(8,128)(2,1)S(1)}, u32[]{:S(2)}, u32[]{:S(2)}) collective-permute-start(bf16[144,128]{1,0:T(8,128)(2,1)S(1)} %shard_map.67.own_ref), channel_id=1, source_target_pairs={{0,32},{32,64},{64,96},{96,0},{1,33},{33,65},{65,97},{97,1},{2,34}... | collective-permute-start | bytes 110600 | tf_op jit(solution)/shard_map/ppermute | solution.py:457
  82.8 3.3 %collective-permute-start.8 = (bf16[144,128]{1,0:T(8,128)(2,1)S(1)}, bf16[144,128]{1,0:T(8,128)(2,1)S(1)}, u32[]{:S(2)}, u32[]{:S(2)}) collective-permute-start(bf16[144,128]{1,0:T(8,128)(2,1)S(1)} %shard_map.67.own_ref), channel_id=1, source_target_pairs={{0,96},{32,0},{64,32},{96,64},{1,97},{33,1},{65,33},{97,65},{2,98}... | collective-permute-start | bytes 110600 | tf_op jit(solution)/shard_map/ppermute | solution.py:457
  86.1 4.4 %collective-permute-start.13 = (bf16[144,128]{1,0:T(8,128)(2,1)S(1)}, bf16[144,128]{1,0:T(8,128)(2,1)S(1)}, u32[]{:S(2)}, u32[]{:S(2)}) collective-permute-start(bf16[144,128]{1,0:T(8,128)(2,1)S(1)} %shard_map.68.own_ref), channel_id=1, source_target_pairs={{0,144},{16,128},{128,16},{144,0},{1,145},{17,129},{129,17},{145,1... | collective-permute-start | bytes 110600 | tf_op jit(solution)/shard_map/ppermute | solution.py:466
  88.2 2.3 %collective-permute-start.12 = (bf16[144,128]{1,0:T(8,128)(2,1)S(1)}, bf16[144,128]{1,0:T(8,128)(2,1)S(1)}, u32[]{:S(2)}, u32[]{:S(2)}) collective-permute-start(bf16[144,128]{1,0:T(8,128)(2,1)S(1)} %shard_map.68.own_ref), channel_id=1, source_target_pairs={{0,16},{16,0},{1,17},{17,1},{2,18},{18,2},{3,19},{19,3},{4,20},{20... | collective-permute-start | bytes 110600 | tf_op jit(solution)/shard_map/ppermute | solution.py:465
  88.3 3.0 %collective-permute-start.11 = (bf16[144,128]{1,0:T(8,128)(2,1)S(1)}, bf16[144,128]{1,0:T(8,128)(2,1)S(1)}, u32[]{:S(2)}, u32[]{:S(2)}) collective-permute-start(bf16[144,128]{1,0:T(8,128)(2,1)S(1)} %shard_map.68.own_ref), channel_id=1, source_target_pairs={{0,128},{128,0},{1,129},{129,1},{2,130},{130,2},{3,131},{131,3},{4... | collective-permute-start | bytes 110600 | tf_op jit(solution)/shard_map/ppermute | solution.py:464
